TPU v7x, 256 devices: a whole 4x4x8 slice. The times are simulated.
256 devices in a mesh: tm: 16 (over y, x), height: 8 (over z), head: 2 (over core).
Axes of the slice: x: 4, y: 4, z: 8, core: 2. Of those that a mesh axis runs over, the one named last changes fastest.
Arguments:
- video_q: bfloat16 [128, 32, 8, 1536], P('tm', 'height', None, 'head'), may hold values from -41 to 41
- video_kv: bfloat16 [2, 128, 32, 8, 1536], P(None, 'tm', 'height', None, 'head'), may hold values from -4.5 to 4.5
- text_q: bfloat16 [256, 1536], P(None, 'head'), may hold values from -41 to 41
- text_k: bfloat16 [256, 1536], P(None, 'head'), may hold values from -4.5 to 4.5
- text_v: bfloat16 [256, 1536], P(None, 'head'), may hold values from -4.5 to 4.5
- tile_mask: int32 [32, 8, 2, 27], P('tm', 'height'), may hold values 0 or 1
- text_valid: int32 [256], replicated, may hold values 0 or 1
- w_out: bfloat16 [1536, 3072], P('head', 'height'), may hold values from -0.15625 to 0.15625
Outputs:
- video_out: bfloat16 [128, 32, 8, 3072], P('tm', 'height', None, 'head')
- text_out: bfloat16 [256, 3072], P(None, 'head')
All inputs are finite; a program needn't handle non-finite values. No bound on the sum of `tile_mask` on one device may be relied on, other than what follows from the above.
Results may differ from a plain program's by a relative error of at most 0.023.
Values may be sent and summed in bfloat16 or wider, within the bound.
No kernel may reach another device: no remote copies, remote signals or barrier semaphores. Data moves between devices by JAX's collectives and lax.ppermute only.
A program may use at most 64 MiB of HBM per device.

v0:
```python
import jax
import jax.numpy as jnp
from jax import lax
from jax.sharding import PartitionSpec as P

HEAD_DIM = 128
TILE = 4


def padded(block, sides, width):
    for axis, dim in sides:
        count = lax.axis_size(axis)
        forward = [(i, i + 1) for i in range(count - 1)]
        backward = [(target, source) for source, target in forward]
        low = lax.ppermute(
            lax.slice_in_dim(block, block.shape[dim] - width, None, axis=dim), axis, forward
        )
        high = lax.ppermute(lax.slice_in_dim(block, 0, width, axis=dim), axis, backward)
        block = jnp.concatenate([low, block, high], axis=dim)
    return block


def attend_block(q_split, k_split, v_split, allowed):
    head_width = q_split.shape[2]
    scores = jnp.einsum(
        "qhd,khd->hqk", q_split, k_split, preferred_element_type=jnp.float32
    ) * head_width ** (-0.5)
    scores = jnp.where(allowed[None, :, :], scores, -jnp.inf)
    highest = jnp.max(scores, axis=-1, keepdims=True)
    weights = jnp.exp(scores - highest)
    totals = jnp.sum(weights, axis=-1)
    mixture = jnp.einsum(
        "hqk,khd->qhd", weights.astype(jnp.bfloat16), v_split, preferred_element_type=jnp.float32
    )
    mixture = mixture / totals.T[:, :, None]
    return mixture.reshape(q_split.shape[0], -1).astype(jnp.bfloat16)


def shards(video_q, video_kv, text_q, text_k, text_v, tile_mask, text_valid, w_out):
    frame_count, row_count, col_count, local_width = video_q.shape
    head_count = local_width // HEAD_DIM
    tiles_t = frame_count // TILE
    tiles_h = row_count // TILE
    tiles_w = col_count // TILE
    tokens = frame_count * row_count * col_count
    text_count = text_q.shape[0]
    score_scale = HEAD_DIM ** (-0.5)
    text_ok = text_valid > 0
    grown = padded(video_kv, (("tm", 1), ("height", 2)), TILE)
    own_keys = video_kv[0].reshape(tokens, head_count, HEAD_DIM)
    own_values = video_kv[1].reshape(tokens, head_count, HEAD_DIM)
    text_q3 = text_q.reshape(text_count, head_count, HEAD_DIM)
    text_k3 = text_k.reshape(text_count, head_count, HEAD_DIM)
    text_v3 = text_v.reshape(text_count, head_count, HEAD_DIM)
    part_scores = (
        jnp.einsum("thd,khd->htk", text_q3, own_keys, preferred_element_type=jnp.float32)
        * score_scale
    )
    part_high = jnp.max(part_scores, axis=-1)
    part_weights = jnp.exp(part_scores - part_high[..., None])
    part_total = jnp.sum(part_weights, axis=-1)
    part_sums = jnp.einsum(
        "htk,khd->htd",
        part_weights.astype(jnp.bfloat16),
        own_values,
        preferred_element_type=jnp.float32,
    )
    global_high = lax.pmax(part_high, ("tm", "height"))
    rescale = jnp.exp(part_high - global_high)
    part_total, part_sums = lax.psum(
        (part_total * rescale, part_sums * rescale[..., None]), ("tm", "height")
    )
    part_high = global_high
    self_scores = (
        jnp.einsum("thd,khd->htk", text_q3, text_k3, preferred_element_type=jnp.float32)
        * score_scale
    )
    self_high = jnp.max(jnp.where(text_ok[None, None, :], self_scores, -jnp.inf), axis=-1)
    peak_all = jnp.maximum(part_high, self_high)
    self_weights = jnp.where(
        text_ok[None, None, :], jnp.exp(self_scores - peak_all[..., None]), 0.0
    )
    factor_part = jnp.exp(part_high - peak_all)
    text_total = part_total * factor_part + jnp.sum(self_weights, axis=-1)
    self_sums = jnp.einsum(
        "htk,khd->htd",
        self_weights.astype(jnp.bfloat16),
        text_v3,
        preferred_element_type=jnp.float32,
    )
    text_sums = part_sums * factor_part[..., None] + self_sums
    text_attended = (
        (text_sums / text_total[..., None])
        .transpose(1, 0, 2)
        .reshape(text_count, local_width)
        .astype(jnp.bfloat16)
    )
    time_base = lax.axis_index("tm") * tiles_t
    row_base = lax.axis_index("height") * tiles_h
    all_time = tiles_t * lax.axis_size("tm")
    all_rows = tiles_h * lax.axis_size("height")
    query_tile = jnp.arange(tiles_w, dtype=jnp.int32)[:, None, None, None]
    step_t = jnp.arange(3, dtype=jnp.int32)[None, :, None, None]
    step_h = jnp.arange(3, dtype=jnp.int32)[None, None, :, None]
    key_tile = jnp.arange(tiles_w, dtype=jnp.int32)[None, None, None, :]
    col_step = key_tile - query_tile + 1
    col_near = (col_step >= 0) & (col_step <= 2)
    offset_id = 9 * step_t + 3 * step_h + jnp.clip(col_step, 0, 2)
    q_rows = TILE * TILE * col_count
    k_rows = 9 * TILE * TILE * col_count
    text_allowed = jnp.broadcast_to(text_ok[None, :], (q_rows, text_count))

    def one_pair(pair_id):
        tile_a = pair_id // tiles_h
        tile_b = pair_id % tiles_h
        start_kv = (jnp.int32(0), tile_a * TILE, tile_b * TILE, jnp.int32(0), jnp.int32(0))
        block = lax.dynamic_slice(grown, start_kv, (2, 3 * TILE, 3 * TILE, col_count, local_width))
        block = block.reshape(2, k_rows, head_count, HEAD_DIM)
        start_q = (tile_a * TILE, tile_b * TILE, jnp.int32(0), jnp.int32(0))
        queries = lax.dynamic_slice(video_q, start_q, (TILE, TILE, col_count, local_width)).reshape(
            q_rows, head_count, HEAD_DIM
        )
        mask_row = tile_mask[tile_a, tile_b]
        picked = (
            jnp.take_along_axis(mask_row, offset_id.reshape(tiles_w, -1), axis=1).reshape(
                offset_id.shape
            )
            > 0
        )
        global_t = time_base + tile_a + step_t - 1
        global_h = row_base + tile_b + step_h - 1
        inside = (global_t >= 0) & (global_t < all_time) & (global_h >= 0) & (global_h < all_rows)
        chosen = (picked | (offset_id == 13)) & col_near & inside
        cell_mask = jnp.broadcast_to(
            chosen.reshape(1, 1, tiles_w, 1, 3, 1, 3, 1, tiles_w, 1),
            (TILE, TILE, tiles_w, TILE, 3, TILE, 3, TILE, tiles_w, TILE),
        ).reshape(q_rows, k_rows)
        allowed = jnp.concatenate([cell_mask, text_allowed], axis=1)
        key_rows = jnp.concatenate([block[0], text_k3], axis=0)
        value_rows = jnp.concatenate([block[1], text_v3], axis=0)
        return attend_block(queries, key_rows, value_rows, allowed)

    outputs = lax.map(one_pair, jnp.arange(tiles_t * tiles_h, dtype=jnp.int32))
    outputs = outputs.reshape(tiles_t, tiles_h, TILE, TILE, col_count, local_width)
    attended = outputs.transpose(0, 2, 1, 3, 4, 5).reshape(tokens, local_width)
    stacked = jnp.concatenate([attended, text_attended], axis=0)
    terms = jnp.dot(
        stacked,
        lax.all_gather(w_out, "height", axis=1, tiled=True),
        preferred_element_type=jnp.float32,
    )
    shares = lax.psum_scatter(
        terms.astype(jnp.bfloat16), "head", scatter_dimension=1, tiled=True
    ).astype(jnp.float32)
    video_out = shares[:tokens].reshape(frame_count, row_count, col_count, -1).astype(jnp.bfloat16)
    text_out = shares[tokens:].astype(jnp.bfloat16)
    return (video_out, text_out)


def solution(mesh):
    return jax.shard_map(
        shards,
        mesh=mesh,
        in_specs=(
            P("tm", "height", None, "head"),
            P(None, "tm", "height", None, "head"),
            P(None, "head"),
            P(None, "head"),
            P(None, "head"),
            P("tm", "height", None, None),
            P(),
            P("head", "height"),
        ),
        out_specs=(P("tm", "height", None, "head"), P(None, "head")),
        check_vma=False,
    )
```

profile of v0, /device:TPU:1, one launch (start us, length us, event | category | flops | bytes accessed | tf_op | source)
XLA Modules:
  0.0 939.5 jit_solution(15081563196082220412)
XLA Ops:
  10.2 4.7 collective-permute-start
  18.0 302.9 %pmax.7 = f32[6,256]{1,0:T(8,128)} all-reduce(f32[6,256]{1,0:T(8,128)S(1)} %get-tuple-element.366), channel_id=1, replica_groups=mesh['tm'=16,'height'=8,'head'=2] {'tm','height'}, use_global_device_ids=true, to_apply=%region_5.6 | all-reduce | flops 1536 | bytes 12288 | tf_op jit(solution)/shard_map/pmax | solution.py:68
  333.3 2.6 collective-permute-start.2
  337.7 302.6 %psum.15 = f32[6,256]{1,0:T(8,128)S(1)} all-reduce(f32[6,256]{1,0:T(8,128)S(1)} %copy-done.10), channel_id=1, replica_groups=mesh['tm'=16,'height'=8,'head'=2] {'tm','height'}, use_global_device_ids=true, to_apply=%region_9.10 | all-reduce | flops 1536 | bytes 12288 | tf_op jit(solution)/shard_map/psum | solution.py:70
  643.9 4.0 pad_maximum_fusion
  647.9 124.0 %while.15 = (s32[]{:T(128)}, bf16[2,128,768]{2,1,0:T(8,128)(2,1)}, s32[2]{0:T(128)S(1)}, bf16[2,16,12,8,768]{4,3,2,1,0:T(8,128)(2,1)}, bf16[256,6,128]{0,2,1:T(8...) while((s32[]{:T(128)}, bf16[2,128,768]{2,1,0:T(8,128)(2,1)}, ...), condition=%wide.region_3.0_spmd.clone.clone, body=%wide.region_0.3_spmd.clone.clone.sunk | while | flops 570244480 | bytes 61921352 | solution.py:143
  652.5 12.8 %broadcast_in_dim.112 = pred[4,4,2,4,3,4,3,4,2,4]{9,8,7,6,5,4,3,2,1,0:T(4,128)(4,1)} broadcast(pred[2,3,3,2]{3,2,1,0:T(4,128)(4,1)S(1)} %and_and_fusion.5), dimensions={2,4,6,8} | broadcast | bytes 147492 | tf_op jit(solution)/shard_map/while/body/eval_jaxpr/broadcast_in_dim | solution.py:134
  665.3 19.2 %reshape.366 = pred[128,1152]{1,0:T(8,128)(4,1)S(1)} reshape(pred[4,4,2,4,3,4,3,4,2,4]{9,8,7,6,5,4,3,2,1,0:T(4,128)(4,1)} %broadcast_in_dim.112) | data formatting | bytes 294912 | tf_op jit(solution)/shard_map/while/body/eval_jaxpr/reshape | solution.py:137
  685.1 4.0 constant_dynamic-slice_fusion.6
  689.1 3.6 squeeze.39
  698.9 3.6 squeeze.40
  702.6 2.6 copy.61
  705.1 3.8 fusion.90
  714.5 12.8 %broadcast_in_dim.112 = pred[4,4,2,4,3,4,3,4,2,4]{9,8,7,6,5,4,3,2,1,0:T(4,128)(4,1)} broadcast(pred[2,3,3,2]{3,2,1,0:T(4,128)(4,1)S(1)} %and_and_fusion.5), dimensions={2,4,6,8} | broadcast | bytes 147492 | tf_op jit(solution)/shard_map/while/body/eval_jaxpr/broadcast_in_dim | solution.py:134
  727.2 19.2 %reshape.366 = pred[128,1152]{1,0:T(8,128)(4,1)S(1)} reshape(pred[4,4,2,4,3,4,3,4,2,4]{9,8,7,6,5,4,3,2,1,0:T(4,128)(4,1)} %broadcast_in_dim.112) | data formatting | bytes 294912 | tf_op jit(solution)/shard_map/while/body/eval_jaxpr/reshape | solution.py:137
  747.1 4.0 constant_dynamic-slice_fusion.6
  751.1 3.6 squeeze.39
  756.4 2.5 fusion.88
  760.9 3.6 squeeze.40
  764.5 2.6 copy.61
  767.1 3.8 fusion.90
  771.9 6.8 convolution_convert_fusion
  778.7 150.8 %reduce-scatter.2.cloned.1.call-done = bf16[512,1536]{1,0:T(8,128)(2,1)} async-done(((bf16[512,3072]{1,0:T(8,128)(2,1)}), bf16[512,1536]{1,0:T(8,128)(2,1)}) %reduce-scatter.2.cloned.1.call-update) | async-done | bytes 1572880 | tf_op jit(solution)/shard_map/reduce_scatter | solution.py:152
  929.5 2.6 fusion.68
  (128 shorter events, 39.1 us)
Async XLA Ops:
  8.0 8.2 copy-start.1
  8.0 9.4 %copy-start.6 = (bf16[256,768]{1,0:T(8,128)(2,1)S(1)}, bf16[256,768]{1,0:T(8,128)(2,1)}, u32[]{:S(2)}) copy-start(bf16[256,768]{1,0:T(8,128)(2,1)} %param.12) | copy-start | bytes 1179652
  8.0 632.8 %all-reduce.2.cloned.1.call-start = ((), (), s32[]{:S(2)}) async-start(), calls=%async_computation.1 | async-start | bytes 1572864 | tf_op jit(solution)/shard_map/psum | solution.py:70
  10.2 318.4 %collective-permute-start = (bf16[2,4,4,8,768]{4,3,2,1,0:T(8,128)(2,1)}, bf16[2,4,4,8,768]{4,3,2,1,0:T(8,128)(2,1)}, u32[]{:S(2)}, u32[]{:S(2)}) collective-permute-start(bf16[2,4,4,8,768]{4,3,2,1,0:T(8,128)(2,1)} %get-tuple-element.362), channel_id=1, source_target_pairs={{0,16},{16,32},{32,48},{48,64},{64,80},{80,96},{96,112},{112,128},... | collective-permute-start | bytes 1179656 | tf_op jit(solution)/shard_map/ppermute | solution.py:15
  14.9 316.5 %collective-permute-start.1 = (bf16[2,4,4,8,768]{4,3,2,1,0:T(8,128)(2,1)}, bf16[2,4,4,8,768]{4,3,2,1,0:T(8,128)(2,1)}, u32[]{:S(2)}, u32[]{:S(2)}) collective-permute-start(bf16[2,4,4,8,768]{4,3,2,1,0:T(8,128)(2,1)} %get-tuple-element.361), channel_id=1, source_target_pairs={{16,0},{32,16},{48,32},{64,48},{80,64},{96,80},{112,96},{128,112},... | collective-permute-start | bytes 1179656 | tf_op jit(solution)/shard_map/ppermute | solution.py:18
  17.6 304.1 %copy-start.17 = (s32[256]{0:T(256)S(1)}, s32[256]{0:T(256)}, u32[]{:S(2)}) copy-start(s32[256]{0:T(256)} %param.16) | copy-start | bytes 3076
  18.0 304.9 %copy-start.5 = (bf16[1,8,4,8,768]{4,3,2,1,0:T(8,128)(2,1)S(1)}, bf16[1,8,4,8,768]{4,3,2,1,0:T(8,128)(2,1)}, u32[]{:S(2)}) copy-start(bf16[1,8,4,8,768]{4,3,2,1,0:T(8,128)(2,1)} %get-tuple-element.363) | copy-start | bytes 1179652
  321.8 4.0 copy-start.11
  328.6 443.3 %all-gather.2.cloned.1.call-start = ((), (), s32[]{:S(2)}) async-start(), calls=%async_computation.2 | async-start | bytes 5308416 | tf_op jit(solution)/shard_map/all_gather | solution.py:149
  330.4 7.1 copy-start.7
  331.4 6.3 copy-start.10
  331.4 309.0 %copy-start.2 = (f32[6,256,256]{1,2,0:T(8,128)S(1)}, f32[6,256,256]{1,2,0:T(8,128)}, u32[]{:S(2)}) copy-start(f32[6,256,256]{1,2,0:T(8,128)} %get-tuple-element.369) | copy-start | bytes 4718596
  331.4 309.0 %copy-start.12 = (pred[256]{0:T(512)(128)(4,1)S(1)}, pred[256]{0:T(512)(128)(4,1)}, u32[]{:S(2)}) copy-start(pred[256]{0:T(512)(128)(4,1)} %copy-done.11) | copy-start | bytes 772
  333.3 307.5 %copy-start.9 = (f32[6,256]{1,0:T(8,128)S(1)}, f32[6,256]{1,0:T(8,128)}, u32[]{:S(2)}) copy-start(f32[6,256]{1,0:T(8,128)} %pmax.7) | copy-start | bytes 18436
  333.3 310.6 %collective-permute-start.2 = (bf16[2,16,4,8,768]{4,3,2,1,0:T(8,128)(2,1)}, bf16[2,16,4,8,768]{4,3,2,1,0:T(8,128)(2,1)}, u32[]{:S(2)}, u32[]{:S(2)}) collective-permute-start(bf16[2,16,4,8,768]{4,3,2,1,0:T(8,128)(2,1)} %constant_dynamic-update-slice_fusion.1), channel_id=1, source_target_pairs={{0,2},{2,4},{4,6},{6,8},{8,10},{10,12},{12,14},{1,3},{3,5},{5,7},{... | collective-permute-start | bytes 4718600 | tf_op jit(solution)/shard_map/ppermute | solution.py:15
  335.9 308.0 %collective-permute-start.3 = (bf16[2,16,4,8,768]{4,3,2,1,0:T(8,128)(2,1)}, bf16[2,16,4,8,768]{4,3,2,1,0:T(8,128)(2,1)}, u32[]{:S(2)}, u32[]{:S(2)}) collective-permute-start(bf16[2,16,4,8,768]{4,3,2,1,0:T(8,128)(2,1)} %constant_dynamic-update-slice_fusion.1), channel_id=1, source_target_pairs={{2,0},{4,2},{6,4},{8,6},{10,8},{12,10},{14,12},{3,1},{5,3},{7,5},{... | collective-permute-start | bytes 4718600 | tf_op jit(solution)/shard_map/ppermute | solution.py:18
  337.2 592.3 %reduce-scatter.2.cloned.1.call-start = ((), (), s32[]{:S(2)}) async-start(), calls=%async_computation.3 | async-start | bytes 4718592 | tf_op jit(solution)/shard_map/reduce_scatter | solution.py:152
  337.6 305.1 %copy-start.8 = (bf16[256,768]{0,1:T(8,128)(2,1)}, bf16[256,768]{0,1:T(8,128)(2,1)S(1)}, u32[]{:S(2)}) copy-start(bf16[256,768]{0,1:T(8,128)(2,1)S(1)} %copy.22) | copy-start | bytes 1179652
  643.9 4.1 copy-start.3
  643.9 4.1 copy-start.14
  705.1 4.0 copy-start.15
  705.1 4.8 copy-start.13
  767.1 4.0 copy-start.15
  767.1 4.8 copy-start.13
  (5 other events, 8.4 us)
Sparse Core Ops, SparseCore 0:
  328.7 288.1 all-reduce.1
  778.9 150.5 reduce-scatter.1
Sparse Core Ops, SparseCore 1:
  337.3 125.9 all-gather.1
where the time goes:
time: 941 us; the launch traced here: 940 us
  blocking collectives  606 us (64%)
  waiting for transfers between devices  151 us (16%)
  local copies, waits for them, and re-layouts  118 us (13%)
  matrix products  24.8 us (3%)
  between operations  15.7 us (2%)
  starting transfers between devices  9.94 us (1%)
    pmax x1, blocking collectives, shards(): global_high = lax.pmax(part_high, ('tm', 'height'))  303 us
    psum x1, blocking collectives, shards(): lax.psum((part_total * rescale, part_sums * rescale[..., None]), ('tm', '...  303 us
    reduce_scatter x1, waiting for transfers between devices, shards(): lax.psum_scatter(terms.astype(jnp.bfloat16), 'head', scatter_dimension=1,...  151 us
    reshape x2, local copies, waits for them, and re-layouts, one_pair(): cell_mask = jnp.broadcast_to(chosen.reshape(1, 1, tiles_w, 1, 3, 1, 3, 1,...  38.3 us
    broadcast_in_dim x2, local copies, waits for them, and re-layouts, one_pair(): jnp.broadcast_to(chosen.reshape(1, 1, tiles_w, 1, 3, 1, 3, 1, tiles_w, 1)...  25.6 us
  transfers between devices with their start and end apart: 7, of which 1 were waited for; matrix products, arithmetic and copies ran while one was open for 14% of the time, Pallas kernels for 0%

commit v1 on v0

v1 whole, which is shorter than its diff:
```python
import functools

import jax
import jax.numpy as jnp
from jax import lax
from jax.experimental import pallas as pl
from jax.experimental.pallas import tpu as pltpu
from jax.sharding import PartitionSpec as P

HEAD_DIM = 128
TILE = 4
HEADS_HERE = 6
PAIR = 128
OWN = 256
TEXT = 256
WIDTH = HEADS_HERE * HEAD_DIM
RANKS = 128
ROWS_EACH = HEADS_HERE * TEXT // RANKS
SLOT = 16
SCALE2 = HEAD_DIM ** (-0.5) * 1.4426950408889634
LOW = -1e30
BF = jnp.bfloat16
F32 = jnp.float32


def dot_t(a, b):
    return lax.dot_general(a, b, (((1,), (1,)), ((), ())), preferred_element_type=F32)


def dot(a, b):
    return jnp.dot(a, b, preferred_element_type=F32)


def text_part_kernel(pos, valid, tq, kv, tk, tv, out, acc_s, stat_s):
    head = pl.program_id(0)
    first = (pos[0] == 0) & (pos[1] == 0)
    q = tq[...]
    s_own = dot_t(q, kv[0]) * SCALE2
    bias = jnp.where((valid[...] > 0) & first, 0.0, LOW)
    s_text = dot_t(q, tk[...]) * SCALE2 + bias
    high = jnp.max(jnp.maximum(s_own, s_text), axis=1, keepdims=True)
    high = high.astype(BF).astype(F32)
    p_own = jnp.exp2(s_own - high)
    p_text = jnp.exp2(s_text - high)
    total = jnp.sum(p_own + p_text, axis=1, keepdims=True)
    acc = dot(p_own.astype(BF), kv[1]) + dot(p_text.astype(BF), tv[...])
    rows = pl.ds(pl.multiple_of(head * TEXT, TEXT), TEXT)
    acc_s[rows, :] = acc
    lane = lax.broadcasted_iota(jnp.int32, (TEXT, HEAD_DIM), 1)
    total_high = total.astype(BF).astype(F32)
    stat_s[rows, :] = jnp.where(
        lane < SLOT, high, jnp.where(lane < 2 * SLOT, total_high, total - total_high)
    )

    @pl.when(head == HEADS_HERE - 1)
    def _():
        row = lax.broadcasted_iota(jnp.int32, (SLOT, HEAD_DIM), 0)
        col = lax.broadcasted_iota(jnp.int32, (SLOT, HEAD_DIM), 1)
        same = (jnp.bitwise_and(col, SLOT - 1) == row) & (row < ROWS_EACH) & (col < 3 * SLOT)
        for rank in range(RANKS):
            start = rank * ROWS_EACH
            part = acc_s[start : start + SLOT, :]
            stat = stat_s[start : start + SLOT, :]
            stat_row = jnp.sum(jnp.where(same, stat, 0.0), axis=0, keepdims=True)
            full = jnp.where(row < ROWS_EACH, part, jnp.where(row == ROWS_EACH, stat_row, 0.0))
            out[rank] = full.astype(BF)


def text_part(pos, valid, tq, kv, tk, tv):
    col = lambda h, *_: (0, h)
    return pl.pallas_call(
        text_part_kernel,
        grid_spec=pltpu.PrefetchScalarGridSpec(
            num_scalar_prefetch=1,
            grid=(HEADS_HERE,),
            in_specs=[
                pl.BlockSpec((1, TEXT), lambda h, *_: (0, 0)),
                pl.BlockSpec((TEXT, HEAD_DIM), col),
                pl.BlockSpec((2, OWN, HEAD_DIM), lambda h, *_: (0, 0, h)),
                pl.BlockSpec((TEXT, HEAD_DIM), col),
                pl.BlockSpec((TEXT, HEAD_DIM), col),
            ],
            out_specs=pl.BlockSpec((RANKS, SLOT, HEAD_DIM), lambda h, *_: (0, 0, 0)),
            scratch_shapes=[
                pltpu.VMEM((HEADS_HERE * TEXT + SLOT, HEAD_DIM), F32),
                pltpu.VMEM((HEADS_HERE * TEXT + SLOT, HEAD_DIM), F32),
            ],
        ),
        out_shape=jax.ShapeDtypeStruct((RANKS, SLOT, HEAD_DIM), BF),
        compiler_params=pltpu.CompilerParams(vmem_limit_bytes=32 << 20),
        name="text_part",
    )(pos, valid, tq, kv, tk, tv)


def combine_kernel(parts, out):
    count = RANKS * SLOT
    data = parts[...].reshape(count, HEAD_DIM)
    sel_row = lax.broadcasted_iota(jnp.int32, (RANKS, count), 0)
    sel_col = lax.broadcasted_iota(jnp.int32, (RANKS, count), 1)
    pick = jnp.where(sel_col == sel_row * SLOT + ROWS_EACH, 1.0, 0.0).astype(BF)
    stats = dot(pick, data)
    high = jnp.max(stats, axis=0, keepdims=True)
    weight = jnp.exp2(stats - high)
    totals = pltpu.roll(stats, HEAD_DIM - SLOT, 1) + pltpu.roll(stats, HEAD_DIM - 2 * SLOT, 1)
    total = jnp.sum(weight * totals, axis=0, keepdims=True)
    lane = lax.broadcasted_iota(jnp.int32, (RANKS, HEAD_DIM), 1)
    weight = jnp.where(lane < ROWS_EACH, weight / total, 0.0)
    weight_high = weight.astype(BF)
    weight_low = (weight - weight_high.astype(F32)).astype(BF)
    ex_row = lax.broadcasted_iota(jnp.int32, (count, RANKS), 0)
    ex_col = lax.broadcasted_iota(jnp.int32, (count, RANKS), 1)
    spread = jnp.where(lax.shift_right_logical(ex_row, 4) == ex_col, 1.0, 0.0).astype(BF)
    diag = jnp.bitwise_and(ex_row, SLOT - 1) == ex_col
    total_rows = jnp.zeros((HEAD_DIM, HEAD_DIM), F32)
    for part in (weight_high, weight_low):
        grown = jnp.where(diag, dot(spread, part), 0.0).astype(BF)
        total_rows += lax.dot_general(
            grown, data, (((0,), (0,)), ((), ())), preferred_element_type=F32
        )
    done = total_rows[:SLOT].astype(BF)
    for rank in range(RANKS):
        out[rank] = done


def combine(parts):
    return pl.pallas_call(
        combine_kernel,
        out_shape=jax.ShapeDtypeStruct((RANKS, SLOT, HEAD_DIM), BF),
        compiler_params=pltpu.CompilerParams(vmem_limit_bytes=32 << 20),
        name="text_combine",
    )(parts)


def unpack_kernel(parts, out, flat):
    for rank in range(RANKS):
        start = rank * ROWS_EACH
        flat[start : start + ROWS_EACH, :] = parts[rank].astype(F32)[:ROWS_EACH]
    for head in range(HEADS_HERE):
        out[:, head * HEAD_DIM : (head + 1) * HEAD_DIM] = flat[
            head * TEXT : (head + 1) * TEXT, :
        ].astype(BF)


def unpack(parts):
    return pl.pallas_call(
        unpack_kernel,
        out_shape=jax.ShapeDtypeStruct((TEXT, WIDTH), BF),
        scratch_shapes=[pltpu.VMEM((HEADS_HERE * TEXT, HEAD_DIM), F32)],
        compiler_params=pltpu.CompilerParams(vmem_limit_bytes=32 << 20),
        name="text_unpack",
    )(parts)


def video_kernel(pos, mask, valid, q, tk, tv, own, *rest):
    chunks = rest[:10]
    out, bias_s = rest[10:]

    @pl.when(pl.program_id(0) == 0)
    def _():
        row = lax.broadcasted_iota(jnp.int32, (8, PAIR), 0)
        col = lax.broadcasted_iota(jnp.int32, (8, PAIR), 1)
        second_q = row >= TILE
        second_k = jnp.bitwise_and(col, 7) >= TILE
        for a in range(2):
            for i in range(3):
                for j in range(3):
                    where_t = pos[0] * 2 + a + i - 1
                    where_h = pos[1] + j - 1
                    inside = (where_t >= 0) & (where_t < pos[3]) & (where_h >= 0) & (where_h < pos[4])
                    base = 9 * i + 3 * j

                    def one(c, k):
                        if base + k == 13:
                            return jnp.where(inside, 0.0, LOW)
                        ok = inside & (mask[(a * 2 + c) * 27 + base + k] > 0)
                        return jnp.where(ok, 0.0, LOW)

                    low = jnp.where(second_k, one(0, 2), one(0, 1))
                    high = jnp.where(second_k, one(1, 1), one(1, 0))
                    bias_s[a, i, j] = jnp.where(second_q, high, low)

    text_bias = jnp.where(valid[...] > 0, 0.0, LOW)
    low_t, own_low, own_high, high_t = (
        [chunks[0], chunks[1], chunks[2]],
        [chunks[3], None, chunks[4]],
        [chunks[5], None, chunks[6]],
        [chunks[7], chunks[8], chunks[9]],
    )

    def load(ref, part, a):
        if ref is None:
            return own[part, a * PAIR : (a + 1) * PAIR, :]
        return ref[part]

    def rows(part):
        return (
            jnp.concatenate([load(r, part, 0) for r in low_t], axis=0),
            jnp.concatenate(
                [load(r, part, 0) for r in own_low] + [load(r, part, 1) for r in own_high],
                axis=0,
            ),
            jnp.concatenate([load(r, part, 0) for r in high_t], axis=0),
        )

    queries = q[...]
    k_low, k_mid, k_high = rows(0)
    v_low, v_mid, v_high = rows(1)
    s_mid = dot_t(queries, k_mid)
    s_text = dot_t(queries, tk[...])
    s_sides = (dot_t(queries[:PAIR], k_low), dot_t(queries[PAIR:], k_high))
    v_sides = (v_low, v_high)
    for a in range(2):
        mine = slice(a * PAIR, (a + 1) * PAIR)
        pieces = []
        for i in range(3):
            for j in range(3):
                at = (a + i - 1) * 3 + j
                if 0 <= a + i - 1 <= 1:
                    piece = s_mid[mine, at * PAIR : (at + 1) * PAIR]
                else:
                    piece = s_sides[a][:, j * PAIR : (j + 1) * PAIR]
                piece = piece.reshape(PAIR // 8, 8, PAIR) * SCALE2 + bias_s[a, i, j][None]
                pieces.append(piece.reshape(PAIR, PAIR))
        text_piece = s_text[mine] * SCALE2 + text_bias
        pieces.append(text_piece[:, :PAIR])
        pieces.append(text_piece[:, PAIR:])
        high = functools.reduce(jnp.maximum, pieces)
        high = jnp.max(high, axis=1, keepdims=True)
        weights = [jnp.exp2(piece - high) for piece in pieces]
        total = jnp.sum(functools.reduce(jnp.add, weights), axis=1, keepdims=True)
        weights = [w.astype(BF) for w in weights]
        side = weights[:3] if a == 0 else weights[6:9]
        mid = weights[3:9] if a == 0 else weights[:6]
        mixed = (
            dot(jnp.concatenate(side, axis=1), v_sides[a])
            + dot(jnp.concatenate(mid, axis=1), v_mid)
            + dot(jnp.concatenate(weights[9:], axis=1), tv[...])
        )
        out[mine, :] = (mixed / total).astype(BF)


def video_attention(pos, mask, valid, q, tk, tv, own, chunks):
    col = lambda h, *_: (0, h)
    col3 = lambda h, *_: (0, 0, h)
    return pl.pallas_call(
        video_kernel,
        grid_spec=pltpu.PrefetchScalarGridSpec(
            num_scalar_prefetch=2,
            grid=(HEADS_HERE,),
            in_specs=[
                pl.BlockSpec((1, TEXT), lambda h, *_: (0, 0)),
                pl.BlockSpec((OWN, HEAD_DIM), col),
                pl.BlockSpec((TEXT, HEAD_DIM), col),
                pl.BlockSpec((TEXT, HEAD_DIM), col),
                pl.BlockSpec((2, OWN, HEAD_DIM), col3),
            ]
            + [pl.BlockSpec((2, PAIR, HEAD_DIM), col3)] * 10,
            out_specs=pl.BlockSpec((OWN, HEAD_DIM), col),
            scratch_shapes=[pltpu.VMEM((2, 3, 3, 8, PAIR), F32)],
        ),
        out_shape=jax.ShapeDtypeStruct((OWN, WIDTH), BF),
        compiler_params=pltpu.CompilerParams(vmem_limit_bytes=40 << 20),
        name="video_attention",
    )(pos, mask, valid, q, tk, tv, own, *chunks)


def share_kernel(pos, rows, w, out):
    out[...] = dot(rows[...], w[...]).astype(BF)


def finish_kernel(pos, rows, w, other, out):
    out[...] = (dot(rows[...], w[...]) + other[...].astype(F32)).astype(BF)


def project(pos, rows, w_all, other):
    count = rows.shape[0]
    depth, width = w_all.shape[0] // 8, w_all.shape[1]
    if other is None:
        pick = lambda g, p: ((1 - p[2]) * 4 + g, 0)
    else:
        pick = lambda g, p: (p[2] * 4 + g, 0)
    specs = [
        pl.BlockSpec((count, WIDTH), lambda g, p: (0, 0)),
        pl.BlockSpec((depth, width), pick),
    ]
    args = [rows, w_all]
    if other is not None:
        specs.append(pl.BlockSpec((count, width), lambda g, p: (0, g)))
        args.append(other)
    return pl.pallas_call(
        share_kernel if other is None else finish_kernel,
        grid_spec=pltpu.PrefetchScalarGridSpec(
            num_scalar_prefetch=1,
            grid=(4,),
            in_specs=specs,
            out_specs=pl.BlockSpec((count, width), lambda g, p: (0, g)),
        ),
        out_shape=jax.ShapeDtypeStruct((count, 4 * width), BF),
        compiler_params=pltpu.CompilerParams(vmem_limit_bytes=32 << 20),
        name="project_share" if other is None else "project_finish",
    )(pos, *args)


def shards(video_q, video_kv, text_q, text_k, text_v, tile_mask, text_valid, w_out):
    frames, rows, cols, width = video_q.shape
    t_count, h_count = lax.axis_size("tm"), lax.axis_size("height")
    zero = jnp.int32(0)
    pos = jnp.stack(
        [
            lax.axis_index("tm"),
            lax.axis_index("height"),
            lax.axis_index("head"),
            zero + t_count * 2,
            zero + h_count,
        ]
    ).astype(jnp.int32)
    mask = tile_mask.reshape(-1)
    valid = text_valid.reshape(1, TEXT)
    own = video_kv.reshape(2, OWN, width)
    q = video_q.reshape(OWN, width)
    early, late = own[:, :PAIR], own[:, PAIR:]

    def up(x, axis, n):
        return lax.ppermute(x, axis, [(i, i + 1) for i in range(n - 1)])

    def down(x, axis, n):
        return lax.ppermute(x, axis, [(i + 1, i) for i in range(n - 1)])

    zl_late, zh_late = up(late, "height", h_count), down(late, "height", h_count)
    tm_low, tm_high = up(late, "tm", t_count), down(early, "tm", t_count)
    zl_early, zh_early = up(early, "height", h_count), down(early, "height", h_count)
    low_zl, low_zh = up(zl_late, "tm", t_count), up(zh_late, "tm", t_count)
    high_zl, high_zh = down(zl_early, "tm", t_count), down(zh_early, "tm", t_count)
    w_all = lax.all_gather(w_out, "height", axis=0, tiled=True)

    parts = text_part(pos, valid, text_q, own, text_k, text_v)
    parts = lax.all_to_all(parts, ("tm", "height"), 0, 0, tiled=True)
    parts = combine(parts)
    parts = lax.all_to_all(parts, ("tm", "height"), 0, 0, tiled=True)
    text_rows = unpack(parts)

    chunks = [low_zl, tm_low, low_zh, zl_early, zh_early, zl_late, zh_late, high_zl, tm_high, high_zh]
    video_rows = video_attention(pos, mask, valid, q, text_k, text_v, own, chunks)

    swap = [(0, 1), (1, 0)]
    video_share = lax.ppermute(project(pos, video_rows, w_all, None), "head", swap)
    text_share = lax.ppermute(project(pos, text_rows, w_all, None), "head", swap)
    video_out = project(pos, video_rows, w_all, video_share)
    text_out = project(pos, text_rows, w_all, text_share)
    return video_out.reshape(frames, rows, cols, -1), text_out


def solution(mesh):
    return jax.shard_map(
        shards,
        mesh=mesh,
        in_specs=(
            P("tm", "height", None, "head"),
            P(None, "tm", "height", None, "head"),
            P(None, "head"),
            P(None, "head"),
            P(None, "head"),
            P("tm", "height", None, None),
            P(),
            P("head", "height"),
        ),
        out_specs=(P("tm", "height", None, "head"), P(None, "head")),
        check_vma=False,
    )
```

time: 941 us -> 167 us (0.18)
  blocking collectives: 606 us -> 42.1 us
  waiting for transfers between devices: 151 us -> 38.6 us
  local copies, waits for them, and re-layouts: 118 us -> 11.7 us
  matrix products: 24.8 us -> 0 us
  Pallas kernels: 0 us -> 24.4 us
  starting transfers between devices: 9.94 us -> 33.5 us
    pmax x1 -> x0, blocking collectives: 303 us -> none  [shards(): global_high = lax.pmax(part_high, ('tm', 'height'))]
    psum x1 -> x0, blocking collectives: 303 us -> none  [shards(): lax.psum((part_total * rescale, part_sums * rescale[..., None]), ('tm', '...]
    reduce_scatter x1 -> x0, waiting for transfers between devices: 151 us -> none  [shards(): lax.psum_scatter(terms.astype(jnp.bfloat16), 'head', scatter_dimension=1,...]
    all_to_all x0 -> x1, blocking collectives: none -> 42.1 us  [shards(): parts = lax.all_to_all(parts, ('tm', 'height'), 0, 0, tiled=True)]
    reshape x6 -> x1, local copies, waits for them, and re-layouts: 39 us -> 0.08 us  [shards(): mask = tile_mask.reshape(-1)]
    ppermute x4 -> x12, waiting for transfers between devices: 0.01 us -> 37.9 us  [the longest x5 25.1 us: up(): return lax.ppermute(x, axis, [(i, i + 1) for i in range(n - 1)])]
    broadcast_in_dim x2 -> x0, local copies, waits for them, and re-layouts: 25.6 us -> none  [one_pair(): jnp.broadcast_to(chosen.reshape(1, 1, tiles_w, 1, 3, 1, 3, 1, tiles_w, 1)...]
    dot_general x9 -> x0, matrix products: 24.8 us -> none  [the longest x2 7.62 us: attend_block(): jnp.einsum('hqk,khd->qhd', weights.astype(jnp.bfloat16), v_split, preferr...]
  transfers between devices with their start and end apart: 7 -> 14, of which waited for: 1 -> 6; matrix products, arithmetic and copies ran while one was open for 14% -> 1% of each run, Pallas kernels for 0% -> 12%
where the time goes in v1:
time: 167 us; the launch traced here: 165 us
  blocking collectives  42.1 us (25%)
  waiting for transfers between devices  38.6 us (23%)
  starting transfers between devices  33.5 us (20%)
  Pallas kernels  24.4 us (15%)
  between operations  14.3 us (9%)
  local copies, waits for them, and re-layouts  11.7 us (7%)
    all_to_all x1, blocking collectives, shards(): parts = lax.all_to_all(parts, ('tm', 'height'), 0, 0, tiled=True)  42.1 us
    ppermute x5, waiting for transfers between devices, up(): return lax.ppermute(x, axis, [(i, i + 1) for i in range(n - 1)])  25.1 us
    ppermute x5, starting transfers between devices, up(): return lax.ppermute(x, axis, [(i, i + 1) for i in range(n - 1)])  18.1 us
    ppermute x5, waiting for transfers between devices, down(): return lax.ppermute(x, axis, [(i + 1, i) for i in range(n - 1)])  12.8 us
    unnamed x34, local copies, waits for them, and re-layouts  10.7 us
    pallas_call x4, Pallas kernels, project(): pl.pallas_call(share_kernel if other is None else finish_kernel, grid_spe...  10.5 us
    pallas_call x1, Pallas kernels, video_attention(): pl.pallas_call(video_kernel, grid_spec=pltpu.PrefetchScalarGridSpec(num_s...  7.75 us
    ppermute x5, starting transfers between devices, down(): return lax.ppermute(x, axis, [(i + 1, i) for i in range(n - 1)])  6.41 us
  transfers between devices with their start and end apart: 14, of which 6 were waited for; matrix products, arithmetic and copies ran while one was open for 1% of the time, Pallas kernels for 12%

profile of v1, /device:TPU:1, one launch (start us, length us, event | category | flops | bytes accessed | tf_op | source)
XLA Modules:
  0.0 164.5 jit_solution(16234388082906935120)
XLA Ops:
  12.8 4.0 %text_part.1 = bf16[128,16,128]{2,1,0:T(8,128)(2,1)S(1)} custom-call(s32[5]{0:T(128)S(1)} %stack.15.pos, s32[1,256]{1,0:T(1,128)S(1)} %bitcast.11, bf16[256,768]{1,0:T(8,128)(2,1)S(1)} %copy-done.8, bf16[2,256,768]{2,1,0:T(8,128)(2,1)S(1)} %bitcast.7, bf16[256,768]{1,0:T(8,128)(2,1)S(1)} %copy-done.4, bf16[256,768]{1,0:T(8,128)(2,1)S(1)} %copy-done.6), custom_call_target="tpu_custom_call" | custom-call | tf_op jit(solution)/shard_map/text_part/pallas_call | solution.py:71
  16.8 42.1 %all_to_all.10.parts = bf16[128,16,128]{2,1,0:T(8,128)(2,1)S(1)} all-to-all(bf16[128,16,128]{2,1,0:T(8,128)(2,1)S(1)} %text_part.1), channel_id=1, replica_groups=mesh['tm'=16,'height'=8,'head'=2] {'tm','height'}, dimensions={0} | all-to-all | bytes 1048576 | tf_op jit(solution)/shard_map/all_to_all | solution.py:337
  58.9 2.0 %text_combine.1 = bf16[128,16,128]{2,1,0:T(8,128)(2,1)} custom-call(bf16[128,16,128]{2,1,0:T(8,128)(2,1)S(1)} %all_to_all.10.parts), custom_call_target="tpu_custom_call" | custom-call | tf_op jit(solution)/shard_map/text_combine/pallas_call | solution.py:126
  60.9 6.2 %all-to-all-start.1 = ((bf16[128,16,128]{2,1,0:T(8,128)(2,1)}), bf16[128,16,128]{2,1,0:T(8,128)(2,1)S(1)}, u32[]{:S(2)}, u32[]{:S(2)}) async-start(bf16[128,16,128]{2,1,0:T(8,128)(2,1)} %text_combine.1), calls=%async_computation.1 | async-start | bytes 1048576 | tf_op jit(solution)/shard_map/all_to_all | solution.py:339
  67.9 2.4 %collective-permute-start = (bf16[2,128,768]{2,1,0:T(8,128)(2,1)S(1)}, bf16[2,128,768]{2,1,0:T(8,128)(2,1)S(1)}, u32[]{:S(2)}, u32[]{:S(2)}) collective-permute-start(bf16[2,128,768]{2,1,0:T(8,128)(2,1)S(1)} %get-tuple-element.3), channel_id=1, source_target_pairs={{0,2},{2,4},{4,6},{6,8},{8,10},{10,12},{12,14},{1,3},{3,5},{5,7},{... | collective-permute-start | bytes 1179656 | tf_op jit(solution)/shard_map/ppermute | solution.py:324
  70.2 1.3 collective-permute-start.3
  71.5 4.7 %collective-permute-start.5 = (bf16[2,128,768]{2,1,0:T(8,128)(2,1)}, bf16[2,128,768]{2,1,0:T(8,128)(2,1)}, u32[]{:S(2)}, u32[]{:S(2)}) collective-permute-start(bf16[2,128,768]{2,1,0:T(8,128)(2,1)} %get-tuple-element.2), channel_id=1, source_target_pairs={{0,2},{2,4},{4,6},{6,8},{8,10},{10,12},{12,14},{1,3},{3,5},{5,7},{... | collective-permute-start | bytes 1179656 | tf_op jit(solution)/shard_map/ppermute | solution.py:324
  76.3 1.3 collective-permute-start.6
  77.6 3.2 %collective-permute-start.2 = (bf16[2,128,768]{2,1,0:T(8,128)(2,1)S(1)}, bf16[2,128,768]{2,1,0:T(8,128)(2,1)S(1)}, u32[]{:S(2)}, u32[]{:S(2)}) collective-permute-start(bf16[2,128,768]{2,1,0:T(8,128)(2,1)S(1)} %get-tuple-element.3), channel_id=1, source_target_pairs={{0,16},{16,32},{32,48},{48,64},{64,80},{80,96},{96,112},{112,128},... | collective-permute-start | bytes 1179656 | tf_op jit(solution)/shard_map/ppermute | solution.py:324
  80.8 18.5 %collective-permute-done.rest_5_ = bf16[2,128,768]{2,1,0:T(8,128)(2,1)S(1)} collective-permute-done((bf16[2,128,768]{2,1,0:T(8,128)(2,1)S(1)}, bf16[2,128,768]{2,1,0:T(8,128)(2,1)S(1)}, u32[]{:S(2)}, u32[]{:S(2)}) %collective-permute-start) | collective-permute-done | bytes 393248 | tf_op jit(solution)/shard_map/ppermute | solution.py:324
  101.2 4.1 %collective-permute-start.1 = (bf16[2,128,768]{2,1,0:T(8,128)(2,1)S(1)}, bf16[2,128,768]{2,1,0:T(8,128)(2,1)}, u32[]{:S(2)}, u32[]{:S(2)}) collective-permute-start(bf16[2,128,768]{2,1,0:T(8,128)(2,1)S(1)} %collective-permute-done.rest_5_), channel_id=1, source_target_pairs={{0,16},{16,32},{32,48},{48,64},{64,80},{80,96},{96,112},{112,128},... | collective-permute-start | bytes 1179656 | tf_op jit(solution)/shard_map/ppermute | solution.py:324
  105.3 2.6 %collective-permute-done.5.rest_3_ = bf16[2,128,768]{2,1,0:T(8,128)(2,1)} collective-permute-done((bf16[2,128,768]{2,1,0:T(8,128)(2,1)}, bf16[2,128,768]{2,1,0:T(8,128)(2,1)}, u32[]{:S(2)}, u32[]{:S(2)}) %collective-permute-start.5) | collective-permute-done | bytes 393248 | tf_op jit(solution)/shard_map/ppermute | solution.py:324
  107.9 3.7 %collective-permute-start.4 = (bf16[2,128,768]{2,1,0:T(8,128)(2,1)S(1)}, bf16[2,128,768]{2,1,0:T(8,128)(2,1)}, u32[]{:S(2)}, u32[]{:S(2)}) collective-permute-start(bf16[2,128,768]{2,1,0:T(8,128)(2,1)S(1)} %collective-permute-done.3.rest_6_), channel_id=1, source_target_pairs={{0,16},{16,32},{32,48},{48,64},{64,80},{80,96},{96,112},{112,128},... | collective-permute-start | bytes 1179656 | tf_op jit(solution)/shard_map/ppermute | solution.py:324
  112.4 1.3 collective-permute-start.7
  115.9 3.9 %collective-permute-done.4.rest_2_ = bf16[2,128,768]{2,1,0:T(8,128)(2,1)} collective-permute-done((bf16[2,128,768]{2,1,0:T(8,128)(2,1)S(1)}, bf16[2,128,768]{2,1,0:T(8,128)(2,1)}, u32[]{:S(2)}, u32[]{:S(2)}) %collective-permute-start.4) | collective-permute-done | bytes 393248 | tf_op jit(solution)/shard_map/ppermute | solution.py:324
  119.8 3.8 %collective-permute-done.7.rest_7_ = bf16[2,128,768]{2,1,0:T(8,128)(2,1)} collective-permute-done((bf16[2,128,768]{2,1,0:T(8,128)(2,1)}, bf16[2,128,768]{2,1,0:T(8,128)(2,1)}, u32[]{:S(2)}, u32[]{:S(2)}) %collective-permute-start.7) | collective-permute-done | bytes 393248 | tf_op jit(solution)/shard_map/ppermute | solution.py:327
  123.6 8.4 %collective-permute-done.9.rest_9_ = bf16[2,128,768]{2,1,0:T(8,128)(2,1)} collective-permute-done((bf16[2,128,768]{2,1,0:T(8,128)(2,1)}, bf16[2,128,768]{2,1,0:T(8,128)(2,1)}, u32[]{:S(2)}, u32[]{:S(2)}) %collective-permute-start.9) | collective-permute-done | bytes 393248 | tf_op jit(solution)/shard_map/ppermute | solution.py:327
  134.0 7.8 %video_attention.1.rows = bf16[256,768]{1,0:T(8,128)(2,1)S(1)} custom-call(s32[5]{0:T(128)S(1)} %stack.15.pos, s32[108]{0:T(128)S(1)} %reshape.19.mask, s32[1,256]{1,0:T(1,128)S(1)} %bitcast.12, bf16[256,768]{1,0:T(8,128)(2,1)S(1)} %bitcast.10, bf16[256,768]{1,0:T(8,128)(2,1)S(1)} %copy-done.5, bf16[256,768]{1,0:T(8,128)(2,1)S(1)} %copy-done.7, ...), custom_call_target="tpu_custom_call" | custom-call | tf_op jit(solution)/shard_map/video_attention/pallas_call | solution.py:245
  142.0 2.3 %copy-done = bf16[6144,384]{1,0:T(8,128)(2,1)S(1)} copy-done((bf16[6144,384]{1,0:T(8,128)(2,1)S(1)}, bf16[6144,384]{1,0:T(8,128)(2,1)}, u32[]{:S(2)}) %copy-start) | copy-done | bytes 4718616
  144.3 2.1 %project_share.2 = bf16[256,1536]{1,0:T(8,128)(2,1)S(1)} custom-call(s32[5]{0:T(128)S(1)} %stack.15.pos, bf16[256,768]{1,0:T(8,128)(2,1)S(1)} %video_attention.1.rows, bf16[6144,384]{1,0:T(8,128)(2,1)S(1)} %copy-done), custom_call_target="tpu_custom_call" | custom-call | tf_op jit(solution)/shard_map/project_share/pallas_call | solution.py:290
  146.5 2.6 %collective-permute-start.10 = (bf16[256,1536]{1,0:T(8,128)(2,1)S(1)}, bf16[256,1536]{1,0:T(8,128)(2,1)S(1)}, u32[]{:S(2)}, u32[]{:S(2)}) collective-permute-start(bf16[256,1536]{1,0:T(8,128)(2,1)S(1)} %project_share.2), channel_id=1, source_target_pairs={{0,1},{1,0},{2,3},{3,2},{4,5},{5,4},{6,7},{7,6},{8,9},{9,8},{10,11... | collective-permute-start | bytes 2359304 | tf_op jit(solution)/shard_map/ppermute | solution.py:346
  149.1 2.1 %project_share.3 = bf16[256,1536]{1,0:T(8,128)(2,1)S(1)} custom-call(s32[5]{0:T(128)S(1)} %stack.15.pos, bf16[256,768]{1,0:T(8,128)(2,1)S(1)} %text_unpack.1.rows, bf16[6144,384]{1,0:T(8,128)(2,1)S(1)} %copy-done.1), custom_call_target="tpu_custom_call" | custom-call | tf_op jit(solution)/shard_map/project_share/pallas_call | solution.py:290
  151.4 3.1 %project_finish.2 = bf16[256,1536]{1,0:T(8,128)(2,1)} custom-call(s32[5]{0:T(128)S(1)} %stack.15.pos, bf16[256,768]{1,0:T(8,128)(2,1)S(1)} %video_attention.1.rows, bf16[6144,384]{1,0:T(8,128)(2,1)S(1)} %copy-done.1, bf16[256,1536]{1,0:T(8,128)(2,1)S(1)} %collective-permute-done.10.other), custom_call_target="tpu_custom_call" | custom-call | tf_op jit(solution)/shard_map/project_finish/pallas_call | solution.py:290
  154.5 3.1 %project_finish.3 = bf16[256,1536]{1,0:T(8,128)(2,1)} custom-call(s32[5]{0:T(128)S(1)} %stack.15.pos, bf16[256,768]{1,0:T(8,128)(2,1)S(1)} %text_unpack.1.rows, bf16[6144,384]{1,0:T(8,128)(2,1)S(1)} %copy-done.1, bf16[256,1536]{1,0:T(8,128)(2,1)S(1)} %collective-permute-done.11.other), custom_call_target="tpu_custom_call" | custom-call | tf_op jit(solution)/shard_map/project_finish/pallas_call | solution.py:290
  (51 shorter events, 13.6 us)
Async XLA Ops:
  7.2 124.9 %copy-start.15 = (s32[256]{0:T(256)S(1)}, s32[256]{0:T(256)}, u32[]{:S(2)}) copy-start(s32[256]{0:T(256)} %param.14) | copy-start | bytes 3076
  7.2 124.9 %copy-start.5 = (bf16[256,768]{1,0:T(8,128)(2,1)S(1)}, bf16[256,768]{1,0:T(8,128)(2,1)}, u32[]{:S(2)}) copy-start(bf16[256,768]{1,0:T(8,128)(2,1)} %tk.3) | copy-start | bytes 1179652
  7.2 108.6 %copy-start.16 = (s32[2,1,2,27]{3,2,1,0:T(2,128)S(1)}, s32[2,1,2,27]{3,2,1,0:T(2,128)}, u32[]{:S(2)}) copy-start(s32[2,1,2,27]{3,2,1,0:T(2,128)} %param.13) | copy-start | bytes 1300
  7.2 134.8 %all-gather.2.cloned.1.call-start = ((), (), s32[]{:S(2)}) async-start(), calls=%async_computation.2 | async-start | bytes 5308416 | tf_op jit(solution)/shard_map/all_gather | solution.py:334
  8.0 1.1 copy-start.2
  12.8 54.2 %copy-start.3 = (bf16[2,8,4,8,768]{4,3,2,1,0:T(8,128)(2,1)S(1)}, bf16[2,8,4,8,768]{4,3,2,1,0:T(8,128)(2,1)}, u32[]{:S(2)}) copy-start(bf16[2,8,4,8,768]{4,3,2,1,0:T(8,128)(2,1)} %param.9) | copy-start | bytes 2359300
  12.8 119.2 %copy-start.7 = (bf16[256,768]{1,0:T(8,128)(2,1)S(1)}, bf16[256,768]{1,0:T(8,128)(2,1)}, u32[]{:S(2)}) copy-start(bf16[256,768]{1,0:T(8,128)(2,1)} %tv.3) | copy-start | bytes 1179652
  12.8 119.2 %copy-start.9 = (bf16[8,4,8,768]{3,2,1,0:T(8,128)(2,1)S(1)}, bf16[8,4,8,768]{3,2,1,0:T(8,128)(2,1)}, u32[]{:S(2)}) copy-start(bf16[8,4,8,768]{3,2,1,0:T(8,128)(2,1)} %param.8) | copy-start | bytes 1179652
  60.9 80.9 %all-to-all-start.1 = ((bf16[128,16,128]{2,1,0:T(8,128)(2,1)}), bf16[128,16,128]{2,1,0:T(8,128)(2,1)S(1)}, u32[]{:S(2)}, u32[]{:S(2)}) async-start(bf16[128,16,128]{2,1,0:T(8,128)(2,1)} %text_combine.1), calls=%async_computation.1 | async-start | bytes 1048576 | tf_op jit(solution)/shard_map/all_to_all | solution.py:339
  67.9 31.4 %collective-permute-start = (bf16[2,128,768]{2,1,0:T(8,128)(2,1)S(1)}, bf16[2,128,768]{2,1,0:T(8,128)(2,1)S(1)}, u32[]{:S(2)}, u32[]{:S(2)}) collective-permute-start(bf16[2,128,768]{2,1,0:T(8,128)(2,1)S(1)} %get-tuple-element.3), channel_id=1, source_target_pairs={{0,2},{2,4},{4,6},{6,8},{8,10},{10,12},{12,14},{1,3},{3,5},{5,7},{... | collective-permute-start | bytes 1179656 | tf_op jit(solution)/shard_map/ppermute | solution.py:324
  70.2 30.9 %collective-permute-start.3 = (bf16[2,128,768]{2,1,0:T(8,128)(2,1)S(1)}, bf16[2,128,768]{2,1,0:T(8,128)(2,1)S(1)}, u32[]{:S(2)}, u32[]{:S(2)}) collective-permute-start(bf16[2,128,768]{2,1,0:T(8,128)(2,1)S(1)} %get-tuple-element.3), channel_id=1, source_target_pairs={{2,0},{4,2},{6,4},{8,6},{10,8},{12,10},{14,12},{3,1},{5,3},{7,5},{... | collective-permute-start | bytes 1179656 | tf_op jit(solution)/shard_map/ppermute | solution.py:327
  71.5 36.4 %collective-permute-start.5 = (bf16[2,128,768]{2,1,0:T(8,128)(2,1)}, bf16[2,128,768]{2,1,0:T(8,128)(2,1)}, u32[]{:S(2)}, u32[]{:S(2)}) collective-permute-start(bf16[2,128,768]{2,1,0:T(8,128)(2,1)} %get-tuple-element.2), channel_id=1, source_target_pairs={{0,2},{2,4},{4,6},{6,8},{8,10},{10,12},{12,14},{1,3},{3,5},{5,7},{... | collective-permute-start | bytes 1179656 | tf_op jit(solution)/shard_map/ppermute | solution.py:324
  76.3 36.1 %collective-permute-start.6 = (bf16[2,128,768]{2,1,0:T(8,128)(2,1)}, bf16[2,128,768]{2,1,0:T(8,128)(2,1)}, u32[]{:S(2)}, u32[]{:S(2)}) collective-permute-start(bf16[2,128,768]{2,1,0:T(8,128)(2,1)} %get-tuple-element.2), channel_id=1, source_target_pairs={{2,0},{4,2},{6,4},{8,6},{10,8},{12,10},{14,12},{3,1},{5,3},{7,5},{... | collective-permute-start | bytes 1179656 | tf_op jit(solution)/shard_map/ppermute | solution.py:327
  77.6 36.1 %collective-permute-start.2 = (bf16[2,128,768]{2,1,0:T(8,128)(2,1)S(1)}, bf16[2,128,768]{2,1,0:T(8,128)(2,1)S(1)}, u32[]{:S(2)}, u32[]{:S(2)}) collective-permute-start(bf16[2,128,768]{2,1,0:T(8,128)(2,1)S(1)} %get-tuple-element.3), channel_id=1, source_target_pairs={{0,16},{16,32},{32,48},{48,64},{64,80},{80,96},{96,112},{112,128},... | collective-permute-start | bytes 1179656 | tf_op jit(solution)/shard_map/ppermute | solution.py:324
  99.3 16.6 %collective-permute-start.8 = (bf16[2,128,768]{2,1,0:T(8,128)(2,1)}, bf16[2,128,768]{2,1,0:T(8,128)(2,1)}, u32[]{:S(2)}, u32[]{:S(2)}) collective-permute-start(bf16[2,128,768]{2,1,0:T(8,128)(2,1)} %get-tuple-element.2), channel_id=1, source_target_pairs={{16,0},{32,16},{48,32},{64,48},{80,64},{96,80},{112,96},{128,112},... | collective-permute-start | bytes 1179656 | tf_op jit(solution)/shard_map/ppermute | solution.py:327
  101.2 14.7 %collective-permute-start.1 = (bf16[2,128,768]{2,1,0:T(8,128)(2,1)S(1)}, bf16[2,128,768]{2,1,0:T(8,128)(2,1)}, u32[]{:S(2)}, u32[]{:S(2)}) collective-permute-start(bf16[2,128,768]{2,1,0:T(8,128)(2,1)S(1)} %collective-permute-done.rest_5_), channel_id=1, source_target_pairs={{0,16},{16,32},{32,48},{48,64},{64,80},{80,96},{96,112},{112,128},... | collective-permute-start | bytes 1179656 | tf_op jit(solution)/shard_map/ppermute | solution.py:324
  107.9 11.9 %collective-permute-start.4 = (bf16[2,128,768]{2,1,0:T(8,128)(2,1)S(1)}, bf16[2,128,768]{2,1,0:T(8,128)(2,1)}, u32[]{:S(2)}, u32[]{:S(2)}) collective-permute-start(bf16[2,128,768]{2,1,0:T(8,128)(2,1)S(1)} %collective-permute-done.3.rest_6_), channel_id=1, source_target_pairs={{0,16},{16,32},{32,48},{48,64},{64,80},{80,96},{96,112},{112,128},... | collective-permute-start | bytes 1179656 | tf_op jit(solution)/shard_map/ppermute | solution.py:324
  112.4 11.2 %collective-permute-start.7 = (bf16[2,128,768]{2,1,0:T(8,128)(2,1)}, bf16[2,128,768]{2,1,0:T(8,128)(2,1)}, u32[]{:S(2)}, u32[]{:S(2)}) collective-permute-start(bf16[2,128,768]{2,1,0:T(8,128)(2,1)} %collective-permute-done.5.rest_3_), channel_id=1, source_target_pairs={{16,0},{32,16},{48,32},{64,48},{80,64},{96,80},{112,96},{128,112},... | collective-permute-start | bytes 1179656 | tf_op jit(solution)/shard_map/ppermute | solution.py:327
  114.5 17.5 %collective-permute-start.9 = (bf16[2,128,768]{2,1,0:T(8,128)(2,1)}, bf16[2,128,768]{2,1,0:T(8,128)(2,1)}, u32[]{:S(2)}, u32[]{:S(2)}) collective-permute-start(bf16[2,128,768]{2,1,0:T(8,128)(2,1)} %collective-permute-done.6.rest_4_), channel_id=1, source_target_pairs={{16,0},{32,16},{48,32},{64,48},{80,64},{96,80},{112,96},{128,112},... | collective-permute-start | bytes 1179656 | tf_op jit(solution)/shard_map/ppermute | solution.py:327
  132.0 1.0 copy-start.11
  142.0 2.3 %copy-start = (bf16[6144,384]{1,0:T(8,128)(2,1)S(1)}, bf16[6144,384]{1,0:T(8,128)(2,1)}, u32[]{:S(2)}) copy-start(bf16[6144,384]{1,0:T(8,128)(2,1)} %all-gather.2.cloned.1.call-done.w) | copy-start | bytes 14155780
  144.3 4.8 %copy-start.1 = (bf16[6144,384]{1,0:T(8,128)(2,1)S(1)}, bf16[6144,384]{1,0:T(8,128)(2,1)}, u32[]{:S(2)}) copy-start(bf16[6144,384]{1,0:T(8,128)(2,1)} %all-gather.2.cloned.1.call-done.w) | copy-start | bytes 14155780
  146.5 4.9 %collective-permute-start.10 = (bf16[256,1536]{1,0:T(8,128)(2,1)S(1)}, bf16[256,1536]{1,0:T(8,128)(2,1)S(1)}, u32[]{:S(2)}, u32[]{:S(2)}) collective-permute-start(bf16[256,1536]{1,0:T(8,128)(2,1)S(1)} %project_share.2), channel_id=1, source_target_pairs={{0,1},{1,0},{2,3},{3,2},{4,5},{5,4},{6,7},{7,6},{8,9},{9,8},{10,11... | collective-permute-start | bytes 2359304 | tf_op jit(solution)/shard_map/ppermute | solution.py:346
  151.2 3.3 %collective-permute-start.11 = (bf16[256,1536]{1,0:T(8,128)(2,1)S(1)}, bf16[256,1536]{1,0:T(8,128)(2,1)S(1)}, u32[]{:S(2)}, u32[]{:S(2)}) collective-permute-start(bf16[256,1536]{1,0:T(8,128)(2,1)S(1)} %project_share.3), channel_id=1, source_target_pairs={{0,1},{1,0},{2,3},{3,2},{4,5},{5,4},{6,7},{7,6},{8,9},{9,8},{10,11... | collective-permute-start | bytes 2359304 | tf_op jit(solution)/shard_map/ppermute | solution.py:347
  (7 other events, 6.3 us)
Sparse Core Ops, SparseCore 0:
  9.8 92.0 all-gather.1

commit v2 on v1

v2 whole, which is shorter than its diff:
```python
import functools

import jax
import jax.numpy as jnp
from jax import lax
from jax.experimental import pallas as pl
from jax.experimental.pallas import tpu as pltpu
from jax.sharding import PartitionSpec as P

HEAD_DIM = 128
TILE = 4
HEADS_HERE = 6
PAIR = 128
OWN = 256
TEXT = 256
WIDTH = HEADS_HERE * HEAD_DIM
PLANE = 16
EACH = HEADS_HERE * TEXT // PLANE
SLOT = 112
SCALE2 = HEAD_DIM ** (-0.5) * 1.4426950408889634
LOW = -1e30
VMEM = 60 << 20
BF = jnp.bfloat16
F32 = jnp.float32


def dot_t(a, b):
    return lax.dot_general(a, b, (((1,), (1,)), ((), ())), preferred_element_type=F32)


def dot(a, b):
    return jnp.dot(a, b, preferred_element_type=F32)


def fetch(pairs, sems, columns):
    copies = []
    for at, (source, target) in enumerate(pairs):
        where = (slice(None),) * (len(source.shape) - 1) + (columns,)
        copies.append(pltpu.make_async_copy(source.at[where], target.at[where], sems.at[at]))
    for copy in copies:
        copy.start()
    return copies


def wait_all(copies):
    for copy in copies:
        copy.wait()


FIRST, REST = slice(0, HEAD_DIM), slice(HEAD_DIM, WIDTH)


def stat_rows(values):
    row = lax.broadcasted_iota(jnp.int32, (EACH, HEAD_DIM), 0)
    col = lax.broadcasted_iota(jnp.int32, (EACH, HEAD_DIM), 1)
    lines = [jnp.sum(jnp.where(row == col, v, 0.0), axis=0, keepdims=True) for v in values]
    return lay_out(lines)


def lay_out(lines):
    row = lax.broadcasted_iota(jnp.int32, (SLOT - EACH, HEAD_DIM), 0)
    full = jnp.zeros((SLOT - EACH, HEAD_DIM), F32)
    for at, line in enumerate(lines):
        full = jnp.where(row == at, line, full)
    return full.astype(BF)


def split(total):
    high = total.astype(BF).astype(F32)
    return high, total - high


def text_part_kernel(
    pos, valid, tq_h, kv_h, tk_h, tv_h, out, tq, kv, tk, tv, acc_s, high_s, total_s, sems
):
    pairs = [(tq_h, tq), (kv_h, kv), (tk_h, tk), (tv_h, tv)]
    begun = fetch(pairs, sems.at[0], FIRST)
    later = fetch(pairs, sems.at[1], REST)
    first = (pos[0] == 0) & (pos[1] == 0)
    bias = jnp.where((valid[...] > 0) & first, 0.0, LOW)
    for head in range(HEADS_HERE):
        if head == 0:
            wait_all(begun)
        elif head == 1:
            wait_all(later)
        cols = slice(head * HEAD_DIM, (head + 1) * HEAD_DIM)
        q = tq[:, cols]
        s_own = dot_t(q, kv[0, :, cols]) * SCALE2
        s_text = dot_t(q, tk[:, cols]) * SCALE2 + bias
        high = jnp.max(jnp.maximum(s_own, s_text), axis=1, keepdims=True)
        high = high.astype(BF).astype(F32)
        p_own = jnp.exp2(s_own - high)
        p_text = jnp.exp2(s_text - high)
        total = jnp.sum(p_own + p_text, axis=1, keepdims=True)
        acc = dot(p_own.astype(BF), kv[1, :, cols]) + dot(p_text.astype(BF), tv[:, cols])
        rows = slice(head * TEXT, (head + 1) * TEXT)
        acc_s[rows, :] = acc.astype(BF)
        high_s[rows, :] = jnp.broadcast_to(high, (TEXT, HEAD_DIM))
        total_s[rows, :] = jnp.broadcast_to(total, (TEXT, HEAD_DIM))

    for rank in range(PLANE):
        rows = slice(rank * EACH, (rank + 1) * EACH)
        out[rank, :EACH] = acc_s[rows, :]
        out[rank, EACH:] = stat_rows((high_s[rows, :], *split(total_s[rows, :])))


WHOLE = pl.BlockSpec(memory_space=pltpu.VMEM)
SCALARS = pl.BlockSpec(memory_space=pltpu.SMEM)
FAR = pl.BlockSpec(memory_space=pltpu.HBM)
ANY = pl.BlockSpec(memory_space=pl.ANY)


def text_part(pos, valid, tq, kv, tk, tv):
    count = HEADS_HERE * TEXT
    return pl.pallas_call(
        text_part_kernel,
        in_specs=[SCALARS, WHOLE, FAR, FAR, FAR, FAR],
        out_specs=WHOLE,
        out_shape=jax.ShapeDtypeStruct((PLANE, SLOT, HEAD_DIM), BF),
        scratch_shapes=[pltpu.VMEM(x.shape, BF) for x in (tq, kv, tk, tv)]
        + [pltpu.VMEM((count, HEAD_DIM), t) for t in (BF, F32, F32)]
        + [pltpu.SemaphoreType.DMA((2, 4))],
        cost_estimate=pl.CostEstimate(
            flops=5 * 10**9, bytes_accessed=2 << 20, transcendentals=10**6
        ),
        compiler_params=pltpu.CompilerParams(vmem_limit_bytes=VMEM),
        name="text_part",
    )(pos, valid, tq, kv, tk, tv)


def corners_kernel(own, z_low, z_high, after, low, high, held, sems):
    inward, outward = [], []
    for j, ref in enumerate((z_low, own, z_high)):
        for side, out in enumerate((low, high)):
            part = ref.at[:, pl.ds((1 - side) * PAIR, PAIR), :]
            inward.append(pltpu.make_async_copy(part, held.at[j, side], sems.at[0, j, side]))
            outward.append(pltpu.make_async_copy(held.at[j, side], out.at[j], sems.at[1, j, side]))
    for copy in inward:
        copy.start()
    for copy, onward in zip(inward, outward):
        copy.wait()
        onward.start()
    wait_all(outward)


def corners(own, z_low, z_high, after):
    shape = jax.ShapeDtypeStruct((3, 2, PAIR, WIDTH), BF)
    return pl.pallas_call(
        corners_kernel,
        in_specs=[ANY] * 4,
        out_specs=(ANY, ANY),
        out_shape=(shape, shape),
        scratch_shapes=[
            pltpu.VMEM((3, 2, 2, PAIR, WIDTH), BF),
            pltpu.SemaphoreType.DMA((2, 3, 2)),
        ],
        cost_estimate=pl.CostEstimate(flops=0, bytes_accessed=5 << 20, transcendentals=0),
        compiler_params=pltpu.CompilerParams(vmem_limit_bytes=VMEM),
        name="corners",
    )(own, z_low, z_high, after)


def merge_kernel(parts, w_h, z_low, z_high, out, w_out, w, sems):
    inward = pltpu.make_async_copy(w_h, w, sems.at[0])
    onward = pltpu.make_async_copy(w, w_out, sems.at[1])
    inward.start()
    combine_kernel(parts, out, between=lambda: (inward.wait(), onward.start()))
    onward.wait()


def combine_kernel(parts, out, between=lambda: None):
    sources, copies = parts.shape[0], out.shape[0]
    stats = [parts[i, EACH:].astype(F32) for i in range(sources)]
    highs = [s[0:1] for s in stats]
    high = functools.reduce(jnp.maximum, highs)
    weights = [jnp.exp2(h - high) for h in highs]
    total = sum(w * (s[1:2] + s[2:3]) for w, s in zip(weights, stats))
    finish = out.shape[1] == EACH
    if finish:
        lane = lax.broadcasted_iota(jnp.int32, (1, HEAD_DIM), 1)
        total = jnp.where(lane < EACH, total, 1.0)
        weights = [w / total for w in weights]
    row = lax.broadcasted_iota(jnp.int32, (HEAD_DIM, HEAD_DIM), 0)
    table = jnp.zeros((HEAD_DIM, HEAD_DIM), F32)
    for i, w in enumerate(weights):
        table = jnp.where(row == i, w, table)
    table = table.T
    between()
    sums = jnp.zeros((EACH, HEAD_DIM), F32)
    for i in range(sources):
        sums += table[:EACH, i : i + 1] * parts[i, :EACH].astype(F32)
    sums = sums.astype(BF)
    for at in range(copies):
        out[at, :EACH] = sums
    if not finish:
        lines = lay_out((high, *split(total)))
        for at in range(copies):
            out[at, EACH:] = lines


def merge(parts, copies, w, *after):
    return pl.pallas_call(
        merge_kernel,
        in_specs=[WHOLE, FAR] + [ANY] * len(after),
        out_specs=(WHOLE, FAR),
        out_shape=(
            jax.ShapeDtypeStruct((copies, SLOT, HEAD_DIM), BF),
            jax.ShapeDtypeStruct(w.shape, BF),
        ),
        scratch_shapes=[pltpu.VMEM(w.shape, BF), pltpu.SemaphoreType.DMA((2,))],
        cost_estimate=pl.CostEstimate(
            flops=10**9, bytes_accessed=2 << 20, transcendentals=0
        ),
        compiler_params=pltpu.CompilerParams(vmem_limit_bytes=16 << 20),
        name="text_merge",
    )(parts, w, *after)


def relay_kernel(low, high, after, low_out, high_out, held, sems):
    pairs = ((low, low_out), (high, high_out))
    inward = [
        pltpu.make_async_copy(ref, held.at[i], sems.at[0, i]) for i, (ref, _) in enumerate(pairs)
    ]
    onward = [
        pltpu.make_async_copy(held.at[i], out, sems.at[1, i]) for i, (_, out) in enumerate(pairs)
    ]
    for copy in inward:
        copy.start()
    for copy, following in zip(inward, onward):
        copy.wait()
        following.start()
    wait_all(onward)


def relay(low, high, after):
    return pl.pallas_call(
        relay_kernel,
        in_specs=[ANY] * 3,
        out_specs=(ANY, ANY),
        out_shape=[jax.ShapeDtypeStruct(x.shape, BF) for x in (low, high)],
        scratch_shapes=[pltpu.VMEM((2, *low.shape), BF), pltpu.SemaphoreType.DMA((2, 2))],
        cost_estimate=pl.CostEstimate(flops=0, bytes_accessed=4 << 20, transcendentals=0),
        compiler_params=pltpu.CompilerParams(vmem_limit_bytes=16 << 20),
        name="relay",
    )(low, high, after)


def finish_sums(parts, copies, *after):
    return pl.pallas_call(
        lambda parts, *rest: combine_kernel(parts, rest[-1]),
        in_specs=[WHOLE] + [ANY] * len(after),
        out_specs=WHOLE,
        out_shape=jax.ShapeDtypeStruct((copies, EACH, HEAD_DIM), BF),
        cost_estimate=pl.CostEstimate(
            flops=10**9, bytes_accessed=1 << 20, transcendentals=0
        ),
        compiler_params=pltpu.CompilerParams(vmem_limit_bytes=16 << 20),
        name="text_finish_sums",
    )(parts, *after)


def video_kernel(pos, mask, valid, *rest):
    far, out, near, bias_s, sems = rest[:8], rest[9], rest[10:18], rest[18], rest[19]
    q, tk, tv, own, z_low, z_high, t_low, t_high = near
    pairs = list(zip(far, near))
    begun = fetch(pairs, sems.at[0], FIRST)
    later = fetch(pairs, sems.at[1], REST)
    fill_bias(pos, mask, bias_s)
    text_bias = jnp.where(valid[...] > 0, 0.0, LOW)
    for head in range(HEADS_HERE):
        if head == 0:
            wait_all(begun)
        elif head == 1:
            wait_all(later)
        cols = slice(head * HEAD_DIM, (head + 1) * HEAD_DIM)
        one_head(
            q.at[:, cols],
            tk.at[:, cols],
            tv.at[:, cols],
            [ref.at[:, :, cols] for ref in (z_low, own, z_high)],
            [ref.at[:, :, :, cols] for ref in (t_low, t_high)],
            text_bias,
            bias_s,
            out.at[:, cols],
        )


def fill_bias(pos, mask, bias_s):
    row = lax.broadcasted_iota(jnp.int32, (8, PAIR), 0)
    col = lax.broadcasted_iota(jnp.int32, (8, PAIR), 1)
    second_q = row >= TILE
    second_k = jnp.bitwise_and(col, 7) >= TILE
    for a in range(2):
        for i in range(3):
            for j in range(3):
                where_t = pos[0] * 2 + a + i - 1
                where_h = pos[1] + j - 1
                inside = (where_t >= 0) & (where_t < pos[3]) & (where_h >= 0) & (where_h < pos[4])
                base = 9 * i + 3 * j

                def one(c, k):
                    if base + k == 13:
                        return jnp.where(inside, 0.0, LOW)
                    ok = inside & (mask[(a * 2 + c) * 27 + base + k] > 0)
                    return jnp.where(ok, 0.0, LOW)

                low = jnp.where(second_k, one(0, 2), one(0, 1))
                high = jnp.where(second_k, one(1, 1), one(1, 0))
                bias_s[a, i, j] = jnp.where(second_q, high, low)


def one_head(q, tk, tv, mids, sides, text_bias, bias_s, out):
    def rows(part):
        return (
            jnp.concatenate([sides[0][j, part] for j in range(3)], axis=0),
            jnp.concatenate(
                [ref[part, a * PAIR : (a + 1) * PAIR, :] for a in range(2) for ref in mids],
                axis=0,
            ),
            jnp.concatenate([sides[1][j, part] for j in range(3)], axis=0),
        )

    queries = q[...]
    k_low, k_mid, k_high = rows(0)
    v_low, v_mid, v_high = rows(1)
    s_mid = dot_t(queries, k_mid)
    s_text = dot_t(queries, tk[...])
    s_sides = (dot_t(queries[:PAIR], k_low), dot_t(queries[PAIR:], k_high))
    v_sides = (v_low, v_high)
    for a in range(2):
        mine = slice(a * PAIR, (a + 1) * PAIR)
        pieces = []
        for i in range(3):
            for j in range(3):
                at = (a + i - 1) * 3 + j
                if 0 <= a + i - 1 <= 1:
                    piece = s_mid[mine, at * PAIR : (at + 1) * PAIR]
                else:
                    piece = s_sides[a][:, j * PAIR : (j + 1) * PAIR]
                piece = piece.reshape(PAIR // 8, 8, PAIR) * SCALE2 + bias_s[a, i, j][None]
                pieces.append(piece.reshape(PAIR, PAIR))
        text_piece = s_text[mine] * SCALE2 + text_bias
        pieces.append(text_piece[:, :PAIR])
        pieces.append(text_piece[:, PAIR:])
        high = functools.reduce(jnp.maximum, pieces)
        high = jnp.max(high, axis=1, keepdims=True)
        weights = [jnp.exp2(piece - high) for piece in pieces]
        total = jnp.sum(functools.reduce(jnp.add, weights), axis=1, keepdims=True)
        weights = [w.astype(BF) for w in weights]
        side = weights[:3] if a == 0 else weights[6:9]
        mid = weights[3:9] if a == 0 else weights[:6]
        mixed = (
            dot(jnp.concatenate(side, axis=1), v_sides[a])
            + dot(jnp.concatenate(mid, axis=1), v_mid)
            + dot(jnp.concatenate(weights[9:], axis=1), tv[...])
        )
        out[mine, :] = (mixed / total).astype(BF)


def video_attention(pos, mask, valid, *arrays):
    return pl.pallas_call(
        video_kernel,
        in_specs=[SCALARS, SCALARS, WHOLE] + [FAR] * 4 + [ANY] * (len(arrays) - 4),
        out_specs=WHOLE,
        out_shape=jax.ShapeDtypeStruct((OWN, WIDTH), BF),
        scratch_shapes=[pltpu.VMEM(x.shape, BF) for x in arrays[:8]]
        + [pltpu.VMEM((2, 3, 3, 8, PAIR), F32), pltpu.SemaphoreType.DMA((2, 8))],
        cost_estimate=pl.CostEstimate(
            flops=9 * 10**9, bytes_accessed=6 << 20, transcendentals=2 * 10**6
        ),
        compiler_params=pltpu.CompilerParams(vmem_limit_bytes=VMEM),
        name="video_attention",
    )(pos, mask, valid, *arrays)


def project(pos, blocks, mine, held, sems, read, put, out, sent, out_sems):
    width = held.shape[1] // 4
    near, (top, bottom) = blocks[:7], blocks[7:]
    half = top.shape[0]
    for step, ref in list(zip((0, 1, 2, 3, 5, 6, 7), near)) + [(4, None)]:
        column = jnp.bitwise_and(pos[1] + step, 7)
        is_mine = lax.shift_right_logical(column, 2) == pos[2]
        slot = jnp.bitwise_and(column, 3)
        columns = pl.ds(pl.multiple_of(slot * width, width), width)

        @pl.when(is_mine if mine else jnp.logical_not(is_mine))
        def _():
            if ref is None:
                for part, piece in enumerate((top, bottom)):
                    target = held.at[part * half : (part + 1) * half, columns]
                    pltpu.make_async_copy(piece, target, sems.at[slot]).start()
            else:
                pltpu.make_async_copy(ref, held.at[:, columns], sems.at[slot]).start()

    left = read()
    copies = []
    for pair in range(2):
        for slot in (2 * pair, 2 * pair + 1):
            columns = slice(slot * width, (slot + 1) * width)
            pltpu.make_async_copy(near[0], held.at[:, columns], sems.at[slot]).wait()
        columns = slice(2 * pair * width, 2 * (pair + 1) * width)
        sent[:, columns] = put(columns, dot(left, held[:, columns])).astype(BF)
        copies.append(
            pltpu.make_async_copy(sent.at[:, columns], out.at[:, columns], out_sems.at[pair])
        )
        copies[-1].start()
    wait_all(copies)


def text_share_kernel(pos, parts_h, *rest):
    blocks, rest = rest[:9], rest[9:]
    rows, share, parts, in_sems, held, sent, sems, out_sems = rest
    copy = pltpu.make_async_copy(parts_h, parts, in_sems.at[0])
    copy.start()

    def read():
        copy.wait()
        flat = parts[...].reshape(HEADS_HERE * TEXT, HEAD_DIM)
        heads = [flat[head * TEXT : (head + 1) * TEXT] for head in range(HEADS_HERE)]
        rows[...] = jnp.concatenate(heads, axis=1)
        return rows[...]

    project(pos, blocks, False, held, sems, read, lambda _, x: x, share, sent, out_sems)


def share_kernel(pos, rows_h, *rest):
    blocks, rest = rest[:9], rest[9:]
    share, rows, in_sems, held, sent, sems, out_sems = rest
    copy = pltpu.make_async_copy(rows_h, rows, in_sems.at[0])
    copy.start()

    def read():
        copy.wait()
        return rows[...]

    project(pos, blocks, False, held, sems, read, lambda _, x: x, share, sent, out_sems)


def finish_kernel(pos, rows_h, other_h, *rest):
    blocks, rest = rest[:9], rest[9:]
    out, rows, other, in_sems, held, sent, sems, out_sems = rest
    copies = [
        pltpu.make_async_copy(rows_h, rows, in_sems.at[0]),
        pltpu.make_async_copy(other_h, other, in_sems.at[1]),
    ]
    for copy in copies:
        copy.start()

    def read():
        wait_all(copies)
        return rows[...]

    def put(columns, terms):
        return terms + other[:, columns].astype(F32)

    project(pos, blocks, True, held, sems, read, put, out, sent, out_sems)


def project_call(kernel, name, pos, left, blocks, out_shape, out_specs, scratch):
    depth, width = blocks[0].shape
    return pl.pallas_call(
        kernel,
        in_specs=[SCALARS] + [ANY] * len(left) + [FAR] * 7 + [ANY] * 2,
        out_specs=out_specs,
        out_shape=out_shape,
        scratch_shapes=[pltpu.VMEM(x.shape, BF) for x in left]
        + scratch
        + [
            pltpu.SemaphoreType.DMA((2,)),
            pltpu.VMEM((depth, 4 * width), BF),
            pltpu.VMEM((TEXT, 4 * width), BF),
            pltpu.SemaphoreType.DMA((4,)),
            pltpu.SemaphoreType.DMA((2,)),
        ],
        cost_estimate=pl.CostEstimate(
            flops=8 * TEXT * depth * width, bytes_accessed=4 << 20, transcendentals=0
        ),
        compiler_params=pltpu.CompilerParams(vmem_limit_bytes=24 << 20),
        name=name,
    )(pos, *left, *blocks)


def shards(video_q, video_kv, text_q, text_k, text_v, tile_mask, text_valid, w_out):
    frames, rows, cols, width = video_q.shape
    t_count, h_count = lax.axis_size("tm"), lax.axis_size("height")
    zero = jnp.int32(0)
    pos = jnp.stack(
        [
            lax.axis_index("tm"),
            lax.axis_index("height"),
            lax.axis_index("head"),
            zero + t_count * 2,
            zero + h_count,
        ]
    ).astype(jnp.int32)
    mask = tile_mask.reshape(-1)
    valid = text_valid.reshape(1, TEXT)
    own = video_kv.reshape(2, OWN, width)
    q = video_q.reshape(OWN, width)

    def up(x, axis):
        n = lax.axis_size(axis)
        return lax.ppermute(x, axis, [(i, (i + 1) % n) for i in range(n)])

    def down(x, axis):
        n = lax.axis_size(axis)
        return lax.ppermute(x, axis, [((i + 1) % n, i) for i in range(n)])

    z_low, z_high = up(own, "height"), down(own, "height")
    parts = text_part(pos, valid, text_q, own, text_k, text_v)
    parts = lax.all_to_all(parts, "tm", 0, 0, tiled=True)
    parts, ring = merge(parts, lax.axis_size("height"), w_out, z_low, z_high)
    low, high = corners(own, z_low, z_high, parts)
    t_low, t_high = up(low, "tm"), down(high, "tm")

    parts = lax.all_to_all(parts, "height", 0, 0, tiled=True)
    before, after = [], []
    for step in range(3):
        low, high = (before[-1], after[-1]) if step else (ring, ring)
        if step == 2:
            low, high = relay(low, high, parts)
        before.append(up(low, "height"))
        after.append(down(high, "height"))
    half = w_out.shape[0] // 2
    far = [up(before[2][:half], "height"), down(after[2][half:], "height")]

    sums = finish_sums(parts, lax.axis_size("tm"), t_low, t_high)
    parts = lax.all_to_all(sums, "tm", 0, 0, tiled=True)

    video_rows = video_attention(
        pos, mask, valid, q, text_k, text_v, own, z_low, z_high, t_low, t_high, sums
    )

    def swap(x):
        return lax.ppermute(x, "head", [(0, 1), (1, 0)])

    blocks = [w_out] + after + before[::-1] + far
    full = jax.ShapeDtypeStruct((OWN, 4 * w_out.shape[1]), BF)
    video_other = swap(
        project_call(share_kernel, "video_share", pos, [video_rows], blocks, full, FAR, [])
    )
    text_rows, text_other = project_call(
        text_share_kernel,
        "text_share",
        pos,
        [parts],
        blocks,
        (jax.ShapeDtypeStruct((TEXT, WIDTH), BF), full),
        (WHOLE, FAR),
        [],
    )
    text_other = swap(text_other)
    video_out = project_call(
        finish_kernel, "video_finish", pos, [video_rows, video_other], blocks, full, FAR, []
    )
    text_out = project_call(
        finish_kernel, "text_finish", pos, [text_rows, text_other], blocks, full, FAR, []
    )
    return video_out.reshape(frames, rows, cols, -1), text_out


def solution(mesh):
    return jax.shard_map(
        shards,
        mesh=mesh,
        in_specs=(
            P("tm", "height", None, "head"),
            P(None, "tm", "height", None, "head"),
            P(None, "head"),
            P(None, "head"),
            P(None, "head"),
            P("tm", "height", None, None),
            P(),
            P("head", "height"),
        ),
        out_specs=(P("tm", "height", None, "head"), P(None, "head")),
        check_vma=False,
    )
```

time: 167 us -> 115 us (0.69); the launches traced: 165 us -> 115 us
  waiting for transfers between devices: 38.6 us -> 4.25 us
  between operations: 14.3 us -> 1.01 us
  blocking collectives: 42.1 us -> 32.2 us
  Pallas kernels: 24.4 us -> 31.8 us
  starting transfers between devices: 33.5 us -> 35.5 us
  local copies, waits for them, and re-layouts: 11.7 us -> 9.78 us
    ppermute x12 -> x14, waiting for transfers between devices: 37.9 us -> 4.24 us  [the longest x6 3.86 us: down(): return lax.ppermute(x, axis, [((i + 1) % n, i) for i in range(n)])]
    all_to_all x1 -> x2, blocking collectives: 42.1 us -> 32.2 us  [the longest x1 16.3 us: shards(): parts = lax.all_to_all(parts, 'tm', 0, 0, tiled=True)]
    pallas_call x8 -> x10, Pallas kernels: 24.4 us -> 31.8 us  [the longest x4 13.9 us: project_call(): pl.pallas_call(kernel, in_specs=[SCALARS] + [ANY] * len(left) + [FAR] * 7...]
    unnamed x34 -> x36, local copies, waits for them, and re-layouts: 10.7 us -> 7.01 us
    ppermute x12 -> x14, starting transfers between devices: 27.3 us -> 31 us  [the longest x6 13.9 us: down(): return lax.ppermute(x, axis, [((i + 1) % n, i) for i in range(n)])]
  transfers between devices with their start and end apart: 14 -> 15, of which waited for: 6 -> 2; matrix products, arithmetic and copies ran while one was open for 1% -> 2% of each run, Pallas kernels for 12% -> 24%
where the time goes in v2:
time: 115 us
  starting transfers between devices  35.5 us (31%)
  blocking collectives  32.2 us (28%)
  Pallas kernels  31.8 us (28%)
  local copies, waits for them, and re-layouts  9.78 us (9%)
  waiting for transfers between devices  4.25 us (4%)
    all_to_all x1, blocking collectives, shards(): parts = lax.all_to_all(parts, 'tm', 0, 0, tiled=True)  16.3 us
    all_to_all x1, blocking collectives, shards(): parts = lax.all_to_all(parts, 'height', 0, 0, tiled=True)  15.9 us
    ppermute x6, starting transfers between devices, down(): return lax.ppermute(x, axis, [((i + 1) % n, i) for i in range(n)])  13.9 us
    pallas_call x4, Pallas kernels, project_call(): pl.pallas_call(kernel, in_specs=[SCALARS] + [ANY] * len(left) + [FAR] * 7...  13.9 us
    ppermute x2, starting transfers between devices, swap(): return lax.ppermute(x, 'head', [(0, 1), (1, 0)])  10.7 us
    pallas_call x1, Pallas kernels, video_attention(): pl.pallas_call(video_kernel, in_specs=[SCALARS, SCALARS, WHOLE] + [FAR] *...  8 us
    unnamed x36, local copies, waits for them, and re-layouts  7.01 us
    ppermute x6, starting transfers between devices, up(): return lax.ppermute(x, axis, [(i, (i + 1) % n) for i in range(n)])  6.37 us
  transfers between devices with their start and end apart: 15, of which 2 were waited for; matrix products, arithmetic and copies ran while one was open for 2% of the time, Pallas kernels for 24%

profile of v2, /device:TPU:1, one launch (start us, length us, event | category | flops | bytes accessed | tf_op | source)
XLA Modules:
  0.0 114.5 jit_solution(59626374462482345)
XLA Ops:
  0.6 2.5 %collective-permute-start = (bf16[2,256,768]{2,1,0:T(8,128)(2,1)}, bf16[2,256,768]{2,1,0:T(8,128)(2,1)S(1)}, u32[]{:S(2)}, u32[]{:S(2)}) collective-permute-start(bf16[2,256,768]{2,1,0:T(8,128)(2,1)} %bitcast.7), channel_id=1, source_target_pairs={{0,2},{2,4},{4,6},{6,8},{8,10},{10,12},{12,14},{14,0},{1,3},{3,5},... | collective-permute-start | bytes 2359304 | tf_op jit(solution)/shard_map/ppermute | solution.py:503
  3.2 4.0 %collective-permute-start.1 = (bf16[2,256,768]{2,1,0:T(8,128)(2,1)}, bf16[2,256,768]{2,1,0:T(8,128)(2,1)S(1)}, u32[]{:S(2)}, u32[]{:S(2)}) collective-permute-start(bf16[2,256,768]{2,1,0:T(8,128)(2,1)} %bitcast.8), channel_id=1, source_target_pairs={{2,0},{4,2},{6,4},{8,6},{10,8},{12,10},{14,12},{0,14},{3,1},{5,3},... | collective-permute-start | bytes 2359304 | tf_op jit(solution)/shard_map/ppermute | solution.py:507
  7.9 5.1 %text_part.1 = bf16[16,112,128]{2,1,0:T(8,128)(2,1)} custom-call(s32[5]{0:T(128)} %stack.15.pos, s32[1,256]{1,0:T(1,128)} %bitcast.14, bf16[256,768]{1,0:T(8,128)(2,1)} %tq_h.1, bf16[2,256,768]{2,1,0:T(8,128)(2,1)} %bitcast.9, bf16[256,768]{1,0:T(8,128)(2,1)} %rest_1_.1, bf16[256,768]{1,0:T(8,128)(2,1)} %rest_2_.1), custom_call_target="tpu_custom_call" | custom-call | flops 5000000000 | bytes 2097152 | tf_op jit(solution)/shard_map/text_part/pallas_call | solution.py:115
  12.9 16.3 %all_to_all.15.parts = bf16[16,112,128]{2,1,0:T(8,128)(2,1)S(1)} all-to-all(bf16[16,112,128]{2,1,0:T(8,128)(2,1)} %text_part.1), channel_id=1, replica_groups=mesh['tm'=16,'height'=8,'head'=2] {'tm'}, dimensions={0} | all-to-all | bytes 917504 | tf_op jit(solution)/shard_map/all_to_all | solution.py:511
  31.1 1.1 collective-permute-start.4
  32.6 2.6 %corners.1 = (bf16[3,2,128,768]{3,2,1,0:T(8,128)(2,1)}, bf16[3,2,128,768]{3,2,1,0:T(8,128)(2,1)}) custom-call(bf16[2,256,768]{2,1,0:T(8,128)(2,1)} %bitcast.10, bf16[2,256,768]{2,1,0:T(8,128)(2,1)} %copy-done.13, bf16[2,256,768]{2,1,0:T(8,128)(2,1)} %copy-done.14, bf16[8,112,128]{2,1,0:T(8,128)(2,1)} %copy-done.9), custom_call_target="tpu_custom_call" | custom-call | bytes 5242880 | tf_op jit(solution)/shard_map/corners/pallas_call | solution.py:148
  35.7 4.3 %collective-permute-start.3 = (bf16[3,2,128,768]{3,2,1,0:T(8,128)(2,1)}, bf16[3,2,128,768]{3,2,1,0:T(8,128)(2,1)}, u32[]{:S(2)}, u32[]{:S(2)}) collective-permute-start(bf16[3,2,128,768]{3,2,1,0:T(8,128)(2,1)} %get-tuple-element.12), channel_id=1, source_target_pairs={{16,0},{32,16},{48,32},{64,48},{80,64},{96,80},{112,96},{128,112},... | collective-permute-start | bytes 3538952 | tf_op jit(solution)/shard_map/ppermute | solution.py:507
  40.0 3.8 %collective-permute-done.4.rest_1_ = bf16[768,384]{1,0:T(8,128)(2,1)S(1)} collective-permute-done((bf16[768,384]{1,0:T(8,128)(2,1)S(1)}, bf16[768,384]{1,0:T(8,128)(2,1)S(1)}, u32[]{:S(2)}, u32[]{:S(2)}) %collective-permute-start.4) | collective-permute-done | bytes 589856 | tf_op jit(solution)/shard_map/ppermute | solution.py:507
  43.9 1.9 %collective-permute-start.5 = (bf16[768,384]{1,0:T(8,128)(2,1)S(1)}, bf16[768,384]{1,0:T(8,128)(2,1)S(1)}, u32[]{:S(2)}, u32[]{:S(2)}) collective-permute-start(bf16[768,384]{1,0:T(8,128)(2,1)S(1)} %collective-permute-done.4.rest_1_), channel_id=1, source_target_pairs={{2,0},{4,2},{6,4},{8,6},{10,8},{12,10},{14,12},{0,14},{3,1},{5,3},... | collective-permute-start | bytes 1769480 | tf_op jit(solution)/shard_map/ppermute | solution.py:507
  45.8 15.9 %all_to_all.16.parts.after = bf16[8,112,128]{2,1,0:T(8,128)(2,1)S(1)} all-to-all(bf16[8,112,128]{2,1,0:T(8,128)(2,1)S(1)} %copy-done.10), channel_id=1, replica_groups=mesh['tm'=16,'height'=8,'head'=2] {'height'}, dimensions={0} | all-to-all | bytes 458752 | tf_op jit(solution)/shard_map/all_to_all | solution.py:516
  61.7 1.3 %relay.1 = (bf16[768,384]{1,0:T(8,128)(2,1)}, bf16[768,384]{1,0:T(8,128)(2,1)}) custom-call(bf16[768,384]{1,0:T(8,128)(2,1)S(1)} %collective-permute-done.7.low.rest_5_, bf16[768,384]{1,0:T(8,128)(2,1)S(1)} %collective-permute-done.5.high.rest_2_, bf16[8,112,128]{2,1,0:T(8,128)(2,1)S(1)} %all_to_all.16.parts.after), custom_call_target="tpu_custom_call" | custom-call | bytes 4194304 | tf_op jit(solution)/shard_map/relay/pallas_call | solution.py:236
  63.0 1.3 %collective-permute-start.9 = (bf16[768,384]{1,0:T(8,128)(2,1)}, bf16[768,384]{1,0:T(8,128)(2,1)S(1)}, u32[]{:S(2)}, u32[]{:S(2)}) collective-permute-start(bf16[768,384]{1,0:T(8,128)(2,1)} %get-tuple-element.15), channel_id=1, source_target_pairs={{0,2},{2,4},{4,6},{6,8},{8,10},{10,12},{12,14},{14,0},{1,3},{3,5},... | collective-permute-start | bytes 1769480 | tf_op jit(solution)/shard_map/ppermute | solution.py:503
  64.4 1.4 %collective-permute-start.8 = (bf16[768,384]{1,0:T(8,128)(2,1)}, bf16[768,384]{1,0:T(8,128)(2,1)S(1)}, u32[]{:S(2)}, u32[]{:S(2)}) collective-permute-start(bf16[768,384]{1,0:T(8,128)(2,1)} %get-tuple-element.14), channel_id=1, source_target_pairs={{2,0},{4,2},{6,4},{8,6},{10,8},{12,10},{14,12},{0,14},{3,1},{5,3},... | collective-permute-start | bytes 1769480 | tf_op jit(solution)/shard_map/ppermute | solution.py:507
  68.4 4.5 %all-to-all-start.2 = ((bf16[16,96,128]{2,1,0:T(8,128)(2,1)}), bf16[16,96,128]{2,1,0:T(8,128)(2,1)}, u32[]{:S(2)}, u32[]{:S(2)}) async-start(bf16[16,96,128]{2,1,0:T(8,128)(2,1)} %copy-done.15), calls=%async_computation.2 | async-start | bytes 786432 | tf_op jit(solution)/shard_map/all_to_all | solution.py:528
  74.1 1.6 %collective-permute-start.10 = (bf16[384,384]{1,0:T(8,128)(2,1)}, bf16[384,384]{1,0:T(8,128)(2,1)S(1)}, u32[]{:S(2)}, u32[]{:S(2)}) collective-permute-start(bf16[384,384]{1,0:T(8,128)(2,1)} %slice.8), channel_id=1, source_target_pairs={{0,2},{2,4},{4,6},{6,8},{8,10},{10,12},{12,14},{14,0},{1,3},{3,5},... | collective-permute-start | bytes 884744 | tf_op jit(solution)/shard_map/ppermute | solution.py:503
  76.4 1.1 collective-permute-start.11
  77.5 8.0 %video_attention.1.rows_h = bf16[256,768]{1,0:T(8,128)(2,1)} custom-call(s32[5]{0:T(128)} %stack.15.pos, s32[108]{0:T(128)} %reshape.19.mask, s32[1,256]{1,0:T(1,128)} %bitcast.15, bf16[256,768]{1,0:T(8,128)(2,1)} %bitcast.13, bf16[256,768]{1,0:T(8,128)(2,1)} %rest_1_.1, bf16[256,768]{1,0:T(8,128)(2,1)} %rest_2_.1, bf16[2,256,768]{2,1,0:T(8,128)(2,1)} %bitcast.11, ...), custom_call_target="tpu_custom_call" | custom-call | flops 8999999488 | bytes 6291456 | tf_op jit(solution)/shard_map/video_attention/pallas_call | solution.py:361
  85.6 1.2 %copy-done.2 = bf16[768,384]{1,0:T(8,128)(2,1)S(1)} copy-done((bf16[768,384]{1,0:T(8,128)(2,1)S(1)}, bf16[768,384]{1,0:T(8,128)(2,1)}, u32[]{:S(2)}) %copy-start.2) | copy-done | bytes 589848
  87.7 3.0 %video_share.1 = bf16[256,1536]{1,0:T(8,128)(2,1)} custom-call(s32[5]{0:T(128)S(1)} %copy-done.16, bf16[256,768]{1,0:T(8,128)(2,1)S(1)} %copy-done.7, bf16[768,384]{1,0:T(8,128)(2,1)S(1)} %copy-done, bf16[768,384]{1,0:T(8,128)(2,1)S(1)} %collective-permute-done.4.rest_1_, bf16[768,384]{1,0:T(8,128)(2,1)S(1)} %collective-permute-done.5.high.rest_2_, ...), custom_call_target="tpu_custom_call" | custom-call | flops 603979776 | bytes 4194304 | tf_op jit(solution)/shard_map/video_share/pallas_call | solution.py:461
  90.7 10.4 %collective-permute-start.12 = (bf16[256,1536]{1,0:T(8,128)(2,1)}, bf16[256,1536]{1,0:T(8,128)(2,1)}, u32[]{:S(2)}, u32[]{:S(2)}) collective-permute-start(bf16[256,1536]{1,0:T(8,128)(2,1)} %video_share.1), channel_id=1, source_target_pairs={{0,1},{1,0},{2,3},{3,2},{4,5},{5,4},{6,7},{7,6},{8,9},{9,8},{10,11... | collective-permute-start | bytes 2359304 | tf_op jit(solution)/shard_map/ppermute | solution.py:535
  101.1 1.1 copy-done.3
  103.1 2.9 %text_share.1 = (bf16[256,768]{1,0:T(8,128)(2,1)S(1)}, bf16[256,1536]{1,0:T(8,128)(2,1)S(1)}) custom-call(s32[5]{0:T(128)S(1)} %copy-done.16, bf16[16,96,128]{2,1,0:T(8,128)(2,1)} %all-to-all-done.2.parts_h, bf16[768,384]{1,0:T(8,128)(2,1)S(1)} %copy-done, bf16[768,384]{1,0:T(8,128)(2,1)S(1)} %collective-permute-done.4.rest_1_, ...), custom_call_target="tpu_custom_call" | custom-call | flops 603979776 | bytes 4194304 | tf_op jit(solution)/shard_map/text_share/pallas_call | solution.py:461
  106.4 4.0 %video_finish.1 = bf16[256,1536]{1,0:T(8,128)(2,1)} custom-call(s32[5]{0:T(128)S(1)} %copy-done.16, bf16[256,768]{1,0:T(8,128)(2,1)S(1)} %copy-done.8, bf16[256,1536]{1,0:T(8,128)(2,1)} %collective-permute-done.12.other_h, bf16[768,384]{1,0:T(8,128)(2,1)S(1)} %copy-done, bf16[768,384]{1,0:T(8,128)(2,1)S(1)} %collective-permute-done.4.rest_1_, ...), custom_call_target="tpu_custom_call" | custom-call | flops 603979776 | bytes 4194304 | tf_op jit(solution)/shard_map/video_finish/pallas_call | solution.py:461
  110.4 4.0 %text_finish.1 = bf16[256,1536]{1,0:T(8,128)(2,1)} custom-call(s32[5]{0:T(128)S(1)} %copy-done.16, bf16[256,768]{1,0:T(8,128)(2,1)S(1)} %get-tuple-element.16.rows_h, bf16[256,1536]{1,0:T(8,128)(2,1)S(1)} %collective-permute-done.13.other_h, bf16[768,384]{1,0:T(8,128)(2,1)S(1)} %copy-done, bf16[768,384]{1,0:T(8,128)(2,1)S(1)} %collective-permute-done.4.rest_1_, ...), custom_call_target="tpu_custom_call" | custom-call | flops 603979776 | bytes 4194304 | tf_op jit(solution)/shard_map/text_finish/pallas_call | solution.py:461
  (58 shorter events, 10.2 us)
Async XLA Ops:
  0.6 28.7 %collective-permute-start = (bf16[2,256,768]{2,1,0:T(8,128)(2,1)}, bf16[2,256,768]{2,1,0:T(8,128)(2,1)S(1)}, u32[]{:S(2)}, u32[]{:S(2)}) collective-permute-start(bf16[2,256,768]{2,1,0:T(8,128)(2,1)} %bitcast.7), channel_id=1, source_target_pairs={{0,2},{2,4},{4,6},{6,8},{8,10},{10,12},{12,14},{14,0},{1,3},{3,5},... | collective-permute-start | bytes 2359304 | tf_op jit(solution)/shard_map/ppermute | solution.py:503
  3.2 26.1 %collective-permute-start.1 = (bf16[2,256,768]{2,1,0:T(8,128)(2,1)}, bf16[2,256,768]{2,1,0:T(8,128)(2,1)S(1)}, u32[]{:S(2)}, u32[]{:S(2)}) collective-permute-start(bf16[2,256,768]{2,1,0:T(8,128)(2,1)} %bitcast.8), channel_id=1, source_target_pairs={{2,0},{4,2},{6,4},{8,6},{10,8},{12,10},{14,12},{0,14},{3,1},{5,3},... | collective-permute-start | bytes 2359304 | tf_op jit(solution)/shard_map/ppermute | solution.py:507
  7.9 21.4 %copy-start = (bf16[768,384]{1,0:T(8,128)(2,1)S(1)}, bf16[768,384]{1,0:T(8,128)(2,1)}, u32[]{:S(2)}) copy-start(bf16[768,384]{1,0:T(8,128)(2,1)} %rest_0_.7) | copy-start | bytes 1769476
  31.1 12.8 %collective-permute-start.4 = (bf16[768,384]{1,0:T(8,128)(2,1)S(1)}, bf16[768,384]{1,0:T(8,128)(2,1)S(1)}, u32[]{:S(2)}, u32[]{:S(2)}) collective-permute-start(bf16[768,384]{1,0:T(8,128)(2,1)S(1)} %get-tuple-element.13), channel_id=1, source_target_pairs={{2,0},{4,2},{6,4},{8,6},{10,8},{12,10},{14,12},{0,14},{3,1},{5,3},... | collective-permute-start | bytes 1769480 | tf_op jit(solution)/shard_map/ppermute | solution.py:507
  32.2 13.6 %collective-permute-start.6 = (bf16[768,384]{1,0:T(8,128)(2,1)S(1)}, bf16[768,384]{1,0:T(8,128)(2,1)S(1)}, u32[]{:S(2)}, u32[]{:S(2)}) collective-permute-start(bf16[768,384]{1,0:T(8,128)(2,1)S(1)} %get-tuple-element.13), channel_id=1, source_target_pairs={{0,2},{2,4},{4,6},{6,8},{8,10},{10,12},{12,14},{14,0},{1,3},{3,5},... | collective-permute-start | bytes 1769480 | tf_op jit(solution)/shard_map/ppermute | solution.py:503
  32.6 13.2 %copy-start.10 = (bf16[8,112,128]{2,1,0:T(8,128)(2,1)S(1)}, bf16[8,112,128]{2,1,0:T(8,128)(2,1)}, u32[]{:S(2)}) copy-start(bf16[8,112,128]{2,1,0:T(8,128)(2,1)} %copy-done.9) | copy-start | bytes 688132
  35.2 30.6 %copy-start.17 = (s32[2,1,2,27]{3,2,1,0:T(2,128)S(1)}, s32[2,1,2,27]{3,2,1,0:T(2,128)}, u32[]{:S(2)}) copy-start(s32[2,1,2,27]{3,2,1,0:T(2,128)} %param.13) | copy-start | bytes 1300
  35.2 31.2 %collective-permute-start.2 = (bf16[3,2,128,768]{3,2,1,0:T(8,128)(2,1)}, bf16[3,2,128,768]{3,2,1,0:T(8,128)(2,1)}, u32[]{:S(2)}, u32[]{:S(2)}) collective-permute-start(bf16[3,2,128,768]{3,2,1,0:T(8,128)(2,1)} %get-tuple-element.11), channel_id=1, source_target_pairs={{0,16},{16,32},{32,48},{48,64},{64,80},{80,96},{96,112},{112,128},... | collective-permute-start | bytes 3538952 | tf_op jit(solution)/shard_map/ppermute | solution.py:503
  35.7 30.7 %collective-permute-start.3 = (bf16[3,2,128,768]{3,2,1,0:T(8,128)(2,1)}, bf16[3,2,128,768]{3,2,1,0:T(8,128)(2,1)}, u32[]{:S(2)}, u32[]{:S(2)}) collective-permute-start(bf16[3,2,128,768]{3,2,1,0:T(8,128)(2,1)} %get-tuple-element.12), channel_id=1, source_target_pairs={{16,0},{32,16},{48,32},{64,48},{80,64},{96,80},{112,96},{128,112},... | collective-permute-start | bytes 3538952 | tf_op jit(solution)/shard_map/ppermute | solution.py:507
  43.9 17.8 %collective-permute-start.5 = (bf16[768,384]{1,0:T(8,128)(2,1)S(1)}, bf16[768,384]{1,0:T(8,128)(2,1)S(1)}, u32[]{:S(2)}, u32[]{:S(2)}) collective-permute-start(bf16[768,384]{1,0:T(8,128)(2,1)S(1)} %collective-permute-done.4.rest_1_), channel_id=1, source_target_pairs={{2,0},{4,2},{6,4},{8,6},{10,8},{12,10},{14,12},{0,14},{3,1},{5,3},... | collective-permute-start | bytes 1769480 | tf_op jit(solution)/shard_map/ppermute | solution.py:507
  45.8 17.2 %copy-start.1 = (bf16[768,384]{1,0:T(8,128)(2,1)}, bf16[768,384]{1,0:T(8,128)(2,1)S(1)}, u32[]{:S(2)}) copy-start(bf16[768,384]{1,0:T(8,128)(2,1)S(1)} %collective-permute-done.6.rest_6_) | copy-start | bytes 1769476
  45.8 15.9 %collective-permute-start.7 = (bf16[768,384]{1,0:T(8,128)(2,1)S(1)}, bf16[768,384]{1,0:T(8,128)(2,1)S(1)}, u32[]{:S(2)}, u32[]{:S(2)}) collective-permute-start(bf16[768,384]{1,0:T(8,128)(2,1)S(1)} %collective-permute-done.6.rest_6_), channel_id=1, source_target_pairs={{0,2},{2,4},{4,6},{6,8},{8,10},{10,12},{12,14},{14,0},{1,3},{3,5},... | collective-permute-start | bytes 1769480 | tf_op jit(solution)/shard_map/ppermute | solution.py:503
  61.7 2.7 %copy-start.11 = (bf16[8,112,128]{2,1,0:T(8,128)(2,1)}, bf16[8,112,128]{2,1,0:T(8,128)(2,1)S(1)}, u32[]{:S(2)}) copy-start(bf16[8,112,128]{2,1,0:T(8,128)(2,1)S(1)} %all_to_all.16.parts.after) | copy-start | bytes 688132
  63.0 10.3 %collective-permute-start.9 = (bf16[768,384]{1,0:T(8,128)(2,1)}, bf16[768,384]{1,0:T(8,128)(2,1)S(1)}, u32[]{:S(2)}, u32[]{:S(2)}) collective-permute-start(bf16[768,384]{1,0:T(8,128)(2,1)} %get-tuple-element.15), channel_id=1, source_target_pairs={{0,2},{2,4},{4,6},{6,8},{8,10},{10,12},{12,14},{14,0},{1,3},{3,5},... | collective-permute-start | bytes 1769480 | tf_op jit(solution)/shard_map/ppermute | solution.py:503
  64.4 11.3 %collective-permute-start.8 = (bf16[768,384]{1,0:T(8,128)(2,1)}, bf16[768,384]{1,0:T(8,128)(2,1)S(1)}, u32[]{:S(2)}, u32[]{:S(2)}) collective-permute-start(bf16[768,384]{1,0:T(8,128)(2,1)} %get-tuple-element.14), channel_id=1, source_target_pairs={{2,0},{4,2},{6,4},{8,6},{10,8},{12,10},{14,12},{0,14},{3,1},{5,3},... | collective-permute-start | bytes 1769480 | tf_op jit(solution)/shard_map/ppermute | solution.py:507
  68.4 32.7 %all-to-all-start.2 = ((bf16[16,96,128]{2,1,0:T(8,128)(2,1)}), bf16[16,96,128]{2,1,0:T(8,128)(2,1)}, u32[]{:S(2)}, u32[]{:S(2)}) async-start(bf16[16,96,128]{2,1,0:T(8,128)(2,1)} %copy-done.15), calls=%async_computation.2 | async-start | bytes 786432 | tf_op jit(solution)/shard_map/all_to_all | solution.py:528
  74.1 11.4 %collective-permute-start.10 = (bf16[384,384]{1,0:T(8,128)(2,1)}, bf16[384,384]{1,0:T(8,128)(2,1)S(1)}, u32[]{:S(2)}, u32[]{:S(2)}) collective-permute-start(bf16[384,384]{1,0:T(8,128)(2,1)} %slice.8), channel_id=1, source_target_pairs={{0,2},{2,4},{4,6},{6,8},{8,10},{10,12},{12,14},{14,0},{1,3},{3,5},... | collective-permute-start | bytes 884744 | tf_op jit(solution)/shard_map/ppermute | solution.py:503
  76.4 9.1 %collective-permute-start.11 = (bf16[384,384]{1,0:T(8,128)(2,1)}, bf16[384,384]{1,0:T(8,128)(2,1)}, u32[]{:S(2)}, u32[]{:S(2)}) collective-permute-start(bf16[384,384]{1,0:T(8,128)(2,1)} %slice.9), channel_id=1, source_target_pairs={{2,0},{4,2},{6,4},{8,6},{10,8},{12,10},{14,12},{0,14},{3,1},{5,3},... | collective-permute-start | bytes 884744 | tf_op jit(solution)/shard_map/ppermute | solution.py:507
  77.5 8.0 %copy-start.16 = (s32[5]{0:T(128)S(1)}, s32[5]{0:T(128)}, u32[]{:S(2)}) copy-start(s32[5]{0:T(128)} %stack.15.pos) | copy-start | bytes 64
  85.5 5.2 %copy-start.4 = (bf16[384,384]{1,0:T(8,128)(2,1)}, bf16[384,384]{1,0:T(8,128)(2,1)S(1)}, u32[]{:S(2)}) copy-start(bf16[384,384]{1,0:T(8,128)(2,1)S(1)} %collective-permute-done.10.rest_7_) | copy-start | bytes 884740
  90.7 15.6 %collective-permute-start.12 = (bf16[256,1536]{1,0:T(8,128)(2,1)}, bf16[256,1536]{1,0:T(8,128)(2,1)}, u32[]{:S(2)}, u32[]{:S(2)}) collective-permute-start(bf16[256,1536]{1,0:T(8,128)(2,1)} %video_share.1), channel_id=1, source_target_pairs={{0,1},{1,0},{2,3},{3,2},{4,5},{5,4},{6,7},{7,6},{8,9},{9,8},{10,11... | collective-permute-start | bytes 2359304 | tf_op jit(solution)/shard_map/ppermute | solution.py:535
  103.1 3.2 %copy-start.6 = (bf16[384,384]{1,0:T(8,128)(2,1)S(1)}, bf16[384,384]{1,0:T(8,128)(2,1)}, u32[]{:S(2)}) copy-start(bf16[384,384]{1,0:T(8,128)(2,1)} %copy-done.4) | copy-start | bytes 884740
  103.1 3.2 %copy-start.8 = (bf16[256,768]{1,0:T(8,128)(2,1)S(1)}, bf16[256,768]{1,0:T(8,128)(2,1)}, u32[]{:S(2)}) copy-start(bf16[256,768]{1,0:T(8,128)(2,1)} %video_attention.1.rows_h) | copy-start | bytes 1179652
  106.0 4.3 %collective-permute-start.13 = (bf16[256,1536]{1,0:T(8,128)(2,1)S(1)}, bf16[256,1536]{1,0:T(8,128)(2,1)S(1)}, u32[]{:S(2)}, u32[]{:S(2)}) collective-permute-start(bf16[256,1536]{1,0:T(8,128)(2,1)S(1)} %get-tuple-element.17), channel_id=1, source_target_pairs={{0,1},{1,0},{2,3},{3,2},{4,5},{5,4},{6,7},{7,6},{8,9},{9,8},{10,11... | collective-permute-start | bytes 2359304 | tf_op jit(solution)/shard_map/ppermute | solution.py:535
  (9 other events, 8.6 us)

commit v3 on v2

--- a/solution.py
+++ b/solution.py
@@ -71,11 +71,14 @@
 
 
 def text_part_kernel(
-    pos, valid, tq_h, kv_h, tk_h, tv_h, out, tq, kv, tk, tv, acc_s, high_s, total_s, sems
+    pos, valid, tq_h, kv_h, tk_h, tv_h, w_h, out, w_out, tq, kv, tk, tv, w, acc_s, high_s, total_s, sems, w_sems
 ):
+    inward = pltpu.make_async_copy(w_h, w, w_sems.at[0])
+    onward = pltpu.make_async_copy(w, w_out, w_sems.at[1])
     pairs = [(tq_h, tq), (kv_h, kv), (tk_h, tk), (tv_h, tv)]
     begun = fetch(pairs, sems.at[0], FIRST)
     later = fetch(pairs, sems.at[1], REST)
+    inward.start()
     first = (pos[0] == 0) & (pos[1] == 0)
     bias = jnp.where((valid[...] > 0) & first, 0.0, LOW)
     for head in range(HEADS_HERE):
@@ -83,6 +86,8 @@
             wait_all(begun)
         elif head == 1:
             wait_all(later)
+            inward.wait()
+            onward.start()
         cols = slice(head * HEAD_DIM, (head + 1) * HEAD_DIM)
         q = tq[:, cols]
         s_own = dot_t(q, kv[0, :, cols]) * SCALE2
@@ -102,6 +107,7 @@
         rows = slice(rank * EACH, (rank + 1) * EACH)
         out[rank, :EACH] = acc_s[rows, :]
         out[rank, EACH:] = stat_rows((high_s[rows, :], *split(total_s[rows, :])))
+    onward.wait()
 
 
 WHOLE = pl.BlockSpec(memory_space=pltpu.VMEM)
@@ -110,67 +116,71 @@
 ANY = pl.BlockSpec(memory_space=pl.ANY)
 
 
-def text_part(pos, valid, tq, kv, tk, tv):
+def text_part(pos, valid, tq, kv, tk, tv, w):
     count = HEADS_HERE * TEXT
     return pl.pallas_call(
         text_part_kernel,
-        in_specs=[SCALARS, WHOLE, FAR, FAR, FAR, FAR],
-        out_specs=WHOLE,
-        out_shape=jax.ShapeDtypeStruct((PLANE, SLOT, HEAD_DIM), BF),
-        scratch_shapes=[pltpu.VMEM(x.shape, BF) for x in (tq, kv, tk, tv)]
+        in_specs=[SCALARS, WHOLE, FAR, FAR, FAR, FAR, FAR],
+        out_specs=(WHOLE, FAR),
+        out_shape=(
+            jax.ShapeDtypeStruct((PLANE, SLOT, HEAD_DIM), BF),
+            jax.ShapeDtypeStruct(w.shape, BF),
+        ),
+        scratch_shapes=[pltpu.VMEM(x.shape, BF) for x in (tq, kv, tk, tv, w)]
         + [pltpu.VMEM((count, HEAD_DIM), t) for t in (BF, F32, F32)]
-        + [pltpu.SemaphoreType.DMA((2, 4))],
+        + [pltpu.SemaphoreType.DMA((2, 4)), pltpu.SemaphoreType.DMA((2,))],
         cost_estimate=pl.CostEstimate(
             flops=5 * 10**9, bytes_accessed=2 << 20, transcendentals=10**6
         ),
         compiler_params=pltpu.CompilerParams(vmem_limit_bytes=VMEM),
         name="text_part",
-    )(pos, valid, tq, kv, tk, tv)
-
-
-def corners_kernel(own, z_low, z_high, after, low, high, held, sems):
+    )(pos, valid, tq, kv, tk, tv, w)
+
+
+def merge_kernel(parts, own, z_low, z_high, out, low, high, held, sems):
     inward, outward = [], []
     for j, ref in enumerate((z_low, own, z_high)):
-        for side, out in enumerate((low, high)):
+        for side, target in enumerate((low, high)):
             part = ref.at[:, pl.ds((1 - side) * PAIR, PAIR), :]
             inward.append(pltpu.make_async_copy(part, held.at[j, side], sems.at[0, j, side]))
-            outward.append(pltpu.make_async_copy(held.at[j, side], out.at[j], sems.at[1, j, side]))
+            outward.append(
+                pltpu.make_async_copy(held.at[j, side], target.at[j], sems.at[1, j, side])
+            )
     for copy in inward:
         copy.start()
-    for copy, onward in zip(inward, outward):
-        copy.wait()
-        onward.start()
+
+    def between():
+        for copy, onward in zip(inward, outward):
+            copy.wait()
+            onward.start()
+
+    combine_kernel(1, parts, out, between=between)
     wait_all(outward)
 
 
-def corners(own, z_low, z_high, after):
+def merge(parts, copies, own, z_low, z_high):
     shape = jax.ShapeDtypeStruct((3, 2, PAIR, WIDTH), BF)
     return pl.pallas_call(
-        corners_kernel,
-        in_specs=[ANY] * 4,
-        out_specs=(ANY, ANY),
-        out_shape=(shape, shape),
+        merge_kernel,
+        in_specs=[WHOLE] + [ANY] * 3,
+        out_specs=(WHOLE, ANY, ANY),
+        out_shape=(jax.ShapeDtypeStruct((copies, SLOT, HEAD_DIM), BF), shape, shape),
         scratch_shapes=[
             pltpu.VMEM((3, 2, 2, PAIR, WIDTH), BF),
             pltpu.SemaphoreType.DMA((2, 3, 2)),
         ],
-        cost_estimate=pl.CostEstimate(flops=0, bytes_accessed=5 << 20, transcendentals=0),
-        compiler_params=pltpu.CompilerParams(vmem_limit_bytes=VMEM),
-        name="corners",
-    )(own, z_low, z_high, after)
-
-
-def merge_kernel(parts, w_h, z_low, z_high, out, w_out, w, sems):
-    inward = pltpu.make_async_copy(w_h, w, sems.at[0])
-    onward = pltpu.make_async_copy(w, w_out, sems.at[1])
-    inward.start()
-    combine_kernel(parts, out, between=lambda: (inward.wait(), onward.start()))
-    onward.wait()
-
-
-def combine_kernel(parts, out, between=lambda: None):
-    sources, copies = parts.shape[0], out.shape[0]
-    stats = [parts[i, EACH:].astype(F32) for i in range(sources)]
+        cost_estimate=pl.CostEstimate(
+            flops=2 * 10**9, bytes_accessed=6 << 20, transcendentals=0
+        ),
+        compiler_params=pltpu.CompilerParams(vmem_limit_bytes=24 << 20),
+        name="text_merge",
+    )(parts, own, z_low, z_high)
+
+
+def combine_kernel(count, *refs, between=lambda: None):
+    ins, out = refs[:count], refs[-1]
+    parts = [ref.at[i] for ref in ins for i in range(ref.shape[0])]
+    stats = [part[EACH:].astype(F32) for part in parts]
     highs = [s[0:1] for s in stats]
     high = functools.reduce(jnp.maximum, highs)
     weights = [jnp.exp2(h - high) for h in highs]
@@ -187,36 +197,33 @@
     table = table.T
     between()
     sums = jnp.zeros((EACH, HEAD_DIM), F32)
-    for i in range(sources):
-        sums += table[:EACH, i : i + 1] * parts[i, :EACH].astype(F32)
+    for i, part in enumerate(parts):
+        sums += table[:EACH, i : i + 1] * part[:EACH].astype(F32)
     sums = sums.astype(BF)
-    for at in range(copies):
+    for at in range(out.shape[0]):
         out[at, :EACH] = sums
     if not finish:
         lines = lay_out((high, *split(total)))
-        for at in range(copies):
+        for at in range(out.shape[0]):
             out[at, EACH:] = lines
 
 
-def merge(parts, copies, w, *after):
+def combine(parts, copies, finish, name, *after):
     return pl.pallas_call(
-        merge_kernel,
-        in_specs=[WHOLE, FAR] + [ANY] * len(after),
-        out_specs=(WHOLE, FAR),
-        out_shape=(
-            jax.ShapeDtypeStruct((copies, SLOT, HEAD_DIM), BF),
-            jax.ShapeDtypeStruct(w.shape, BF),
-        ),
-        scratch_shapes=[pltpu.VMEM(w.shape, BF), pltpu.SemaphoreType.DMA((2,))],
+        functools.partial(combine_kernel, len(parts)),
+        in_specs=[WHOLE] * len(parts) + [ANY] * len(after),
+        out_specs=WHOLE,
+        out_shape=jax.ShapeDtypeStruct((copies, EACH if finish else SLOT, HEAD_DIM), BF),
         cost_estimate=pl.CostEstimate(
-            flops=10**9, bytes_accessed=2 << 20, transcendentals=0
+            flops=10**9, bytes_accessed=1 << 20, transcendentals=0
         ),
         compiler_params=pltpu.CompilerParams(vmem_limit_bytes=16 << 20),
-        name="text_merge",
-    )(parts, w, *after)
-
-
-def relay_kernel(low, high, after, low_out, high_out, held, sems):
+        name=name,
+    )(*parts, *after)
+
+
+def relay_kernel(low, high, *rest):
+    low_out, high_out, held, sems = rest[-4:]
     pairs = ((low, low_out), (high, high_out))
     inward = [
         pltpu.make_async_copy(ref, held.at[i], sems.at[0, i]) for i, (ref, _) in enumerate(pairs)
@@ -232,35 +239,53 @@
     wait_all(onward)
 
 
-def relay(low, high, after):
+def halves_kernel(low, high, after, low_out, high_out, held, sems):
+    half = low_out.shape[0]
+    inward = [
+        pltpu.make_async_copy(ref, held.at[i], sems.at[0, i])
+        for i, ref in enumerate((low.at[0:half], high.at[half : 2 * half]))
+    ]
+    onward = [
+        pltpu.make_async_copy(held.at[i], out, sems.at[1, i])
+        for i, out in enumerate((low_out, high_out))
+    ]
+    for copy in inward:
+        copy.start()
+    for copy, following in zip(inward, onward):
+        copy.wait()
+        following.start()
+    wait_all(onward)
+
+
+def halves(low, high, after):
+    shape = (low.shape[0] // 2, low.shape[1])
+    return pl.pallas_call(
+        halves_kernel,
+        in_specs=[ANY] * 3,
+        out_specs=(ANY, ANY),
+        out_shape=[jax.ShapeDtypeStruct(shape, BF)] * 2,
+        scratch_shapes=[pltpu.VMEM((2, *shape), BF), pltpu.SemaphoreType.DMA((2, 2))],
+        cost_estimate=pl.CostEstimate(flops=0, bytes_accessed=2 << 20, transcendentals=0),
+        compiler_params=pltpu.CompilerParams(vmem_limit_bytes=16 << 20),
+        name="halves",
+    )(low, high, after)
+
+
+def relay(low, high, *after):
     return pl.pallas_call(
         relay_kernel,
-        in_specs=[ANY] * 3,
+        in_specs=[ANY] * (2 + len(after)),
         out_specs=(ANY, ANY),
         out_shape=[jax.ShapeDtypeStruct(x.shape, BF) for x in (low, high)],
         scratch_shapes=[pltpu.VMEM((2, *low.shape), BF), pltpu.SemaphoreType.DMA((2, 2))],
         cost_estimate=pl.CostEstimate(flops=0, bytes_accessed=4 << 20, transcendentals=0),
         compiler_params=pltpu.CompilerParams(vmem_limit_bytes=16 << 20),
         name="relay",
-    )(low, high, after)
-
-
-def finish_sums(parts, copies, *after):
-    return pl.pallas_call(
-        lambda parts, *rest: combine_kernel(parts, rest[-1]),
-        in_specs=[WHOLE] + [ANY] * len(after),
-        out_specs=WHOLE,
-        out_shape=jax.ShapeDtypeStruct((copies, EACH, HEAD_DIM), BF),
-        cost_estimate=pl.CostEstimate(
-            flops=10**9, bytes_accessed=1 << 20, transcendentals=0
-        ),
-        compiler_params=pltpu.CompilerParams(vmem_limit_bytes=16 << 20),
-        name="text_finish_sums",
-    )(parts, *after)
+    )(low, high, *after)
 
 
 def video_kernel(pos, mask, valid, *rest):
-    far, out, near, bias_s, sems = rest[:8], rest[9], rest[10:18], rest[18], rest[19]
+    far, out_h, near, out, bias_s, sems = rest[:8], rest[8], rest[9:17], *rest[17:]
     q, tk, tv, own, z_low, z_high, t_low, t_high = near
     pairs = list(zip(far, near))
     begun = fetch(pairs, sems.at[0], FIRST)
@@ -283,6 +308,9 @@
             bias_s,
             out.at[:, cols],
         )
+    copy = pltpu.make_async_copy(out, out_h, sems.at[0, 0])
+    copy.start()
+    copy.wait()
 
 
 def fill_bias(pos, mask, bias_s):
@@ -361,10 +389,10 @@
     return pl.pallas_call(
         video_kernel,
         in_specs=[SCALARS, SCALARS, WHOLE] + [FAR] * 4 + [ANY] * (len(arrays) - 4),
-        out_specs=WHOLE,
+        out_specs=FAR,
         out_shape=jax.ShapeDtypeStruct((OWN, WIDTH), BF),
         scratch_shapes=[pltpu.VMEM(x.shape, BF) for x in arrays[:8]]
-        + [pltpu.VMEM((2, 3, 3, 8, PAIR), F32), pltpu.SemaphoreType.DMA((2, 8))],
+        + [pltpu.VMEM((OWN, WIDTH), BF), pltpu.VMEM((2, 3, 3, 8, PAIR), F32), pltpu.SemaphoreType.DMA((2, 8))],
         cost_estimate=pl.CostEstimate(
             flops=9 * 10**9, bytes_accessed=6 << 20, transcendentals=2 * 10**6
         ),
@@ -409,7 +437,8 @@
 
 def text_share_kernel(pos, parts_h, *rest):
     blocks, rest = rest[:9], rest[9:]
-    rows, share, parts, in_sems, held, sent, sems, out_sems = rest
+    rows_h, share, parts, rows, in_sems, held, sent, sems, out_sems = rest
+    rows_copy = pltpu.make_async_copy(rows, rows_h, in_sems.at[1])
     copy = pltpu.make_async_copy(parts_h, parts, in_sems.at[0])
     copy.start()
 
@@ -418,9 +447,11 @@
         flat = parts[...].reshape(HEADS_HERE * TEXT, HEAD_DIM)
         heads = [flat[head * TEXT : (head + 1) * TEXT] for head in range(HEADS_HERE)]
         rows[...] = jnp.concatenate(heads, axis=1)
+        rows_copy.start()
         return rows[...]
 
     project(pos, blocks, False, held, sems, read, lambda _, x: x, share, sent, out_sems)
+    rows_copy.wait()
 
 
 def share_kernel(pos, rows_h, *rest):
@@ -460,7 +491,7 @@
     depth, width = blocks[0].shape
     return pl.pallas_call(
         kernel,
-        in_specs=[SCALARS] + [ANY] * len(left) + [FAR] * 7 + [ANY] * 2,
+        in_specs=[SCALARS] + [FAR] + [ANY] * (len(left) - 1) + [FAR] * 7 + [ANY] * 2,
         out_specs=out_specs,
         out_shape=out_shape,
         scratch_shapes=[pltpu.VMEM(x.shape, BF) for x in left]
@@ -498,38 +529,34 @@
     own = video_kv.reshape(2, OWN, width)
     q = video_q.reshape(OWN, width)
 
-    def up(x, axis):
+    def up(x, axis, by=1):
         n = lax.axis_size(axis)
-        return lax.ppermute(x, axis, [(i, (i + 1) % n) for i in range(n)])
-
-    def down(x, axis):
-        n = lax.axis_size(axis)
-        return lax.ppermute(x, axis, [((i + 1) % n, i) for i in range(n)])
+        return lax.ppermute(x, axis, [(i, (i + by) % n) for i in range(n)])
+
+    def down(x, axis, by=1):
+        return up(x, axis, -by)
 
     z_low, z_high = up(own, "height"), down(own, "height")
-    parts = text_part(pos, valid, text_q, own, text_k, text_v)
+    parts, ring = text_part(pos, valid, text_q, own, text_k, text_v, w_out)
+    before, after = [up(ring, "height")], [down(ring, "height")]
     parts = lax.all_to_all(parts, "tm", 0, 0, tiled=True)
-    parts, ring = merge(parts, lax.axis_size("height"), w_out, z_low, z_high)
-    low, high = corners(own, z_low, z_high, parts)
+    parts, low, high = merge(parts, h_count, own, z_low, z_high)
     t_low, t_high = up(low, "tm"), down(high, "tm")
 
     parts = lax.all_to_all(parts, "height", 0, 0, tiled=True)
-    before, after = [], []
-    for step in range(3):
-        low, high = (before[-1], after[-1]) if step else (ring, ring)
-        if step == 2:
-            low, high = relay(low, high, parts)
-        before.append(up(low, "height"))
-        after.append(down(high, "height"))
-    half = w_out.shape[0] // 2
-    far = [up(before[2][:half], "height"), down(after[2][half:], "height")]
-
-    sums = finish_sums(parts, lax.axis_size("tm"), t_low, t_high)
+    low, high = before[0], after[0]
+    before.append(up(low, "height"))
+    after.append(down(high, "height"))
+    sums = combine([parts], t_count, True, "text_finish_sums")
     parts = lax.all_to_all(sums, "tm", 0, 0, tiled=True)
-
+    low, high = relay(before[1], after[1], parts, t_low, t_high)
+    before.append(up(low, "height"))
+    after.append(down(high, "height"))
     video_rows = video_attention(
-        pos, mask, valid, q, text_k, text_v, own, z_low, z_high, t_low, t_high, sums
+        pos, mask, valid, q, text_k, text_v, own, z_low, z_high, t_low, t_high
     )
+    low, high = halves(before[2], after[2], video_rows)
+    far = [up(low, "height"), down(high, "height")]
 
     def swap(x):
         return lax.ppermute(x, "head", [(0, 1), (1, 0)])
@@ -546,8 +573,8 @@
         [parts],
         blocks,
         (jax.ShapeDtypeStruct((TEXT, WIDTH), BF), full),
-        (WHOLE, FAR),
-        [],
+        (FAR, FAR),
+        [pltpu.VMEM((TEXT, WIDTH), BF)],
     )
     text_other = swap(text_other)
     video_out = project_call(

time: 115 us -> 107 us (0.930)
  blocking collectives: 32.2 us -> 0 us
  waiting for transfers between devices: 4.25 us -> 28.5 us
  starting transfers between devices: 35.5 us -> 44.2 us
  local copies, waits for them, and re-layouts: 9.78 us -> 2.3 us
  Pallas kernels: 31.8 us -> 30.3 us
    all_to_all x2 -> x0, blocking collectives: 32.2 us -> none  [the longest x1 16.3 us: shards(): parts = lax.all_to_all(parts, 'tm', 0, 0, tiled=True)]
    all_to_all x0 -> x2, waiting for transfers between devices: none -> 14.4 us  [the longest x1 8.04 us: shards(): parts = lax.all_to_all(parts, 'tm', 0, 0, tiled=True)]
    all_to_all x0 -> x2, starting transfers between devices: none -> 11.7 us  [the longest x1 6.77 us: shards(): parts = lax.all_to_all(parts, 'tm', 0, 0, tiled=True)]
    ppermute x12, waiting for transfers between devices: 4.24 us -> 11.4 us  [up(): return lax.ppermute(x, axis, [(i, (i + by) % n) for i in range(n)])]
    unnamed x36 -> x12, local copies, waits for them, and re-layouts: 7.01 us -> 1.02 us
    ppermute x2, starting transfers between devices: 10.7 us -> 5.88 us  [swap(): return lax.ppermute(x, 'head', [(0, 1), (1, 0)])]
    all_to_all x1, waiting for transfers between devices: 0.01 us -> 2.78 us  [shards(): parts = lax.all_to_all(sums, 'tm', 0, 0, tiled=True)]
    ppermute x12, starting transfers between devices: 20.3 us -> 23 us  [up(): return lax.ppermute(x, axis, [(i, (i + by) % n) for i in range(n)])]
  transfers between devices with their start and end apart: 15 -> 17, of which waited for: 2 -> 7; matrix products, arithmetic and copies ran while one was open for 2% -> 1% of each run, Pallas kernels for 24% -> 22%
where the time goes in v3:
time: 107 us; the launch traced here: 106 us
  starting transfers between devices  44.2 us (41%)
  Pallas kernels  30.3 us (28%)
  waiting for transfers between devices  28.5 us (27%)
  local copies, waits for them, and re-layouts  2.3 us (2%)
    ppermute x12, starting transfers between devices, up(): return lax.ppermute(x, axis, [(i, (i + by) % n) for i in range(n)])  23 us
    ppermute x12, waiting for transfers between devices, up(): return lax.ppermute(x, axis, [(i, (i + by) % n) for i in range(n)])  11.4 us
    pallas_call x4, Pallas kernels, project_call(): pl.pallas_call(kernel, in_specs=[SCALARS] + [FAR] + [ANY] * (len(left) -...  11.1 us
    pallas_call x1, Pallas kernels, video_attention(): pl.pallas_call(video_kernel, in_specs=[SCALARS, SCALARS, WHOLE] + [FAR] *...  8.05 us
    all_to_all x1, waiting for transfers between devices, shards(): parts = lax.all_to_all(parts, 'tm', 0, 0, tiled=True)  8.04 us
    all_to_all x1, starting transfers between devices, shards(): parts = lax.all_to_all(parts, 'tm', 0, 0, tiled=True)  6.77 us
    all_to_all x1, waiting for transfers between devices, shards(): parts = lax.all_to_all(parts, 'height', 0, 0, tiled=True)  6.32 us
    ppermute x2, starting transfers between devices, swap(): return lax.ppermute(x, 'head', [(0, 1), (1, 0)])  5.88 us
  transfers between devices with their start and end apart: 17, of which 7 were waited for; matrix products, arithmetic and copies ran while one was open for 1% of the time, Pallas kernels for 22%

profile of v3, /device:TPU:1, one launch (start us, length us, event | category | flops | bytes accessed | tf_op | source)
XLA Modules:
  0.0 106.3 jit_solution(8166996683478689650)
XLA Ops:
  0.6 2.5 %collective-permute-start = (bf16[2,256,768]{2,1,0:T(8,128)(2,1)}, bf16[2,256,768]{2,1,0:T(8,128)(2,1)}, u32[]{:S(2)}, u32[]{:S(2)}) collective-permute-start(bf16[2,256,768]{2,1,0:T(8,128)(2,1)} %bitcast.7), channel_id=1, source_target_pairs={{0,2},{2,4},{4,6},{6,8},{8,10},{10,12},{12,14},{14,0},{1,3},{3,5},... | collective-permute-start | bytes 2359304 | tf_op jit(solution)/shard_map/ppermute | solution.py:534
  3.2 4.0 %collective-permute-start.1 = (bf16[2,256,768]{2,1,0:T(8,128)(2,1)}, bf16[2,256,768]{2,1,0:T(8,128)(2,1)}, u32[]{:S(2)}, u32[]{:S(2)}) collective-permute-start(bf16[2,256,768]{2,1,0:T(8,128)(2,1)} %bitcast.8), channel_id=1, source_target_pairs={{0,14},{2,0},{4,2},{6,4},{8,6},{10,8},{12,10},{14,12},{1,15},{3,1}... | collective-permute-start | bytes 2359304 | tf_op jit(solution)/shard_map/ppermute | solution.py:534
  7.8 5.3 %text_part.1 = (bf16[16,112,128]{2,1,0:T(8,128)(2,1)}, bf16[768,384]{1,0:T(8,128)(2,1)}) custom-call(s32[5]{0:T(128)} %stack.15.pos, s32[1,256]{1,0:T(1,128)} %bitcast.14, bf16[256,768]{1,0:T(8,128)(2,1)} %tq_h.1, bf16[2,256,768]{2,1,0:T(8,128)(2,1)} %bitcast.9, bf16[256,768]{1,0:T(8,128)(2,1)} %rest_1_.1, bf16[256,768]{1,0:T(8,128)(2,1)} %rest_2_.1, ...), custom_call_target="tpu_custom_call" | custom-call | flops 5000000000 | bytes 2097152 | tf_op jit(solution)/shard_map/text_part/pallas_call | solution.py:121
  13.1 6.8 %all-to-all-start = ((bf16[16,112,128]{2,1,0:T(8,128)(2,1)}), bf16[16,112,128]{2,1,0:T(8,128)(2,1)S(1)}, u32[]{:S(2)}, u32[]{:S(2)}) async-start(bf16[16,112,128]{2,1,0:T(8,128)(2,1)} %get-tuple-element.13), calls=%async_computation | async-start | bytes 917504 | tf_op jit(solution)/shard_map/all_to_all | solution.py:542
  19.9 1.4 %collective-permute-start.4 = (bf16[768,384]{1,0:T(8,128)(2,1)}, bf16[768,384]{1,0:T(8,128)(2,1)S(1)}, u32[]{:S(2)}, u32[]{:S(2)}) collective-permute-start(bf16[768,384]{1,0:T(8,128)(2,1)} %get-tuple-element.16), channel_id=1, source_target_pairs={{0,14},{2,0},{4,2},{6,4},{8,6},{10,8},{12,10},{14,12},{1,15},{3,1}... | collective-permute-start | bytes 1769480 | tf_op jit(solution)/shard_map/ppermute | solution.py:534
  21.4 8.0 %all-to-all-done.parts = bf16[16,112,128]{2,1,0:T(8,128)(2,1)S(1)} async-done(((bf16[16,112,128]{2,1,0:T(8,128)(2,1)}), bf16[16,112,128]{2,1,0:T(8,128)(2,1)S(1)}, u32[]{:S(2)}, u32[]{:S(2)}) %all-to-all-start) | async-done | bytes 458784 | tf_op jit(solution)/shard_map/all_to_all | solution.py:542
  29.5 3.2 %text_merge.1 = (bf16[8,112,128]{2,1,0:T(8,128)(2,1)}, bf16[3,2,128,768]{3,2,1,0:T(8,128)(2,1)}, bf16[3,2,128,768]{3,2,1,0:T(8,128)(2,1)}) custom-call(bf16[16,112,128]{2,1,0:T(8,128)(2,1)S(1)} %all-to-all-done.parts, bf16[2,256,768]{2,1,0:T(8,128)(2,1)S(1)} %bitcast.11, bf16[2,256,768]{2,1,0:T(8,128)(2,1)} %collective-permute-done.z_low.rest_4_, ...), custom_call_target="tpu_custom_call" | custom-call | flops 2000000000 | bytes 6291456 | tf_op jit(solution)/shard_map/text_merge/pallas_call | solution.py:163
  33.2 4.3 %collective-permute-start.3 = (bf16[3,2,128,768]{3,2,1,0:T(8,128)(2,1)}, bf16[3,2,128,768]{3,2,1,0:T(8,128)(2,1)}, u32[]{:S(2)}, u32[]{:S(2)}) collective-permute-start(bf16[3,2,128,768]{3,2,1,0:T(8,128)(2,1)} %get-tuple-element.15), channel_id=1, source_target_pairs={{0,240},{16,0},{32,16},{48,32},{64,48},{80,64},{96,80},{112,96},{1... | collective-permute-start | bytes 3538952 | tf_op jit(solution)/shard_map/ppermute | solution.py:534
  37.6 4.9 %all-to-all-start.1 = ((bf16[8,112,128]{2,1,0:T(8,128)(2,1)}), bf16[8,112,128]{2,1,0:T(8,128)(2,1)S(1)}, u32[]{:S(2)}, u32[]{:S(2)}) async-start(bf16[8,112,128]{2,1,0:T(8,128)(2,1)} %get-tuple-element.17), calls=%async_computation.1 | async-start | bytes 458752 | tf_op jit(solution)/shard_map/all_to_all | solution.py:546
  42.5 2.7 %collective-permute-start.5 = (bf16[768,384]{1,0:T(8,128)(2,1)S(1)}, bf16[768,384]{1,0:T(8,128)(2,1)S(1)}, u32[]{:S(2)}, u32[]{:S(2)}) collective-permute-start(bf16[768,384]{1,0:T(8,128)(2,1)S(1)} %collective-permute-done.4.rest_1_), channel_id=1, source_target_pairs={{0,14},{2,0},{4,2},{6,4},{8,6},{10,8},{12,10},{14,12},{1,15},{3,1}... | collective-permute-start | bytes 1769480 | tf_op jit(solution)/shard_map/ppermute | solution.py:534
  45.3 6.3 %all-to-all-done.1.refs_0_ = bf16[8,112,128]{2,1,0:T(8,128)(2,1)S(1)} async-done(((bf16[8,112,128]{2,1,0:T(8,128)(2,1)}), bf16[8,112,128]{2,1,0:T(8,128)(2,1)S(1)}, u32[]{:S(2)}, u32[]{:S(2)}) %all-to-all-start.1) | async-done | bytes 229408 | tf_op jit(solution)/shard_map/all_to_all | solution.py:546
  52.7 3.6 %all-to-all-start.2 = ((bf16[16,96,128]{2,1,0:T(8,128)(2,1)}), bf16[16,96,128]{2,1,0:T(8,128)(2,1)S(1)}, u32[]{:S(2)}, u32[]{:S(2)}) async-start(bf16[16,96,128]{2,1,0:T(8,128)(2,1)} %text_finish_sums.1), calls=%async_computation.2 | async-start | bytes 786432 | tf_op jit(solution)/shard_map/all_to_all | solution.py:551
  56.9 3.6 %collective-permute-done.5.high.rest_2_ = bf16[768,384]{1,0:T(8,128)(2,1)S(1)} collective-permute-done((bf16[768,384]{1,0:T(8,128)(2,1)S(1)}, bf16[768,384]{1,0:T(8,128)(2,1)S(1)}, u32[]{:S(2)}, u32[]{:S(2)}) %collective-permute-start.5) | collective-permute-done | bytes 589856 | tf_op jit(solution)/shard_map/ppermute | solution.py:534
  60.5 2.3 %collective-permute-done.7.low.rest_5_ = bf16[768,384]{1,0:T(8,128)(2,1)S(1)} collective-permute-done((bf16[768,384]{1,0:T(8,128)(2,1)S(1)}, bf16[768,384]{1,0:T(8,128)(2,1)S(1)}, u32[]{:S(2)}, u32[]{:S(2)}) %collective-permute-start.7) | collective-permute-done | bytes 589856 | tf_op jit(solution)/shard_map/ppermute | solution.py:534
  62.9 2.8 %all-to-all-done.2.rest_0_.parts_h = bf16[16,96,128]{2,1,0:T(8,128)(2,1)S(1)} async-done(((bf16[16,96,128]{2,1,0:T(8,128)(2,1)}), bf16[16,96,128]{2,1,0:T(8,128)(2,1)S(1)}, u32[]{:S(2)}, u32[]{:S(2)}) %all-to-all-start.2) | async-done | bytes 393248 | tf_op jit(solution)/shard_map/all_to_all | solution.py:551
  67.1 1.4 %collective-permute-start.9 = (bf16[768,384]{1,0:T(8,128)(2,1)}, bf16[768,384]{1,0:T(8,128)(2,1)S(1)}, u32[]{:S(2)}, u32[]{:S(2)}) collective-permute-start(bf16[768,384]{1,0:T(8,128)(2,1)} %get-tuple-element.19), channel_id=1, source_target_pairs={{0,2},{2,4},{4,6},{6,8},{8,10},{10,12},{12,14},{14,0},{1,3},{3,5},... | collective-permute-start | bytes 1769480 | tf_op jit(solution)/shard_map/ppermute | solution.py:534
  68.5 8.1 %video_attention.1.after.rows_h = bf16[256,768]{1,0:T(8,128)(2,1)} custom-call(s32[5]{0:T(128)} %stack.15.pos, s32[108]{0:T(128)} %reshape.19.mask, s32[1,256]{1,0:T(1,128)} %bitcast.15, bf16[256,768]{1,0:T(8,128)(2,1)} %bitcast.13, bf16[256,768]{1,0:T(8,128)(2,1)} %rest_1_.1, bf16[256,768]{1,0:T(8,128)(2,1)} %rest_2_.1, bf16[2,256,768]{2,1,0:T(8,128)(2,1)} %bitcast.10, ...), custom_call_target="tpu_custom_call" | custom-call | flops 8999999488 | bytes 6291456 | tf_op jit(solution)/shard_map/video_attention/pallas_call | solution.py:389
  79.3 5.7 %collective-permute-start.11 = (bf16[384,384]{1,0:T(8,128)(2,1)S(1)}, bf16[384,384]{1,0:T(8,128)(2,1)S(1)}, u32[]{:S(2)}, u32[]{:S(2)}) collective-permute-start(bf16[384,384]{1,0:T(8,128)(2,1)S(1)} %get-tuple-element.21), channel_id=1, source_target_pairs={{0,14},{2,0},{4,2},{6,4},{8,6},{10,8},{12,10},{14,12},{1,15},{3,1}... | collective-permute-start | bytes 884744 | tf_op jit(solution)/shard_map/ppermute | solution.py:534
  85.0 4.0 %collective-permute-done.10.rest_7_ = bf16[384,384]{1,0:T(8,128)(2,1)S(1)} collective-permute-done((bf16[384,384]{1,0:T(8,128)(2,1)S(1)}, bf16[384,384]{1,0:T(8,128)(2,1)S(1)}, u32[]{:S(2)}, u32[]{:S(2)}) %collective-permute-start.10) | collective-permute-done | bytes 294944 | tf_op jit(solution)/shard_map/ppermute | solution.py:534
  89.1 2.3 %video_share.1 = bf16[256,1536]{1,0:T(8,128)(2,1)S(1)} custom-call(s32[5]{0:T(128)S(1)} %copy-done.3, bf16[256,768]{1,0:T(8,128)(2,1)S(1)} %copy-done.2, bf16[768,384]{1,0:T(8,128)(2,1)S(1)} %copy-done, bf16[768,384]{1,0:T(8,128)(2,1)S(1)} %collective-permute-done.4.rest_1_, bf16[768,384]{1,0:T(8,128)(2,1)S(1)} %collective-permute-done.5.high.rest_2_, ...), custom_call_target="tpu_custom_call" | custom-call | flops 603979776 | bytes 4194304 | tf_op jit(solution)/shard_map/video_share/pallas_call | solution.py:492
  91.4 5.8 %collective-permute-start.12 = (bf16[256,1536]{1,0:T(8,128)(2,1)S(1)}, bf16[256,1536]{1,0:T(8,128)(2,1)S(1)}, u32[]{:S(2)}, u32[]{:S(2)}) collective-permute-start(bf16[256,1536]{1,0:T(8,128)(2,1)S(1)} %video_share.1), channel_id=1, source_target_pairs={{0,1},{1,0},{2,3},{3,2},{4,5},{5,4},{6,7},{7,6},{8,9},{9,8},{10,11... | collective-permute-start | bytes 2359304 | tf_op jit(solution)/shard_map/ppermute | solution.py:562
  97.2 2.6 %text_share.1 = (bf16[256,768]{1,0:T(8,128)(2,1)S(1)}, bf16[256,1536]{1,0:T(8,128)(2,1)S(1)}) custom-call(s32[5]{0:T(128)S(1)} %copy-done.3, bf16[16,96,128]{2,1,0:T(8,128)(2,1)S(1)} %all-to-all-done.2.rest_0_.parts_h, bf16[768,384]{1,0:T(8,128)(2,1)S(1)} %copy-done, bf16[768,384]{1,0:T(8,128)(2,1)S(1)} %collective-permute-done.4.rest_1_, ...), custom_call_target="tpu_custom_call" | custom-call | flops 603979776 | bytes 4194304 | tf_op jit(solution)/shard_map/text_share/pallas_call | solution.py:492
  99.9 3.1 %video_finish.1 = bf16[256,1536]{1,0:T(8,128)(2,1)} custom-call(s32[5]{0:T(128)S(1)} %copy-done.3, bf16[256,768]{1,0:T(8,128)(2,1)S(1)} %copy-done.2, bf16[256,1536]{1,0:T(8,128)(2,1)S(1)} %collective-permute-done.12.other_h, bf16[768,384]{1,0:T(8,128)(2,1)S(1)} %copy-done, bf16[768,384]{1,0:T(8,128)(2,1)S(1)} %collective-permute-done.4.rest_1_, ...), custom_call_target="tpu_custom_call" | custom-call | flops 603979776 | bytes 4194304 | tf_op jit(solution)/shard_map/video_finish/pallas_call | solution.py:492
  103.0 3.1 %text_finish.1 = bf16[256,1536]{1,0:T(8,128)(2,1)} custom-call(s32[5]{0:T(128)S(1)} %copy-done.3, bf16[256,768]{1,0:T(8,128)(2,1)S(1)} %get-tuple-element.22.rows_h, bf16[256,1536]{1,0:T(8,128)(2,1)S(1)} %collective-permute-done.13.other_h, bf16[768,384]{1,0:T(8,128)(2,1)S(1)} %copy-done, bf16[768,384]{1,0:T(8,128)(2,1)S(1)} %collective-permute-done.4.rest_1_, ...), custom_call_target="tpu_custom_call" | custom-call | flops 603979776 | bytes 4194304 | tf_op jit(solution)/shard_map/text_finish/pallas_call | solution.py:492
  (34 shorter events, 7.3 us)
Async XLA Ops:
  0.6 28.8 %collective-permute-start = (bf16[2,256,768]{2,1,0:T(8,128)(2,1)}, bf16[2,256,768]{2,1,0:T(8,128)(2,1)}, u32[]{:S(2)}, u32[]{:S(2)}) collective-permute-start(bf16[2,256,768]{2,1,0:T(8,128)(2,1)} %bitcast.7), channel_id=1, source_target_pairs={{0,2},{2,4},{4,6},{6,8},{8,10},{10,12},{12,14},{14,0},{1,3},{3,5},... | collective-permute-start | bytes 2359304 | tf_op jit(solution)/shard_map/ppermute | solution.py:534
  3.2 26.3 %collective-permute-start.1 = (bf16[2,256,768]{2,1,0:T(8,128)(2,1)}, bf16[2,256,768]{2,1,0:T(8,128)(2,1)}, u32[]{:S(2)}, u32[]{:S(2)}) collective-permute-start(bf16[2,256,768]{2,1,0:T(8,128)(2,1)} %bitcast.8), channel_id=1, source_target_pairs={{0,14},{2,0},{4,2},{6,4},{8,6},{10,8},{12,10},{14,12},{1,15},{3,1}... | collective-permute-start | bytes 2359304 | tf_op jit(solution)/shard_map/ppermute | solution.py:534
  7.8 21.6 %copy-start.4 = (bf16[2,8,4,8,768]{4,3,2,1,0:T(8,128)(2,1)S(1)}, bf16[2,8,4,8,768]{4,3,2,1,0:T(8,128)(2,1)}, u32[]{:S(2)}) copy-start(bf16[2,8,4,8,768]{4,3,2,1,0:T(8,128)(2,1)} %param.9) | copy-start | bytes 2359300
  13.1 16.4 %all-to-all-start = ((bf16[16,112,128]{2,1,0:T(8,128)(2,1)}), bf16[16,112,128]{2,1,0:T(8,128)(2,1)S(1)}, u32[]{:S(2)}, u32[]{:S(2)}) async-start(bf16[16,112,128]{2,1,0:T(8,128)(2,1)} %get-tuple-element.13), calls=%async_computation | async-start | bytes 917504 | tf_op jit(solution)/shard_map/all_to_all | solution.py:542
  19.9 22.6 %collective-permute-start.4 = (bf16[768,384]{1,0:T(8,128)(2,1)}, bf16[768,384]{1,0:T(8,128)(2,1)S(1)}, u32[]{:S(2)}, u32[]{:S(2)}) collective-permute-start(bf16[768,384]{1,0:T(8,128)(2,1)} %get-tuple-element.16), channel_id=1, source_target_pairs={{0,14},{2,0},{4,2},{6,4},{8,6},{10,8},{12,10},{14,12},{1,15},{3,1}... | collective-permute-start | bytes 1769480 | tf_op jit(solution)/shard_map/ppermute | solution.py:534
  21.3 24.0 %collective-permute-start.6 = (bf16[768,384]{1,0:T(8,128)(2,1)}, bf16[768,384]{1,0:T(8,128)(2,1)S(1)}, u32[]{:S(2)}, u32[]{:S(2)}) collective-permute-start(bf16[768,384]{1,0:T(8,128)(2,1)} %get-tuple-element.16), channel_id=1, source_target_pairs={{0,2},{2,4},{4,6},{6,8},{8,10},{10,12},{12,14},{14,0},{1,3},{3,5},... | collective-permute-start | bytes 1769480 | tf_op jit(solution)/shard_map/ppermute | solution.py:534
  32.7 32.9 %collective-permute-start.2 = (bf16[3,2,128,768]{3,2,1,0:T(8,128)(2,1)}, bf16[3,2,128,768]{3,2,1,0:T(8,128)(2,1)}, u32[]{:S(2)}, u32[]{:S(2)}) collective-permute-start(bf16[3,2,128,768]{3,2,1,0:T(8,128)(2,1)} %get-tuple-element.14), channel_id=1, source_target_pairs={{0,16},{16,32},{32,48},{48,64},{64,80},{80,96},{96,112},{112,128},... | collective-permute-start | bytes 3538952 | tf_op jit(solution)/shard_map/ppermute | solution.py:534
  33.2 32.4 %collective-permute-start.3 = (bf16[3,2,128,768]{3,2,1,0:T(8,128)(2,1)}, bf16[3,2,128,768]{3,2,1,0:T(8,128)(2,1)}, u32[]{:S(2)}, u32[]{:S(2)}) collective-permute-start(bf16[3,2,128,768]{3,2,1,0:T(8,128)(2,1)} %get-tuple-element.15), channel_id=1, source_target_pairs={{0,240},{16,0},{32,16},{48,32},{64,48},{80,64},{96,80},{112,96},{1... | collective-permute-start | bytes 3538952 | tf_op jit(solution)/shard_map/ppermute | solution.py:534
  37.6 14.0 %all-to-all-start.1 = ((bf16[8,112,128]{2,1,0:T(8,128)(2,1)}), bf16[8,112,128]{2,1,0:T(8,128)(2,1)S(1)}, u32[]{:S(2)}, u32[]{:S(2)}) async-start(bf16[8,112,128]{2,1,0:T(8,128)(2,1)} %get-tuple-element.17), calls=%async_computation.1 | async-start | bytes 458752 | tf_op jit(solution)/shard_map/all_to_all | solution.py:546
  42.5 13.7 %copy-start.5 = (s32[2,1,2,27]{3,2,1,0:T(2,128)S(1)}, s32[2,1,2,27]{3,2,1,0:T(2,128)}, u32[]{:S(2)}) copy-start(s32[2,1,2,27]{3,2,1,0:T(2,128)} %param.13) | copy-start | bytes 1300
  42.5 18.0 %collective-permute-start.5 = (bf16[768,384]{1,0:T(8,128)(2,1)S(1)}, bf16[768,384]{1,0:T(8,128)(2,1)S(1)}, u32[]{:S(2)}, u32[]{:S(2)}) collective-permute-start(bf16[768,384]{1,0:T(8,128)(2,1)S(1)} %collective-permute-done.4.rest_1_), channel_id=1, source_target_pairs={{0,14},{2,0},{4,2},{6,4},{8,6},{10,8},{12,10},{14,12},{1,15},{3,1}... | collective-permute-start | bytes 1769480 | tf_op jit(solution)/shard_map/ppermute | solution.py:534
  45.3 17.6 %collective-permute-start.7 = (bf16[768,384]{1,0:T(8,128)(2,1)S(1)}, bf16[768,384]{1,0:T(8,128)(2,1)S(1)}, u32[]{:S(2)}, u32[]{:S(2)}) collective-permute-start(bf16[768,384]{1,0:T(8,128)(2,1)S(1)} %collective-permute-done.6.rest_6_), channel_id=1, source_target_pairs={{0,2},{2,4},{4,6},{6,8},{8,10},{10,12},{12,14},{14,0},{1,3},{3,5},... | collective-permute-start | bytes 1769480 | tf_op jit(solution)/shard_map/ppermute | solution.py:534
  52.7 13.0 %all-to-all-start.2 = ((bf16[16,96,128]{2,1,0:T(8,128)(2,1)}), bf16[16,96,128]{2,1,0:T(8,128)(2,1)S(1)}, u32[]{:S(2)}, u32[]{:S(2)}) async-start(bf16[16,96,128]{2,1,0:T(8,128)(2,1)} %text_finish_sums.1), calls=%async_computation.2 | async-start | bytes 786432 | tf_op jit(solution)/shard_map/all_to_all | solution.py:551
  66.9 9.6 %collective-permute-start.8 = (bf16[768,384]{1,0:T(8,128)(2,1)}, bf16[768,384]{1,0:T(8,128)(2,1)S(1)}, u32[]{:S(2)}, u32[]{:S(2)}) collective-permute-start(bf16[768,384]{1,0:T(8,128)(2,1)} %get-tuple-element.18), channel_id=1, source_target_pairs={{0,14},{2,0},{4,2},{6,4},{8,6},{10,8},{12,10},{14,12},{1,15},{3,1}... | collective-permute-start | bytes 1769480 | tf_op jit(solution)/shard_map/ppermute | solution.py:534
  67.1 10.9 %collective-permute-start.9 = (bf16[768,384]{1,0:T(8,128)(2,1)}, bf16[768,384]{1,0:T(8,128)(2,1)S(1)}, u32[]{:S(2)}, u32[]{:S(2)}) collective-permute-start(bf16[768,384]{1,0:T(8,128)(2,1)} %get-tuple-element.19), channel_id=1, source_target_pairs={{0,2},{2,4},{4,6},{6,8},{8,10},{10,12},{12,14},{14,0},{1,3},{3,5},... | collective-permute-start | bytes 1769480 | tf_op jit(solution)/shard_map/ppermute | solution.py:534
  68.5 20.6 %copy-start.3 = (s32[5]{0:T(128)S(1)}, s32[5]{0:T(128)}, u32[]{:S(2)}) copy-start(s32[5]{0:T(128)} %stack.15.pos) | copy-start | bytes 64
  76.5 12.5 %copy-start = (bf16[768,384]{1,0:T(8,128)(2,1)S(1)}, bf16[768,384]{1,0:T(8,128)(2,1)}, u32[]{:S(2)}) copy-start(bf16[768,384]{1,0:T(8,128)(2,1)} %rest_0_.7) | copy-start | bytes 1769476
  77.9 1.0 copy-start.1
  78.9 10.1 %copy-start.2 = (bf16[256,768]{1,0:T(8,128)(2,1)S(1)}, bf16[256,768]{1,0:T(8,128)(2,1)}, u32[]{:S(2)}) copy-start(bf16[256,768]{1,0:T(8,128)(2,1)} %video_attention.1.after.rows_h) | copy-start | bytes 1179652
  79.2 9.8 %collective-permute-start.10 = (bf16[384,384]{1,0:T(8,128)(2,1)S(1)}, bf16[384,384]{1,0:T(8,128)(2,1)S(1)}, u32[]{:S(2)}, u32[]{:S(2)}) collective-permute-start(bf16[384,384]{1,0:T(8,128)(2,1)S(1)} %get-tuple-element.20), channel_id=1, source_target_pairs={{0,2},{2,4},{4,6},{6,8},{8,10},{10,12},{12,14},{14,0},{1,3},{3,5},... | collective-permute-start | bytes 884744 | tf_op jit(solution)/shard_map/ppermute | solution.py:534
  79.3 9.7 %collective-permute-start.11 = (bf16[384,384]{1,0:T(8,128)(2,1)S(1)}, bf16[384,384]{1,0:T(8,128)(2,1)S(1)}, u32[]{:S(2)}, u32[]{:S(2)}) collective-permute-start(bf16[384,384]{1,0:T(8,128)(2,1)S(1)} %get-tuple-element.21), channel_id=1, source_target_pairs={{0,14},{2,0},{4,2},{6,4},{8,6},{10,8},{12,10},{14,12},{1,15},{3,1}... | collective-permute-start | bytes 884744 | tf_op jit(solution)/shard_map/ppermute | solution.py:534
  91.4 8.5 %collective-permute-start.12 = (bf16[256,1536]{1,0:T(8,128)(2,1)S(1)}, bf16[256,1536]{1,0:T(8,128)(2,1)S(1)}, u32[]{:S(2)}, u32[]{:S(2)}) collective-permute-start(bf16[256,1536]{1,0:T(8,128)(2,1)S(1)} %video_share.1), channel_id=1, source_target_pairs={{0,1},{1,0},{2,3},{3,2},{4,5},{5,4},{6,7},{7,6},{8,9},{9,8},{10,11... | collective-permute-start | bytes 2359304 | tf_op jit(solution)/shard_map/ppermute | solution.py:562
  99.8 3.2 %collective-permute-start.13 = (bf16[256,1536]{1,0:T(8,128)(2,1)S(1)}, bf16[256,1536]{1,0:T(8,128)(2,1)S(1)}, u32[]{:S(2)}, u32[]{:S(2)}) collective-permute-start(bf16[256,1536]{1,0:T(8,128)(2,1)S(1)} %get-tuple-element.23), channel_id=1, source_target_pairs={{0,1},{1,0},{2,3},{3,2},{4,5},{5,4},{6,7},{7,6},{8,9},{9,8},{10,11... | collective-permute-start | bytes 2359304 | tf_op jit(solution)/shard_map/ppermute | solution.py:562

commit v4 on v3

--- a/solution.py
+++ b/solution.py
@@ -222,23 +222,6 @@
     )(*parts, *after)
 
 
-def relay_kernel(low, high, *rest):
-    low_out, high_out, held, sems = rest[-4:]
-    pairs = ((low, low_out), (high, high_out))
-    inward = [
-        pltpu.make_async_copy(ref, held.at[i], sems.at[0, i]) for i, (ref, _) in enumerate(pairs)
-    ]
-    onward = [
-        pltpu.make_async_copy(held.at[i], out, sems.at[1, i]) for i, (_, out) in enumerate(pairs)
-    ]
-    for copy in inward:
-        copy.start()
-    for copy, following in zip(inward, onward):
-        copy.wait()
-        following.start()
-    wait_all(onward)
-
-
 def halves_kernel(low, high, after, low_out, high_out, held, sems):
     half = low_out.shape[0]
     inward = [
@@ -271,21 +254,8 @@
     )(low, high, after)
 
 
-def relay(low, high, *after):
-    return pl.pallas_call(
-        relay_kernel,
-        in_specs=[ANY] * (2 + len(after)),
-        out_specs=(ANY, ANY),
-        out_shape=[jax.ShapeDtypeStruct(x.shape, BF) for x in (low, high)],
-        scratch_shapes=[pltpu.VMEM((2, *low.shape), BF), pltpu.SemaphoreType.DMA((2, 2))],
-        cost_estimate=pl.CostEstimate(flops=0, bytes_accessed=4 << 20, transcendentals=0),
-        compiler_params=pltpu.CompilerParams(vmem_limit_bytes=16 << 20),
-        name="relay",
-    )(low, high, *after)
-
-
 def video_kernel(pos, mask, valid, *rest):
-    far, out_h, near, out, bias_s, sems = rest[:8], rest[8], rest[9:17], *rest[17:]
+    far, out_h, near, out, bias_s, sems = rest[:8], rest[9], rest[10:18], *rest[18:]
     q, tk, tv, own, z_low, z_high, t_low, t_high = near
     pairs = list(zip(far, near))
     begun = fetch(pairs, sems.at[0], FIRST)
@@ -401,11 +371,9 @@
     )(pos, mask, valid, *arrays)
 
 
-def project(pos, blocks, mine, held, sems, read, put, out, sent, out_sems):
+def project(pos, near, mine, held, sems, read, put, out, sent, out_sems):
     width = held.shape[1] // 4
-    near, (top, bottom) = blocks[:7], blocks[7:]
-    half = top.shape[0]
-    for step, ref in list(zip((0, 1, 2, 3, 5, 6, 7), near)) + [(4, None)]:
+    for step, ref in zip((0, 1, 2, 3, 5, 6, 7), near):
         column = jnp.bitwise_and(pos[1] + step, 7)
         is_mine = lax.shift_right_logical(column, 2) == pos[2]
         slot = jnp.bitwise_and(column, 3)
@@ -413,19 +381,22 @@
 
         @pl.when(is_mine if mine else jnp.logical_not(is_mine))
         def _():
-            if ref is None:
-                for part, piece in enumerate((top, bottom)):
-                    target = held.at[part * half : (part + 1) * half, columns]
-                    pltpu.make_async_copy(piece, target, sems.at[slot]).start()
-            else:
-                pltpu.make_async_copy(ref, held.at[:, columns], sems.at[slot]).start()
-
+            pltpu.make_async_copy(ref, held.at[:, columns], sems.at[slot]).start()
+
+    column = jnp.bitwise_and(pos[1] + 4, 7)
+    is_mine = lax.shift_right_logical(column, 2) == pos[2]
+    late = is_mine if mine else jnp.logical_not(is_mine)
+    late_slot = jnp.bitwise_and(column, 3)
     left = read()
     copies = []
     for pair in range(2):
         for slot in (2 * pair, 2 * pair + 1):
             columns = slice(slot * width, (slot + 1) * width)
-            pltpu.make_async_copy(near[0], held.at[:, columns], sems.at[slot]).wait()
+
+            @pl.when(jnp.logical_not(late & (late_slot == slot)))
+            def _():
+                pltpu.make_async_copy(near[0], held.at[:, columns], sems.at[slot]).wait()
+
         columns = slice(2 * pair * width, 2 * (pair + 1) * width)
         sent[:, columns] = put(columns, dot(left, held[:, columns])).astype(BF)
         copies.append(
@@ -435,8 +406,14 @@
     wait_all(copies)
 
 
+def by_head(parts):
+    flat = parts.reshape(HEADS_HERE * TEXT, HEAD_DIM)
+    heads = [flat[head * TEXT : (head + 1) * TEXT] for head in range(HEADS_HERE)]
+    return jnp.concatenate(heads, axis=1)
+
+
 def text_share_kernel(pos, parts_h, *rest):
-    blocks, rest = rest[:9], rest[9:]
+    blocks, rest = rest[:7], rest[8:]
     rows_h, share, parts, rows, in_sems, held, sent, sems, out_sems = rest
     rows_copy = pltpu.make_async_copy(rows, rows_h, in_sems.at[1])
     copy = pltpu.make_async_copy(parts_h, parts, in_sems.at[0])
@@ -444,9 +421,7 @@
 
     def read():
         copy.wait()
-        flat = parts[...].reshape(HEADS_HERE * TEXT, HEAD_DIM)
-        heads = [flat[head * TEXT : (head + 1) * TEXT] for head in range(HEADS_HERE)]
-        rows[...] = jnp.concatenate(heads, axis=1)
+        rows[...] = by_head(parts[...])
         rows_copy.start()
         return rows[...]
 
@@ -455,7 +430,7 @@
 
 
 def share_kernel(pos, rows_h, *rest):
-    blocks, rest = rest[:9], rest[9:]
+    blocks, rest = rest[:7], rest[7:]
     share, rows, in_sems, held, sent, sems, out_sems = rest
     copy = pltpu.make_async_copy(rows_h, rows, in_sems.at[0])
     copy.start()
@@ -468,7 +443,7 @@
 
 
 def finish_kernel(pos, rows_h, other_h, *rest):
-    blocks, rest = rest[:9], rest[9:]
+    blocks, rest = rest[:7], rest[7:]
     out, rows, other, in_sems, held, sent, sems, out_sems = rest
     copies = [
         pltpu.make_async_copy(rows_h, rows, in_sems.at[0]),
@@ -487,11 +462,11 @@
     project(pos, blocks, True, held, sems, read, put, out, sent, out_sems)
 
 
-def project_call(kernel, name, pos, left, blocks, out_shape, out_specs, scratch):
+def project_call(kernel, name, pos, left, blocks, out_shape, out_specs, scratch, after=()):
     depth, width = blocks[0].shape
     return pl.pallas_call(
         kernel,
-        in_specs=[SCALARS] + [FAR] + [ANY] * (len(left) - 1) + [FAR] * 7 + [ANY] * 2,
+        in_specs=[SCALARS] + [FAR] + [ANY] * (len(left) - 1) + [FAR] * 7 + [ANY] * len(after),
         out_specs=out_specs,
         out_shape=out_shape,
         scratch_shapes=[pltpu.VMEM(x.shape, BF) for x in left]
@@ -508,7 +483,93 @@
         ),
         compiler_params=pltpu.CompilerParams(vmem_limit_bytes=24 << 20),
         name=name,
-    )(pos, *left, *blocks)
+    )(pos, *left, *blocks, *after)
+
+
+def far_kernel(video_h, parts_h, top_h, bottom_h, terms, share, rows, parts, w, sems):
+    half = top_h.shape[0]
+    copies = [
+        pltpu.make_async_copy(source, target, sems.at[i])
+        for i, (source, target) in enumerate(
+            (
+                (video_h, rows.at[0:OWN]),
+                (parts_h, parts),
+                (top_h, w.at[0:half]),
+                (bottom_h, w.at[half : 2 * half]),
+            )
+        )
+    ]
+    for copy in copies:
+        copy.start()
+    wait_all(copies)
+    rows[OWN : OWN + TEXT] = by_head(parts[...])
+    terms[...] = dot(rows[...], w[...])
+    share[...] = terms[...].astype(BF)
+
+
+def far_terms(video, parts, top, bottom):
+    shape, depth, width = (OWN + TEXT, top.shape[1]), 2 * top.shape[0], top.shape[1]
+    return pl.pallas_call(
+        far_kernel,
+        in_specs=[ANY] * 4,
+        out_specs=(WHOLE, WHOLE),
+        out_shape=(jax.ShapeDtypeStruct(shape, F32), jax.ShapeDtypeStruct(shape, BF)),
+        scratch_shapes=[
+            pltpu.VMEM((OWN + TEXT, depth), BF),
+            pltpu.VMEM(parts.shape, BF),
+            pltpu.VMEM((depth, width), BF),
+            pltpu.SemaphoreType.DMA((4,)),
+        ],
+        cost_estimate=pl.CostEstimate(
+            flops=2 * shape[0] * depth * width, bytes_accessed=4 << 20, transcendentals=0
+        ),
+        compiler_params=pltpu.CompilerParams(vmem_limit_bytes=24 << 20),
+        name="far_terms",
+    )(video, parts, top, bottom)
+
+
+def last_kernel(pos, terms_h, other_h, video_in, text_in, video, text, terms, other, done, sems):
+    width = terms.shape[1]
+    column = jnp.bitwise_and(pos[1] + 4, 7)
+    slot = jnp.bitwise_and(column, 3)
+    columns = pl.ds(pl.multiple_of(slot * width, width), width)
+
+    @pl.when(lax.shift_right_logical(column, 2) == pos[2])
+    def _():
+        copies = [
+            pltpu.make_async_copy(terms_h, terms, sems.at[0]),
+            pltpu.make_async_copy(other_h, other, sems.at[1]),
+        ]
+        for copy in copies:
+            copy.start()
+        wait_all(copies)
+        done[...] = (terms[...] + other[...].astype(F32)).astype(BF)
+        copies = [
+            pltpu.make_async_copy(done.at[0:OWN], video.at[:, columns], sems.at[2]),
+            pltpu.make_async_copy(done.at[OWN : OWN + TEXT], text.at[:, columns], sems.at[3]),
+        ]
+        for copy in copies:
+            copy.start()
+        wait_all(copies)
+
+
+def last_columns(pos, terms, other, video, text):
+    return pl.pallas_call(
+        last_kernel,
+        in_specs=[SCALARS] + [ANY] * 4,
+        out_specs=(ANY, ANY),
+        out_shape=[jax.ShapeDtypeStruct(x.shape, BF) for x in (video, text)],
+        input_output_aliases={3: 0, 4: 1},
+        scratch_shapes=[
+            pltpu.VMEM(terms.shape, F32),
+            pltpu.VMEM(terms.shape, BF),
+            pltpu.VMEM(terms.shape, BF),
+            pltpu.SemaphoreType.DMA((4,)),
+        ],
+        cost_estimate=pl.CostEstimate(flops=0, bytes_accessed=3 << 20, transcendentals=0),
+        compiler_params=pltpu.CompilerParams(vmem_limit_bytes=24 << 20),
+        name="last_columns",
+    )(pos, terms, other, video, text)
 
 
 def shards(video_q, video_kv, text_q, text_k, text_v, tile_mask, text_valid, w_out):
@@ -549,11 +610,11 @@
     after.append(down(high, "height"))
     sums = combine([parts], t_count, True, "text_finish_sums")
     parts = lax.all_to_all(sums, "tm", 0, 0, tiled=True)
-    low, high = relay(before[1], after[1], parts, t_low, t_high)
+    low, high = before[1], after[1]
     before.append(up(low, "height"))
     after.append(down(high, "height"))
     video_rows = video_attention(
-        pos, mask, valid, q, text_k, text_v, own, z_low, z_high, t_low, t_high
+        pos, mask, valid, q, text_k, text_v, own, z_low, z_high, t_low, t_high, parts
     )
     low, high = halves(before[2], after[2], video_rows)
     far = [up(low, "height"), down(high, "height")]
@@ -561,11 +622,12 @@
     def swap(x):
         return lax.ppermute(x, "head", [(0, 1), (1, 0)])
 
-    blocks = [w_out] + after + before[::-1] + far
+    blocks = [w_out] + after + before[::-1]
     full = jax.ShapeDtypeStruct((OWN, 4 * w_out.shape[1]), BF)
     video_other = swap(
         project_call(share_kernel, "video_share", pos, [video_rows], blocks, full, FAR, [])
     )
+    terms, share = far_terms(video_rows, parts, *far)
     text_rows, text_other = project_call(
         text_share_kernel,
         "text_share",
@@ -575,6 +637,7 @@
         (jax.ShapeDtypeStruct((TEXT, WIDTH), BF), full),
         (FAR, FAR),
         [pltpu.VMEM((TEXT, WIDTH), BF)],
+        [terms],
     )
     text_other = swap(text_other)
     video_out = project_call(
@@ -583,6 +646,7 @@
     text_out = project_call(
         finish_kernel, "text_finish", pos, [text_rows, text_other], blocks, full, FAR, []
     )
+    video_out, text_out = last_columns(pos, terms, swap(share), video_out, text_out)
     return video_out.reshape(frames, rows, cols, -1), text_out
 
 

time: 107 us -> 103 us (0.963)
  waiting for transfers between devices: 28.5 us -> 19.8 us
  Pallas kernels: 30.3 us -> 32.7 us
  starting transfers between devices: 44.2 us -> 46.6 us
    ppermute x12, waiting for transfers between devices: 11.4 us -> 5.52 us  [up(): return lax.ppermute(x, axis, [(i, (i + by) % n) for i in range(n)])]
    ppermute x2 -> x3, starting transfers between devices: 5.88 us -> 8.24 us  [swap(): return lax.ppermute(x, 'head', [(0, 1), (1, 0)])]
    pallas_call x1 -> x2, Pallas kernels: 1.28 us -> 3.43 us  [the longest x1 1.78 us: far_terms(): pl.pallas_call(far_kernel, in_specs=[ANY] * 4, out_specs=(WHOLE, WHOLE),...]
    all_to_all x1, waiting for transfers between devices: 2.78 us -> 1.19 us  [shards(): parts = lax.all_to_all(sums, 'tm', 0, 0, tiled=True)]
    all_to_all x1, waiting for transfers between devices: 8.04 us -> 6.83 us  [shards(): parts = lax.all_to_all(parts, 'tm', 0, 0, tiled=True)]
  transfers between devices with their start and end apart: 17 -> 18, of which waited for: 7 -> 5; matrix products, arithmetic and copies ran while one was open for 1% -> 1% of each run, Pallas kernels for 22% -> 30%
where the time goes in v4:
time: 103 us; the launch traced here: 102 us
  starting transfers between devices  46.6 us (45%)
  Pallas kernels  32.7 us (32%)
  waiting for transfers between devices  19.8 us (19%)
  local copies, waits for them, and re-layouts  2.27 us (2%)
    ppermute x12, starting transfers between devices, up(): return lax.ppermute(x, axis, [(i, (i + by) % n) for i in range(n)])  22.5 us
    pallas_call x4, Pallas kernels, project_call(): pl.pallas_call(kernel, in_specs=[SCALARS] + [FAR] + [ANY] * (len(left) -...  11.5 us
    ppermute x3, starting transfers between devices, swap(): return lax.ppermute(x, 'head', [(0, 1), (1, 0)])  8.24 us
    pallas_call x1, Pallas kernels, video_attention(): pl.pallas_call(video_kernel, in_specs=[SCALARS, SCALARS, WHOLE] + [FAR] *...  7.97 us
    all_to_all x1, waiting for transfers between devices, shards(): parts = lax.all_to_all(parts, 'tm', 0, 0, tiled=True)  6.83 us
    all_to_all x1, starting transfers between devices, shards(): parts = lax.all_to_all(parts, 'tm', 0, 0, tiled=True)  6.76 us
    all_to_all x1, waiting for transfers between devices, shards(): parts = lax.all_to_all(parts, 'height', 0, 0, tiled=True)  6.23 us
    ppermute x12, waiting for transfers between devices, up(): return lax.ppermute(x, axis, [(i, (i + by) % n) for i in range(n)])  5.52 us
  transfers between devices with their start and end apart: 18, of which 5 were waited for; matrix products, arithmetic and copies ran while one was open for 1% of the time, Pallas kernels for 30%

profile of v4, /device:TPU:1, one launch (start us, length us, event | category | flops | bytes accessed | tf_op | source)
XLA Modules:
  0.0 102.3 jit_solution(1125868517450010669)
XLA Ops:
  0.6 2.5 %collective-permute-start = (bf16[2,256,768]{2,1,0:T(8,128)(2,1)}, bf16[2,256,768]{2,1,0:T(8,128)(2,1)}, u32[]{:S(2)}, u32[]{:S(2)}) collective-permute-start(bf16[2,256,768]{2,1,0:T(8,128)(2,1)} %bitcast.7), channel_id=1, source_target_pairs={{0,2},{2,4},{4,6},{6,8},{8,10},{10,12},{12,14},{14,0},{1,3},{3,5},... | collective-permute-start | bytes 2359304 | tf_op jit(solution)/shard_map/ppermute | solution.py:595
  3.2 4.0 %collective-permute-start.1 = (bf16[2,256,768]{2,1,0:T(8,128)(2,1)}, bf16[2,256,768]{2,1,0:T(8,128)(2,1)}, u32[]{:S(2)}, u32[]{:S(2)}) collective-permute-start(bf16[2,256,768]{2,1,0:T(8,128)(2,1)} %bitcast.8), channel_id=1, source_target_pairs={{0,14},{2,0},{4,2},{6,4},{8,6},{10,8},{12,10},{14,12},{1,15},{3,1}... | collective-permute-start | bytes 2359304 | tf_op jit(solution)/shard_map/ppermute | solution.py:595
  7.9 5.3 %text_part.1 = (bf16[16,112,128]{2,1,0:T(8,128)(2,1)}, bf16[768,384]{1,0:T(8,128)(2,1)}) custom-call(s32[5]{0:T(128)} %stack.15.pos, s32[1,256]{1,0:T(1,128)} %bitcast.14, bf16[256,768]{1,0:T(8,128)(2,1)} %tq_h.1, bf16[2,256,768]{2,1,0:T(8,128)(2,1)} %bitcast.9, bf16[256,768]{1,0:T(8,128)(2,1)} %rest_1_.1, bf16[256,768]{1,0:T(8,128)(2,1)} %rest_2_.1, ...), custom_call_target="tpu_custom_call" | custom-call | flops 5000000000 | bytes 2097152 | tf_op jit(solution)/shard_map/text_part/pallas_call | solution.py:121
  13.1 6.8 %all-to-all-start = ((bf16[16,112,128]{2,1,0:T(8,128)(2,1)}), bf16[16,112,128]{2,1,0:T(8,128)(2,1)S(1)}, u32[]{:S(2)}, u32[]{:S(2)}) async-start(bf16[16,112,128]{2,1,0:T(8,128)(2,1)} %get-tuple-element.15), calls=%async_computation | async-start | bytes 917504 | tf_op jit(solution)/shard_map/all_to_all | solution.py:603
  20.0 2.7 %collective-permute-start.7 = (bf16[768,384]{1,0:T(8,128)(2,1)}, bf16[768,384]{1,0:T(8,128)(2,1)S(1)}, u32[]{:S(2)}, u32[]{:S(2)}) collective-permute-start(bf16[768,384]{1,0:T(8,128)(2,1)} %get-tuple-element.19), channel_id=1, source_target_pairs={{0,14},{2,0},{4,2},{6,4},{8,6},{10,8},{12,10},{14,12},{1,15},{3,1}... | collective-permute-start | bytes 1769480 | tf_op jit(solution)/shard_map/ppermute | solution.py:595
  22.7 6.8 %all-to-all-done.parts = bf16[16,112,128]{2,1,0:T(8,128)(2,1)S(1)} async-done(((bf16[16,112,128]{2,1,0:T(8,128)(2,1)}), bf16[16,112,128]{2,1,0:T(8,128)(2,1)S(1)}, u32[]{:S(2)}, u32[]{:S(2)}) %all-to-all-start) | async-done | bytes 458784 | tf_op jit(solution)/shard_map/all_to_all | solution.py:603
  29.5 3.2 %text_merge.1 = (bf16[8,112,128]{2,1,0:T(8,128)(2,1)}, bf16[3,2,128,768]{3,2,1,0:T(8,128)(2,1)}, bf16[3,2,128,768]{3,2,1,0:T(8,128)(2,1)}) custom-call(bf16[16,112,128]{2,1,0:T(8,128)(2,1)S(1)} %all-to-all-done.parts, bf16[2,256,768]{2,1,0:T(8,128)(2,1)S(1)} %bitcast.11, bf16[2,256,768]{2,1,0:T(8,128)(2,1)} %collective-permute-done.z_low.rest_4_, ...), custom_call_target="tpu_custom_call" | custom-call | flops 2000000000 | bytes 6291456 | tf_op jit(solution)/shard_map/text_merge/pallas_call | solution.py:163
  33.3 4.3 %collective-permute-start.3 = (bf16[3,2,128,768]{3,2,1,0:T(8,128)(2,1)}, bf16[3,2,128,768]{3,2,1,0:T(8,128)(2,1)}, u32[]{:S(2)}, u32[]{:S(2)}) collective-permute-start(bf16[3,2,128,768]{3,2,1,0:T(8,128)(2,1)} %get-tuple-element.17), channel_id=1, source_target_pairs={{0,240},{16,0},{32,16},{48,32},{64,48},{80,64},{96,80},{112,96},{1... | collective-permute-start | bytes 3538952 | tf_op jit(solution)/shard_map/ppermute | solution.py:595
  37.6 4.9 %all-to-all-start.1 = ((bf16[8,112,128]{2,1,0:T(8,128)(2,1)}), bf16[8,112,128]{2,1,0:T(8,128)(2,1)S(1)}, u32[]{:S(2)}, u32[]{:S(2)}) async-start(bf16[8,112,128]{2,1,0:T(8,128)(2,1)} %get-tuple-element.18), calls=%async_computation.1 | async-start | bytes 458752 | tf_op jit(solution)/shard_map/all_to_all | solution.py:607
  42.5 1.5 %collective-permute-start.5 = (bf16[768,384]{1,0:T(8,128)(2,1)S(1)}, bf16[768,384]{1,0:T(8,128)(2,1)S(1)}, u32[]{:S(2)}, u32[]{:S(2)}) collective-permute-start(bf16[768,384]{1,0:T(8,128)(2,1)S(1)} %collective-permute-done.4.rest_6_), channel_id=1, source_target_pairs={{0,2},{2,4},{4,6},{6,8},{8,10},{10,12},{12,14},{14,0},{1,3},{3,5},... | collective-permute-start | bytes 1769480 | tf_op jit(solution)/shard_map/ppermute | solution.py:595
  45.4 6.2 %all-to-all-done.1.refs_0_ = bf16[8,112,128]{2,1,0:T(8,128)(2,1)S(1)} async-done(((bf16[8,112,128]{2,1,0:T(8,128)(2,1)}), bf16[8,112,128]{2,1,0:T(8,128)(2,1)S(1)}, u32[]{:S(2)}, u32[]{:S(2)}) %all-to-all-start.1) | async-done | bytes 229408 | tf_op jit(solution)/shard_map/all_to_all | solution.py:607
  52.7 4.2 %all-to-all-start.2 = ((bf16[16,96,128]{2,1,0:T(8,128)(2,1)}), bf16[16,96,128]{2,1,0:T(8,128)(2,1)}, u32[]{:S(2)}, u32[]{:S(2)}) async-start(bf16[16,96,128]{2,1,0:T(8,128)(2,1)} %text_finish_sums.1), calls=%async_computation.2 | async-start | bytes 786432 | tf_op jit(solution)/shard_map/all_to_all | solution.py:612
  57.5 4.2 %collective-permute-done.5.rest_5_ = bf16[768,384]{1,0:T(8,128)(2,1)S(1)} collective-permute-done((bf16[768,384]{1,0:T(8,128)(2,1)S(1)}, bf16[768,384]{1,0:T(8,128)(2,1)S(1)}, u32[]{:S(2)}, u32[]{:S(2)}) %collective-permute-start.5) | collective-permute-done | bytes 589856 | tf_op jit(solution)/shard_map/ppermute | solution.py:595
  61.7 2.7 %collective-permute-start.9 = (bf16[768,384]{1,0:T(8,128)(2,1)S(1)}, bf16[768,384]{1,0:T(8,128)(2,1)S(1)}, u32[]{:S(2)}, u32[]{:S(2)}) collective-permute-start(bf16[768,384]{1,0:T(8,128)(2,1)S(1)} %collective-permute-done.8.rest_2_), channel_id=1, source_target_pairs={{0,14},{2,0},{4,2},{6,4},{8,6},{10,8},{12,10},{14,12},{1,15},{3,1}... | collective-permute-start | bytes 1769480 | tf_op jit(solution)/shard_map/ppermute | solution.py:595
  65.6 8.0 %video_attention.1.after.video_h.rows_h = bf16[256,768]{1,0:T(8,128)(2,1)} custom-call(s32[5]{0:T(128)} %stack.15.pos, s32[108]{0:T(128)} %reshape.19.mask, s32[1,256]{1,0:T(1,128)} %bitcast.15, bf16[256,768]{1,0:T(8,128)(2,1)} %bitcast.13, bf16[256,768]{1,0:T(8,128)(2,1)} %rest_1_.1, bf16[256,768]{1,0:T(8,128)(2,1)} %rest_2_.1, ...), custom_call_target="tpu_custom_call" | custom-call | flops 8999999488 | bytes 6291456 | tf_op jit(solution)/shard_map/video_attention/pallas_call | solution.py:359
  76.2 1.4 %collective-permute-start.10 = (bf16[384,384]{1,0:T(8,128)(2,1)S(1)}, bf16[384,384]{1,0:T(8,128)(2,1)S(1)}, u32[]{:S(2)}, u32[]{:S(2)}) collective-permute-start(bf16[384,384]{1,0:T(8,128)(2,1)S(1)} %get-tuple-element.20), channel_id=1, source_target_pairs={{0,2},{2,4},{4,6},{6,8},{8,10},{10,12},{12,14},{14,0},{1,3},{3,5},... | collective-permute-start | bytes 884744 | tf_op jit(solution)/shard_map/ppermute | solution.py:595
  78.9 2.3 %video_share.1 = bf16[256,1536]{1,0:T(8,128)(2,1)S(1)} custom-call(s32[5]{0:T(128)S(1)} %copy-done.3, bf16[256,768]{1,0:T(8,128)(2,1)S(1)} %copy-done.2, bf16[768,384]{1,0:T(8,128)(2,1)S(1)} %copy-done, bf16[768,384]{1,0:T(8,128)(2,1)S(1)} %collective-permute-done.7.rest_1_, bf16[768,384]{1,0:T(8,128)(2,1)S(1)} %collective-permute-done.8.rest_2_, ...), custom_call_target="tpu_custom_call" | custom-call | flops 603979776 | bytes 4194304 | tf_op jit(solution)/shard_map/video_share/pallas_call | solution.py:467
  81.3 5.7 %collective-permute-start.13 = (bf16[256,1536]{1,0:T(8,128)(2,1)S(1)}, bf16[256,1536]{1,0:T(8,128)(2,1)S(1)}, u32[]{:S(2)}, u32[]{:S(2)}) collective-permute-start(bf16[256,1536]{1,0:T(8,128)(2,1)S(1)} %video_share.1), channel_id=1, source_target_pairs={{0,1},{1,0},{2,3},{3,2},{4,5},{5,4},{6,7},{7,6},{8,9},{9,8},{10,11... | collective-permute-start | bytes 2359304 | tf_op jit(solution)/shard_map/ppermute | solution.py:623
  87.0 1.8 %far_terms.1 = (f32[512,384]{1,0:T(8,128)S(1)}, bf16[512,384]{1,0:T(8,128)(2,1)S(1)}) custom-call(bf16[256,768]{1,0:T(8,128)(2,1)S(1)} %copy-done.2, bf16[16,96,128]{2,1,0:T(8,128)(2,1)} %all-to-all-done.2.rest_8_.parts_h, bf16[384,384]{1,0:T(8,128)(2,1)S(1)} %collective-permute-done.10.top_h, bf16[384,384]{1,0:T(8,128)(2,1)S(1)} %collective-permute-done.11.bottom_h), custom_call_target="tpu_custom_call" | custom-call | flops 301989888 | bytes 4194304 | tf_op jit(solution)/shard_map/far_terms/pallas_call | solution.py:512
  88.8 3.1 %text_share.1 = (bf16[256,768]{1,0:T(8,128)(2,1)S(1)}, bf16[256,1536]{1,0:T(8,128)(2,1)S(1)}) custom-call(s32[5]{0:T(128)S(1)} %copy-done.3, bf16[16,96,128]{2,1,0:T(8,128)(2,1)} %all-to-all-done.2.rest_8_.parts_h, bf16[768,384]{1,0:T(8,128)(2,1)S(1)} %copy-done, bf16[768,384]{1,0:T(8,128)(2,1)S(1)} %collective-permute-done.7.rest_1_, ...), custom_call_target="tpu_custom_call" | custom-call | flops 603979776 | bytes 4194304 | tf_op jit(solution)/shard_map/text_share/pallas_call | solution.py:467
  91.9 2.4 %collective-permute-start.14 = (bf16[256,1536]{1,0:T(8,128)(2,1)S(1)}, bf16[256,1536]{1,0:T(8,128)(2,1)S(1)}, u32[]{:S(2)}, u32[]{:S(2)}) collective-permute-start(bf16[256,1536]{1,0:T(8,128)(2,1)S(1)} %get-tuple-element.25), channel_id=1, source_target_pairs={{0,1},{1,0},{2,3},{3,2},{4,5},{5,4},{6,7},{7,6},{8,9},{9,8},{10,11... | collective-permute-start | bytes 2359304 | tf_op jit(solution)/shard_map/ppermute | solution.py:623
  94.4 3.0 %video_finish.1.video_in = bf16[256,1536]{1,0:T(8,128)(2,1)} custom-call(s32[5]{0:T(128)S(1)} %copy-done.3, bf16[256,768]{1,0:T(8,128)(2,1)S(1)} %copy-done.2, bf16[256,1536]{1,0:T(8,128)(2,1)S(1)} %collective-permute-done.13.other_h, bf16[768,384]{1,0:T(8,128)(2,1)S(1)} %copy-done, bf16[768,384]{1,0:T(8,128)(2,1)S(1)} %collective-permute-done.7.rest_1_, ...), custom_call_target="tpu_custom_call" | custom-call | flops 603979776 | bytes 4194304 | tf_op jit(solution)/shard_map/video_finish/pallas_call | solution.py:467
  97.5 3.0 %text_finish.1.text_in = bf16[256,1536]{1,0:T(8,128)(2,1)} custom-call(s32[5]{0:T(128)S(1)} %copy-done.3, bf16[256,768]{1,0:T(8,128)(2,1)S(1)} %get-tuple-element.24.rows_h, bf16[256,1536]{1,0:T(8,128)(2,1)S(1)} %collective-permute-done.14.other_h, bf16[768,384]{1,0:T(8,128)(2,1)S(1)} %copy-done, bf16[768,384]{1,0:T(8,128)(2,1)S(1)} %collective-permute-done.7.rest_1_, ...), custom_call_target="tpu_custom_call" | custom-call | flops 603979776 | bytes 4194304 | tf_op jit(solution)/shard_map/text_finish/pallas_call | solution.py:467
  100.5 1.6 %last_columns.1 = (bf16[256,1536]{1,0:T(8,128)(2,1)}, bf16[256,1536]{1,0:T(8,128)(2,1)}) custom-call(s32[5]{0:T(128)S(1)} %copy-done.3, f32[512,384]{1,0:T(8,128)S(1)} %get-tuple-element.22.rest_7_.terms_h, bf16[512,384]{1,0:T(8,128)(2,1)S(1)} %collective-permute-done.12.other_h, ...), custom_call_target="tpu_custom_call", output_to_operand_aliasing={{0}: (3, {}), {1}: (4, {})} | custom-call | bytes 3145728 | tf_op jit(solution)/shard_map/last_columns/pallas_call | solution.py:557
  (37 shorter events, 9.5 us)
Async XLA Ops:
  0.6 28.9 %collective-permute-start = (bf16[2,256,768]{2,1,0:T(8,128)(2,1)}, bf16[2,256,768]{2,1,0:T(8,128)(2,1)}, u32[]{:S(2)}, u32[]{:S(2)}) collective-permute-start(bf16[2,256,768]{2,1,0:T(8,128)(2,1)} %bitcast.7), channel_id=1, source_target_pairs={{0,2},{2,4},{4,6},{6,8},{8,10},{10,12},{12,14},{14,0},{1,3},{3,5},... | collective-permute-start | bytes 2359304 | tf_op jit(solution)/shard_map/ppermute | solution.py:595
  3.2 26.3 %collective-permute-start.1 = (bf16[2,256,768]{2,1,0:T(8,128)(2,1)}, bf16[2,256,768]{2,1,0:T(8,128)(2,1)}, u32[]{:S(2)}, u32[]{:S(2)}) collective-permute-start(bf16[2,256,768]{2,1,0:T(8,128)(2,1)} %bitcast.8), channel_id=1, source_target_pairs={{0,14},{2,0},{4,2},{6,4},{8,6},{10,8},{12,10},{14,12},{1,15},{3,1}... | collective-permute-start | bytes 2359304 | tf_op jit(solution)/shard_map/ppermute | solution.py:595
  7.9 21.6 %copy-start.4 = (bf16[2,8,4,8,768]{4,3,2,1,0:T(8,128)(2,1)S(1)}, bf16[2,8,4,8,768]{4,3,2,1,0:T(8,128)(2,1)}, u32[]{:S(2)}) copy-start(bf16[2,8,4,8,768]{4,3,2,1,0:T(8,128)(2,1)} %param.9) | copy-start | bytes 2359300
  13.1 16.4 %all-to-all-start = ((bf16[16,112,128]{2,1,0:T(8,128)(2,1)}), bf16[16,112,128]{2,1,0:T(8,128)(2,1)S(1)}, u32[]{:S(2)}, u32[]{:S(2)}) async-start(bf16[16,112,128]{2,1,0:T(8,128)(2,1)} %get-tuple-element.15), calls=%async_computation | async-start | bytes 917504 | tf_op jit(solution)/shard_map/all_to_all | solution.py:603
  19.9 22.6 %collective-permute-start.4 = (bf16[768,384]{1,0:T(8,128)(2,1)}, bf16[768,384]{1,0:T(8,128)(2,1)S(1)}, u32[]{:S(2)}, u32[]{:S(2)}) collective-permute-start(bf16[768,384]{1,0:T(8,128)(2,1)} %get-tuple-element.19), channel_id=1, source_target_pairs={{0,2},{2,4},{4,6},{6,8},{8,10},{10,12},{12,14},{14,0},{1,3},{3,5},... | collective-permute-start | bytes 1769480 | tf_op jit(solution)/shard_map/ppermute | solution.py:595
  20.0 24.1 %collective-permute-start.7 = (bf16[768,384]{1,0:T(8,128)(2,1)}, bf16[768,384]{1,0:T(8,128)(2,1)S(1)}, u32[]{:S(2)}, u32[]{:S(2)}) collective-permute-start(bf16[768,384]{1,0:T(8,128)(2,1)} %get-tuple-element.19), channel_id=1, source_target_pairs={{0,14},{2,0},{4,2},{6,4},{8,6},{10,8},{12,10},{14,12},{1,15},{3,1}... | collective-permute-start | bytes 1769480 | tf_op jit(solution)/shard_map/ppermute | solution.py:595
  32.8 32.9 %collective-permute-start.2 = (bf16[3,2,128,768]{3,2,1,0:T(8,128)(2,1)}, bf16[3,2,128,768]{3,2,1,0:T(8,128)(2,1)}, u32[]{:S(2)}, u32[]{:S(2)}) collective-permute-start(bf16[3,2,128,768]{3,2,1,0:T(8,128)(2,1)} %get-tuple-element.16), channel_id=1, source_target_pairs={{0,16},{16,32},{32,48},{48,64},{64,80},{80,96},{96,112},{112,128},... | collective-permute-start | bytes 3538952 | tf_op jit(solution)/shard_map/ppermute | solution.py:595
  33.3 32.3 %collective-permute-start.3 = (bf16[3,2,128,768]{3,2,1,0:T(8,128)(2,1)}, bf16[3,2,128,768]{3,2,1,0:T(8,128)(2,1)}, u32[]{:S(2)}, u32[]{:S(2)}) collective-permute-start(bf16[3,2,128,768]{3,2,1,0:T(8,128)(2,1)} %get-tuple-element.17), channel_id=1, source_target_pairs={{0,240},{16,0},{32,16},{48,32},{64,48},{80,64},{96,80},{112,96},{1... | collective-permute-start | bytes 3538952 | tf_op jit(solution)/shard_map/ppermute | solution.py:595
  37.6 14.0 %all-to-all-start.1 = ((bf16[8,112,128]{2,1,0:T(8,128)(2,1)}), bf16[8,112,128]{2,1,0:T(8,128)(2,1)S(1)}, u32[]{:S(2)}, u32[]{:S(2)}) async-start(bf16[8,112,128]{2,1,0:T(8,128)(2,1)} %get-tuple-element.18), calls=%async_computation.1 | async-start | bytes 458752 | tf_op jit(solution)/shard_map/all_to_all | solution.py:607
  42.5 14.4 %copy-start.5 = (s32[2,1,2,27]{3,2,1,0:T(2,128)S(1)}, s32[2,1,2,27]{3,2,1,0:T(2,128)}, u32[]{:S(2)}) copy-start(s32[2,1,2,27]{3,2,1,0:T(2,128)} %param.13) | copy-start | bytes 1300
  42.5 19.2 %collective-permute-start.5 = (bf16[768,384]{1,0:T(8,128)(2,1)S(1)}, bf16[768,384]{1,0:T(8,128)(2,1)S(1)}, u32[]{:S(2)}, u32[]{:S(2)}) collective-permute-start(bf16[768,384]{1,0:T(8,128)(2,1)S(1)} %collective-permute-done.4.rest_6_), channel_id=1, source_target_pairs={{0,2},{2,4},{4,6},{6,8},{8,10},{10,12},{12,14},{14,0},{1,3},{3,5},... | collective-permute-start | bytes 1769480 | tf_op jit(solution)/shard_map/ppermute | solution.py:595
  44.1 17.7 %collective-permute-start.8 = (bf16[768,384]{1,0:T(8,128)(2,1)S(1)}, bf16[768,384]{1,0:T(8,128)(2,1)S(1)}, u32[]{:S(2)}, u32[]{:S(2)}) collective-permute-start(bf16[768,384]{1,0:T(8,128)(2,1)S(1)} %collective-permute-done.7.rest_1_), channel_id=1, source_target_pairs={{0,14},{2,0},{4,2},{6,4},{8,6},{10,8},{12,10},{14,12},{1,15},{3,1}... | collective-permute-start | bytes 1769480 | tf_op jit(solution)/shard_map/ppermute | solution.py:595
  52.7 12.9 %all-to-all-start.2 = ((bf16[16,96,128]{2,1,0:T(8,128)(2,1)}), bf16[16,96,128]{2,1,0:T(8,128)(2,1)}, u32[]{:S(2)}, u32[]{:S(2)}) async-start(bf16[16,96,128]{2,1,0:T(8,128)(2,1)} %text_finish_sums.1), calls=%async_computation.2 | async-start | bytes 786432 | tf_op jit(solution)/shard_map/all_to_all | solution.py:612
  61.7 13.2 %collective-permute-start.6 = (bf16[768,384]{1,0:T(8,128)(2,1)S(1)}, bf16[768,384]{1,0:T(8,128)(2,1)S(1)}, u32[]{:S(2)}, u32[]{:S(2)}) collective-permute-start(bf16[768,384]{1,0:T(8,128)(2,1)S(1)} %collective-permute-done.5.rest_5_), channel_id=1, source_target_pairs={{0,2},{2,4},{4,6},{6,8},{8,10},{10,12},{12,14},{14,0},{1,3},{3,5},... | collective-permute-start | bytes 1769480 | tf_op jit(solution)/shard_map/ppermute | solution.py:595
  61.7 13.2 %collective-permute-start.9 = (bf16[768,384]{1,0:T(8,128)(2,1)S(1)}, bf16[768,384]{1,0:T(8,128)(2,1)S(1)}, u32[]{:S(2)}, u32[]{:S(2)}) collective-permute-start(bf16[768,384]{1,0:T(8,128)(2,1)S(1)} %collective-permute-done.8.rest_2_), channel_id=1, source_target_pairs={{0,14},{2,0},{4,2},{6,4},{8,6},{10,8},{12,10},{14,12},{1,15},{3,1}... | collective-permute-start | bytes 1769480 | tf_op jit(solution)/shard_map/ppermute | solution.py:595
  65.6 13.3 %copy-start.3 = (s32[5]{0:T(128)S(1)}, s32[5]{0:T(128)}, u32[]{:S(2)}) copy-start(s32[5]{0:T(128)} %stack.15.pos) | copy-start | bytes 64
  73.6 5.4 %copy-start = (bf16[768,384]{1,0:T(8,128)(2,1)S(1)}, bf16[768,384]{1,0:T(8,128)(2,1)}, u32[]{:S(2)}) copy-start(bf16[768,384]{1,0:T(8,128)(2,1)} %rest_0_.7) | copy-start | bytes 1769476
  74.9 1.0 copy-start.1
  75.9 3.0 %copy-start.2 = (bf16[256,768]{1,0:T(8,128)(2,1)S(1)}, bf16[256,768]{1,0:T(8,128)(2,1)}, u32[]{:S(2)}) copy-start(bf16[256,768]{1,0:T(8,128)(2,1)} %video_attention.1.after.video_h.rows_h) | copy-start | bytes 1179652
  76.2 10.8 %collective-permute-start.10 = (bf16[384,384]{1,0:T(8,128)(2,1)S(1)}, bf16[384,384]{1,0:T(8,128)(2,1)S(1)}, u32[]{:S(2)}, u32[]{:S(2)}) collective-permute-start(bf16[384,384]{1,0:T(8,128)(2,1)S(1)} %get-tuple-element.20), channel_id=1, source_target_pairs={{0,2},{2,4},{4,6},{6,8},{8,10},{10,12},{12,14},{14,0},{1,3},{3,5},... | collective-permute-start | bytes 884744 | tf_op jit(solution)/shard_map/ppermute | solution.py:595
  77.6 9.5 %collective-permute-start.11 = (bf16[384,384]{1,0:T(8,128)(2,1)S(1)}, bf16[384,384]{1,0:T(8,128)(2,1)S(1)}, u32[]{:S(2)}, u32[]{:S(2)}) collective-permute-start(bf16[384,384]{1,0:T(8,128)(2,1)S(1)} %get-tuple-element.21), channel_id=1, source_target_pairs={{0,14},{2,0},{4,2},{6,4},{8,6},{10,8},{12,10},{14,12},{1,15},{3,1}... | collective-permute-start | bytes 884744 | tf_op jit(solution)/shard_map/ppermute | solution.py:595
  81.3 13.1 %collective-permute-start.13 = (bf16[256,1536]{1,0:T(8,128)(2,1)S(1)}, bf16[256,1536]{1,0:T(8,128)(2,1)S(1)}, u32[]{:S(2)}, u32[]{:S(2)}) collective-permute-start(bf16[256,1536]{1,0:T(8,128)(2,1)S(1)} %video_share.1), channel_id=1, source_target_pairs={{0,1},{1,0},{2,3},{3,2},{4,5},{5,4},{6,7},{7,6},{8,9},{9,8},{10,11... | collective-permute-start | bytes 2359304 | tf_op jit(solution)/shard_map/ppermute | solution.py:623
  91.9 5.5 %collective-permute-start.14 = (bf16[256,1536]{1,0:T(8,128)(2,1)S(1)}, bf16[256,1536]{1,0:T(8,128)(2,1)S(1)}, u32[]{:S(2)}, u32[]{:S(2)}) collective-permute-start(bf16[256,1536]{1,0:T(8,128)(2,1)S(1)} %get-tuple-element.25), channel_id=1, source_target_pairs={{0,1},{1,0},{2,3},{3,2},{4,5},{5,4},{6,7},{7,6},{8,9},{9,8},{10,11... | collective-permute-start | bytes 2359304 | tf_op jit(solution)/shard_map/ppermute | solution.py:623
  94.3 6.2 %collective-permute-start.12 = (bf16[512,384]{1,0:T(8,128)(2,1)S(1)}, bf16[512,384]{1,0:T(8,128)(2,1)S(1)}, u32[]{:S(2)}, u32[]{:S(2)}) collective-permute-start(bf16[512,384]{1,0:T(8,128)(2,1)S(1)} %get-tuple-element.23), channel_id=1, source_target_pairs={{0,1},{1,0},{2,3},{3,2},{4,5},{5,4},{6,7},{7,6},{8,9},{9,8},{10,11... | collective-permute-start | bytes 1179656 | tf_op jit(solution)/shard_map/ppermute | solution.py:623

commit v5 on v4

--- a/solution.py
+++ b/solution.py
@@ -413,18 +413,32 @@
 
 
 def text_share_kernel(pos, parts_h, *rest):
-    blocks, rest = rest[:7], rest[8:]
-    rows_h, share, parts, rows, in_sems, held, sent, sems, out_sems = rest
+    blocks, (video_h, top_h, bottom_h), rest = rest[:7], rest[7:10], rest[10:]
+    rows_h, share, terms, far_share, parts, rows, video, w, far_sems, in_sems, *others = rest
+    half = top_h.shape[0]
     rows_copy = pltpu.make_async_copy(rows, rows_h, in_sems.at[1])
     copy = pltpu.make_async_copy(parts_h, parts, in_sems.at[0])
     copy.start()
+    copies = [
+        pltpu.make_async_copy(video_h, video, far_sems.at[0]),
+        pltpu.make_async_copy(top_h, w.at[0:half], far_sems.at[1]),
+        pltpu.make_async_copy(bottom_h, w.at[half : 2 * half], far_sems.at[2]),
+    ]
+    for each in copies:
+        each.start()
 
     def read():
         copy.wait()
         rows[...] = by_head(parts[...])
         rows_copy.start()
+        wait_all(copies)
+        for at, left in enumerate((video, rows)):
+            part = slice(at * OWN, (at + 1) * OWN)
+            terms[part, :] = dot(left[...], w[...])
+            far_share[part, :] = terms[part, :].astype(BF)
         return rows[...]
 
+    held, sent, sems, out_sems = others
     project(pos, blocks, False, held, sems, read, lambda _, x: x, share, sent, out_sems)
     rows_copy.wait()
 
@@ -462,13 +476,14 @@
     project(pos, blocks, True, held, sems, read, put, out, sent, out_sems)
 
 
-def project_call(kernel, name, pos, left, blocks, out_shape, out_specs, scratch, after=()):
+def project_call(kernel, name, pos, left, blocks, out_shape, out_specs, scratch, after=(), aliases=None):
     depth, width = blocks[0].shape
     return pl.pallas_call(
         kernel,
         in_specs=[SCALARS] + [FAR] + [ANY] * (len(left) - 1) + [FAR] * 7 + [ANY] * len(after),
         out_specs=out_specs,
         out_shape=out_shape,
+        input_output_aliases=aliases or {},
         scratch_shapes=[pltpu.VMEM(x.shape, BF) for x in left]
         + scratch
         + [
@@ -486,90 +501,36 @@
     )(pos, *left, *blocks, *after)
 
 
-def far_kernel(video_h, parts_h, top_h, bottom_h, terms, share, rows, parts, w, sems):
-    half = top_h.shape[0]
-    copies = [
-        pltpu.make_async_copy(source, target, sems.at[i])
-        for i, (source, target) in enumerate(
-            (
-                (video_h, rows.at[0:OWN]),
-                (parts_h, parts),
-                (top_h, w.at[0:half]),
-                (bottom_h, w.at[half : 2 * half]),
-            )
-        )
-    ]
-    for copy in copies:
-        copy.start()
-    wait_all(copies)
-    rows[OWN : OWN + TEXT] = by_head(parts[...])
-    terms[...] = dot(rows[...], w[...])
-    share[...] = terms[...].astype(BF)
-
-
-def far_terms(video, parts, top, bottom):
-    shape, depth, width = (OWN + TEXT, top.shape[1]), 2 * top.shape[0], top.shape[1]
-    return pl.pallas_call(
-        far_kernel,
-        in_specs=[ANY] * 4,
-        out_specs=(WHOLE, WHOLE),
-        out_shape=(jax.ShapeDtypeStruct(shape, F32), jax.ShapeDtypeStruct(shape, BF)),
-        scratch_shapes=[
-            pltpu.VMEM((OWN + TEXT, depth), BF),
-            pltpu.VMEM(parts.shape, BF),
-            pltpu.VMEM((depth, width), BF),
-            pltpu.SemaphoreType.DMA((4,)),
-        ],
-        cost_estimate=pl.CostEstimate(
-            flops=2 * shape[0] * depth * width, bytes_accessed=4 << 20, transcendentals=0
-        ),
-        compiler_params=pltpu.CompilerParams(vmem_limit_bytes=24 << 20),
-        name="far_terms",
-    )(video, parts, top, bottom)
-
-
-def last_kernel(pos, terms_h, other_h, video_in, text_in, video, text, terms, other, done, sems):
+def text_finish_kernel(pos, rows_h, other_h, *rest):
+    blocks, (terms_h, far_h, _, out, video), rest = rest[:7], rest[7:12], rest[12:]
+    rows, other, terms, far, done, far_sems, *others = rest
     width = terms.shape[1]
     column = jnp.bitwise_and(pos[1] + 4, 7)
-    slot = jnp.bitwise_and(column, 3)
-    columns = pl.ds(pl.multiple_of(slot * width, width), width)
-
-    @pl.when(lax.shift_right_logical(column, 2) == pos[2])
+    columns = pl.ds(pl.multiple_of(jnp.bitwise_and(column, 3) * width, width), width)
+    is_mine = lax.shift_right_logical(column, 2) == pos[2]
+    inward = [
+        pltpu.make_async_copy(terms_h, terms, far_sems.at[0]),
+        pltpu.make_async_copy(far_h, far, far_sems.at[1]),
+    ]
+    outward = [
+        pltpu.make_async_copy(done.at[0:OWN], video.at[:, columns], far_sems.at[2]),
+        pltpu.make_async_copy(done.at[OWN : OWN + TEXT], out.at[:, columns], far_sems.at[3]),
+    ]
+
+    @pl.when(is_mine)
     def _():
-        copies = [
-            pltpu.make_async_copy(terms_h, terms, sems.at[0]),
-            pltpu.make_async_copy(other_h, other, sems.at[1]),
-        ]
-        for copy in copies:
+        for copy in inward:
             copy.start()
-        wait_all(copies)
-        done[...] = (terms[...] + other[...].astype(F32)).astype(BF)
-        copies = [
-            pltpu.make_async_copy(done.at[0:OWN], video.at[:, columns], sems.at[2]),
-            pltpu.make_async_copy(done.at[OWN : OWN + TEXT], text.at[:, columns], sems.at[3]),
-        ]
-        for copy in copies:
+
+    finish_kernel(pos, rows_h, other_h, *blocks, out, rows, other, *others)
+
+    @pl.when(is_mine)
+    def _():
+        wait_all(inward)
+        done[...] = (terms[...] + far[...].astype(F32)).astype(BF)
+        for copy in outward:
             copy.start()
-        wait_all(copies)
-
-
-def last_columns(pos, terms, other, video, text):
-    return pl.pallas_call(
-        last_kernel,
-        in_specs=[SCALARS] + [ANY] * 4,
-        out_specs=(ANY, ANY),
-        out_shape=[jax.ShapeDtypeStruct(x.shape, BF) for x in (video, text)],
-        input_output_aliases={3: 0, 4: 1},
-        scratch_shapes=[
-            pltpu.VMEM(terms.shape, F32),
-            pltpu.VMEM(terms.shape, BF),
-            pltpu.VMEM(terms.shape, BF),
-            pltpu.SemaphoreType.DMA((4,)),
-        ],
-        cost_estimate=pl.CostEstimate(flops=0, bytes_accessed=3 << 20, transcendentals=0),
-        compiler_params=pltpu.CompilerParams(vmem_limit_bytes=24 << 20),
-        name="last_columns",
-    )(pos, terms, other, video, text)
+        wait_all(outward)
 
 
 def shards(video_q, video_kv, text_q, text_k, text_v, tile_mask, text_valid, w_out):
@@ -627,26 +588,44 @@
     video_other = swap(
         project_call(share_kernel, "video_share", pos, [video_rows], blocks, full, FAR, [])
     )
-    terms, share = far_terms(video_rows, parts, *far)
-    text_rows, text_other = project_call(
+    far_shape = (OWN + TEXT, w_out.shape[1])
+    text_rows, text_other, terms, share = project_call(
         text_share_kernel,
         "text_share",
         pos,
         [parts],
         blocks,
-        (jax.ShapeDtypeStruct((TEXT, WIDTH), BF), full),
-        (FAR, FAR),
-        [pltpu.VMEM((TEXT, WIDTH), BF)],
-        [terms],
+        (
+            jax.ShapeDtypeStruct((TEXT, WIDTH), BF),
+            full,
+            jax.ShapeDtypeStruct(far_shape, F32),
+            jax.ShapeDtypeStruct(far_shape, BF),
+        ),
+        (FAR, FAR, WHOLE, WHOLE),
+        [
+            pltpu.VMEM((TEXT, WIDTH), BF),
+            pltpu.VMEM((OWN, WIDTH), BF),
+            pltpu.VMEM(w_out.shape, BF),
+            pltpu.SemaphoreType.DMA((3,)),
+        ],
+        [video_rows, *far],
     )
     text_other = swap(text_other)
     video_out = project_call(
         finish_kernel, "video_finish", pos, [video_rows, video_other], blocks, full, FAR, []
     )
-    text_out = project_call(
-        finish_kernel, "text_finish", pos, [text_rows, text_other], blocks, full, FAR, []
+    text_out, video_out = project_call(
+        text_finish_kernel,
+        "text_finish",
+        pos,
+        [text_rows, text_other],
+        blocks,
+        (full, full),
+        (FAR, ANY),
+        [pltpu.VMEM(terms.shape, t) for t in (F32, BF, BF)] + [pltpu.SemaphoreType.DMA((4,))],
+        [terms, swap(share), video_out],
+        {12: 1},
     )
-    video_out, text_out = last_columns(pos, terms, swap(share), video_out, text_out)
     return video_out.reshape(frames, rows, cols, -1), text_out
 
 

time: 103 us -> 101 us (0.981)
  starting transfers between devices: 46.6 us -> 43.6 us
  waiting for transfers between devices: 19.8 us -> 22.8 us
  Pallas kernels: 32.7 us -> 31 us
    pallas_call x2 -> x0, Pallas kernels: 3.43 us -> none  [the longest x1 1.78 us: far_terms(): pl.pallas_call(far_kernel, in_specs=[ANY] * 4, out_specs=(WHOLE, WHOLE),...]
    pallas_call x4, Pallas kernels: 11.5 us -> 13.2 us  [project_call(): pl.pallas_call(kernel, in_specs=[SCALARS] + [FAR] + [ANY] * (len(left) -...]
    ppermute x12, starting transfers between devices: 22.5 us -> 20.9 us  [up(): return lax.ppermute(x, axis, [(i, (i + by) % n) for i in range(n)])]
    ppermute x3, starting transfers between devices: 8.24 us -> 6.75 us  [swap(): return lax.ppermute(x, 'head', [(0, 1), (1, 0)])]
    all_to_all x1, waiting for transfers between devices: 1.19 us -> 2.63 us  [shards(): parts = lax.all_to_all(sums, 'tm', 0, 0, tiled=True)]
    all_to_all x1, waiting for transfers between devices: 6.83 us -> 8.04 us  [shards(): parts = lax.all_to_all(parts, 'tm', 0, 0, tiled=True)]
  transfers between devices with their start and end apart: 18 -> 18, of which waited for: 5 -> 5; matrix products, arithmetic and copies ran while one was open for 1% -> 1% of each run, Pallas kernels for 30% -> 26%
where the time goes in v5:
time: 101 us; the launch traced here: 100 us
  starting transfers between devices  43.6 us (43%)
  Pallas kernels  31 us (31%)
  waiting for transfers between devices  22.8 us (23%)
  local copies, waits for them, and re-layouts  2.18 us (2%)
    ppermute x12, starting transfers between devices, up(): return lax.ppermute(x, axis, [(i, (i + by) % n) for i in range(n)])  20.9 us
    pallas_call x4, Pallas kernels, project_call(): pl.pallas_call(kernel, in_specs=[SCALARS] + [FAR] + [ANY] * (len(left) -...  13.2 us
    all_to_all x1, waiting for transfers between devices, shards(): parts = lax.all_to_all(parts, 'tm', 0, 0, tiled=True)  8.04 us
    pallas_call x1, Pallas kernels, video_attention(): pl.pallas_call(video_kernel, in_specs=[SCALARS, SCALARS, WHOLE] + [FAR] *...  7.97 us
    all_to_all x1, starting transfers between devices, shards(): parts = lax.all_to_all(parts, 'tm', 0, 0, tiled=True)  6.76 us
    ppermute x3, starting transfers between devices, swap(): return lax.ppermute(x, 'head', [(0, 1), (1, 0)])  6.75 us
    all_to_all x1, waiting for transfers between devices, shards(): parts = lax.all_to_all(parts, 'height', 0, 0, tiled=True)  6.32 us
    ppermute x12, waiting for transfers between devices, up(): return lax.ppermute(x, axis, [(i, (i + by) % n) for i in range(n)])  5.77 us
  transfers between devices with their start and end apart: 18, of which 5 were waited for; matrix products, arithmetic and copies ran while one was open for 1% of the time, Pallas kernels for 26%

profile of v5, /device:TPU:1, one launch (start us, length us, event | category | flops | bytes accessed | tf_op | source)
XLA Modules:
  0.0 100.5 jit_solution(13529940009839952972)
XLA Ops:
  0.6 2.5 %collective-permute-start = (bf16[2,256,768]{2,1,0:T(8,128)(2,1)}, bf16[2,256,768]{2,1,0:T(8,128)(2,1)}, u32[]{:S(2)}, u32[]{:S(2)}) collective-permute-start(bf16[2,256,768]{2,1,0:T(8,128)(2,1)} %bitcast.7), channel_id=1, source_target_pairs={{0,2},{2,4},{4,6},{6,8},{8,10},{10,12},{12,14},{14,0},{1,3},{3,5},... | collective-permute-start | bytes 2359304 | tf_op jit(solution)/shard_map/ppermute | solution.py:556
  3.2 4.0 %collective-permute-start.1 = (bf16[2,256,768]{2,1,0:T(8,128)(2,1)}, bf16[2,256,768]{2,1,0:T(8,128)(2,1)}, u32[]{:S(2)}, u32[]{:S(2)}) collective-permute-start(bf16[2,256,768]{2,1,0:T(8,128)(2,1)} %bitcast.8), channel_id=1, source_target_pairs={{0,14},{2,0},{4,2},{6,4},{8,6},{10,8},{12,10},{14,12},{1,15},{3,1}... | collective-permute-start | bytes 2359304 | tf_op jit(solution)/shard_map/ppermute | solution.py:556
  7.8 5.3 %text_part.1 = (bf16[16,112,128]{2,1,0:T(8,128)(2,1)}, bf16[768,384]{1,0:T(8,128)(2,1)}) custom-call(s32[5]{0:T(128)} %stack.15.pos, s32[1,256]{1,0:T(1,128)} %bitcast.14, bf16[256,768]{1,0:T(8,128)(2,1)} %tq_h.1, bf16[2,256,768]{2,1,0:T(8,128)(2,1)} %bitcast.9, bf16[256,768]{1,0:T(8,128)(2,1)} %rest_1_.1, bf16[256,768]{1,0:T(8,128)(2,1)} %rest_2_.1, ...), custom_call_target="tpu_custom_call" | custom-call | flops 5000000000 | bytes 2097152 | tf_op jit(solution)/shard_map/text_part/pallas_call | solution.py:121
  13.0 6.8 %all-to-all-start = ((bf16[16,112,128]{2,1,0:T(8,128)(2,1)}), bf16[16,112,128]{2,1,0:T(8,128)(2,1)S(1)}, u32[]{:S(2)}, u32[]{:S(2)}) async-start(bf16[16,112,128]{2,1,0:T(8,128)(2,1)} %get-tuple-element.15), calls=%async_computation | async-start | bytes 917504 | tf_op jit(solution)/shard_map/all_to_all | solution.py:564
  19.8 1.4 %collective-permute-start.2 = (bf16[768,384]{1,0:T(8,128)(2,1)}, bf16[768,384]{1,0:T(8,128)(2,1)S(1)}, u32[]{:S(2)}, u32[]{:S(2)}) collective-permute-start(bf16[768,384]{1,0:T(8,128)(2,1)} %get-tuple-element.17), channel_id=1, source_target_pairs={{0,14},{2,0},{4,2},{6,4},{8,6},{10,8},{12,10},{14,12},{1,15},{3,1}... | collective-permute-start | bytes 1769480 | tf_op jit(solution)/shard_map/ppermute | solution.py:556
  21.4 8.0 %all-to-all-done.parts = bf16[16,112,128]{2,1,0:T(8,128)(2,1)S(1)} async-done(((bf16[16,112,128]{2,1,0:T(8,128)(2,1)}), bf16[16,112,128]{2,1,0:T(8,128)(2,1)S(1)}, u32[]{:S(2)}, u32[]{:S(2)}) %all-to-all-start) | async-done | bytes 458784 | tf_op jit(solution)/shard_map/all_to_all | solution.py:564
  29.4 3.2 %text_merge.1 = (bf16[8,112,128]{2,1,0:T(8,128)(2,1)}, bf16[3,2,128,768]{3,2,1,0:T(8,128)(2,1)}, bf16[3,2,128,768]{3,2,1,0:T(8,128)(2,1)}) custom-call(bf16[16,112,128]{2,1,0:T(8,128)(2,1)S(1)} %all-to-all-done.parts, bf16[2,256,768]{2,1,0:T(8,128)(2,1)S(1)} %bitcast.11, bf16[2,256,768]{2,1,0:T(8,128)(2,1)} %collective-permute-done.z_low.rest_4_, ...), custom_call_target="tpu_custom_call" | custom-call | flops 2000000000 | bytes 6291456 | tf_op jit(solution)/shard_map/text_merge/pallas_call | solution.py:163
  33.2 4.3 %collective-permute-start.9 = (bf16[3,2,128,768]{3,2,1,0:T(8,128)(2,1)}, bf16[3,2,128,768]{3,2,1,0:T(8,128)(2,1)}, u32[]{:S(2)}, u32[]{:S(2)}) collective-permute-start(bf16[3,2,128,768]{3,2,1,0:T(8,128)(2,1)} %get-tuple-element.19), channel_id=1, source_target_pairs={{0,240},{16,0},{32,16},{48,32},{64,48},{80,64},{96,80},{112,96},{1... | collective-permute-start | bytes 3538952 | tf_op jit(solution)/shard_map/ppermute | solution.py:556
  37.5 4.9 %all-to-all-start.1 = ((bf16[8,112,128]{2,1,0:T(8,128)(2,1)}), bf16[8,112,128]{2,1,0:T(8,128)(2,1)S(1)}, u32[]{:S(2)}, u32[]{:S(2)}) async-start(bf16[8,112,128]{2,1,0:T(8,128)(2,1)} %get-tuple-element.16), calls=%async_computation.1 | async-start | bytes 458752 | tf_op jit(solution)/shard_map/all_to_all | solution.py:568
  42.5 2.7 %collective-permute-start.3 = (bf16[768,384]{1,0:T(8,128)(2,1)S(1)}, bf16[768,384]{1,0:T(8,128)(2,1)S(1)}, u32[]{:S(2)}, u32[]{:S(2)}) collective-permute-start(bf16[768,384]{1,0:T(8,128)(2,1)S(1)} %collective-permute-done.2.rest_1_), channel_id=1, source_target_pairs={{0,14},{2,0},{4,2},{6,4},{8,6},{10,8},{12,10},{14,12},{1,15},{3,1}... | collective-permute-start | bytes 1769480 | tf_op jit(solution)/shard_map/ppermute | solution.py:556
  45.2 6.3 %all-to-all-done.1.refs_0_ = bf16[8,112,128]{2,1,0:T(8,128)(2,1)S(1)} async-done(((bf16[8,112,128]{2,1,0:T(8,128)(2,1)}), bf16[8,112,128]{2,1,0:T(8,128)(2,1)S(1)}, u32[]{:S(2)}, u32[]{:S(2)}) %all-to-all-start.1) | async-done | bytes 229408 | tf_op jit(solution)/shard_map/all_to_all | solution.py:568
  52.6 4.2 %all-to-all-start.2 = ((bf16[16,96,128]{2,1,0:T(8,128)(2,1)}), bf16[16,96,128]{2,1,0:T(8,128)(2,1)}, u32[]{:S(2)}, u32[]{:S(2)}) async-start(bf16[16,96,128]{2,1,0:T(8,128)(2,1)} %text_finish_sums.1), calls=%async_computation.2 | async-start | bytes 786432 | tf_op jit(solution)/shard_map/all_to_all | solution.py:573
  57.4 3.0 %collective-permute-done.3.rest_2_ = bf16[768,384]{1,0:T(8,128)(2,1)S(1)} collective-permute-done((bf16[768,384]{1,0:T(8,128)(2,1)S(1)}, bf16[768,384]{1,0:T(8,128)(2,1)S(1)}, u32[]{:S(2)}, u32[]{:S(2)}) %collective-permute-start.3) | collective-permute-done | bytes 589856 | tf_op jit(solution)/shard_map/ppermute | solution.py:556
  60.4 2.4 %collective-permute-start.4 = (bf16[768,384]{1,0:T(8,128)(2,1)S(1)}, bf16[768,384]{1,0:T(8,128)(2,1)S(1)}, u32[]{:S(2)}, u32[]{:S(2)}) collective-permute-start(bf16[768,384]{1,0:T(8,128)(2,1)S(1)} %collective-permute-done.3.rest_2_), channel_id=1, source_target_pairs={{0,14},{2,0},{4,2},{6,4},{8,6},{10,8},{12,10},{14,12},{1,15},{3,1}... | collective-permute-start | bytes 1769480 | tf_op jit(solution)/shard_map/ppermute | solution.py:556
  62.9 2.6 %all-to-all-done.2.rest_8_.parts_h = bf16[16,96,128]{2,1,0:T(8,128)(2,1)} async-done(((bf16[16,96,128]{2,1,0:T(8,128)(2,1)}), bf16[16,96,128]{2,1,0:T(8,128)(2,1)}, u32[]{:S(2)}, u32[]{:S(2)}) %all-to-all-start.2) | async-done | bytes 393248 | tf_op jit(solution)/shard_map/all_to_all | solution.py:573
  65.5 8.0 %video_attention.1.after.rest_7_.rows_h = bf16[256,768]{1,0:T(8,128)(2,1)} custom-call(s32[5]{0:T(128)} %stack.15.pos, s32[108]{0:T(128)} %reshape.21.mask, s32[1,256]{1,0:T(1,128)} %bitcast.15, bf16[256,768]{1,0:T(8,128)(2,1)} %bitcast.13, bf16[256,768]{1,0:T(8,128)(2,1)} %rest_1_.1, bf16[256,768]{1,0:T(8,128)(2,1)} %rest_2_.1, ...), custom_call_target="tpu_custom_call" | custom-call | flops 8999999488 | bytes 6291456 | tf_op jit(solution)/shard_map/video_attention/pallas_call | solution.py:359
  73.5 2.8 %collective-permute-done.7.low.rest_4_ = bf16[768,384]{1,0:T(8,128)(2,1)S(1)} collective-permute-done((bf16[768,384]{1,0:T(8,128)(2,1)S(1)}, bf16[768,384]{1,0:T(8,128)(2,1)S(1)}, u32[]{:S(2)}, u32[]{:S(2)}) %collective-permute-start.7) | collective-permute-done | bytes 589856 | tf_op jit(solution)/shard_map/ppermute | solution.py:556
  77.7 2.7 %collective-permute-start.11 = (bf16[384,384]{1,0:T(8,128)(2,1)S(1)}, bf16[384,384]{1,0:T(8,128)(2,1)S(1)}, u32[]{:S(2)}, u32[]{:S(2)}) collective-permute-start(bf16[384,384]{1,0:T(8,128)(2,1)S(1)} %get-tuple-element.21), channel_id=1, source_target_pairs={{0,14},{2,0},{4,2},{6,4},{8,6},{10,8},{12,10},{14,12},{1,15},{3,1}... | collective-permute-start | bytes 884744 | tf_op jit(solution)/shard_map/ppermute | solution.py:556
  80.3 2.3 %video_share.1 = bf16[256,1536]{1,0:T(8,128)(2,1)S(1)} custom-call(s32[5]{0:T(128)S(1)} %copy-done.3, bf16[256,768]{1,0:T(8,128)(2,1)S(1)} %copy-done.2, bf16[768,384]{1,0:T(8,128)(2,1)S(1)} %copy-done, bf16[768,384]{1,0:T(8,128)(2,1)S(1)} %collective-permute-done.2.rest_1_, bf16[768,384]{1,0:T(8,128)(2,1)S(1)} %collective-permute-done.3.rest_2_, ...), custom_call_target="tpu_custom_call" | custom-call | flops 603979776 | bytes 4194304 | tf_op jit(solution)/shard_map/video_share/pallas_call | solution.py:481
  82.7 4.3 %collective-permute-start.14 = (bf16[256,1536]{1,0:T(8,128)(2,1)S(1)}, bf16[256,1536]{1,0:T(8,128)(2,1)S(1)}, u32[]{:S(2)}, u32[]{:S(2)}) collective-permute-start(bf16[256,1536]{1,0:T(8,128)(2,1)S(1)} %video_share.1), channel_id=1, source_target_pairs={{0,1},{1,0},{2,3},{3,2},{4,5},{5,4},{6,7},{7,6},{8,9},{9,8},{10,11... | collective-permute-start | bytes 2359304 | tf_op jit(solution)/shard_map/ppermute | solution.py:584
  86.9 3.7 %text_share.1 = (bf16[256,768]{1,0:T(8,128)(2,1)S(1)}, bf16[256,1536]{1,0:T(8,128)(2,1)S(1)}, f32[512,384]{1,0:T(8,128)S(1)}, bf16[512,384]{1,0:T(8,128)(2,1)S(1)}) custom-call(s32[5]{0:T(128)S(1)} %copy-done.3, bf16[16,96,128]{2,1,0:T(8,128)(2,1)} %all-to-all-done.2.rest_8_.parts_h, bf16[768,384]{1,0:T(8,128)(2,1)S(1)} %copy-done, ...), custom_call_target="tpu_custom_call" | custom-call | flops 603979776 | bytes 4194304 | tf_op jit(solution)/shard_map/text_share/pallas_call | solution.py:481
  90.6 2.4 %collective-permute-start.12 = (bf16[256,1536]{1,0:T(8,128)(2,1)S(1)}, bf16[256,1536]{1,0:T(8,128)(2,1)S(1)}, u32[]{:S(2)}, u32[]{:S(2)}) collective-permute-start(bf16[256,1536]{1,0:T(8,128)(2,1)S(1)} %get-tuple-element.23), channel_id=1, source_target_pairs={{0,1},{1,0},{2,3},{3,2},{4,5},{5,4},{6,7},{7,6},{8,9},{9,8},{10,11... | collective-permute-start | bytes 2359304 | tf_op jit(solution)/shard_map/ppermute | solution.py:584
  93.1 3.0 %video_finish.1.rest_9_ = bf16[256,1536]{1,0:T(8,128)(2,1)} custom-call(s32[5]{0:T(128)S(1)} %copy-done.3, bf16[256,768]{1,0:T(8,128)(2,1)S(1)} %copy-done.2, bf16[256,1536]{1,0:T(8,128)(2,1)S(1)} %collective-permute-done.14.other_h, bf16[768,384]{1,0:T(8,128)(2,1)S(1)} %copy-done, bf16[768,384]{1,0:T(8,128)(2,1)S(1)} %collective-permute-done.2.rest_1_, ...), custom_call_target="tpu_custom_call" | custom-call | flops 603979776 | bytes 4194304 | tf_op jit(solution)/shard_map/video_finish/pallas_call | solution.py:481
  96.2 4.1 %text_finish.1 = (bf16[256,1536]{1,0:T(8,128)(2,1)}, bf16[256,1536]{1,0:T(8,128)(2,1)}) custom-call(s32[5]{0:T(128)S(1)} %copy-done.3, bf16[256,768]{1,0:T(8,128)(2,1)S(1)} %get-tuple-element.22.rows_h, bf16[256,1536]{1,0:T(8,128)(2,1)S(1)} %collective-permute-done.12.other_h, bf16[768,384]{1,0:T(8,128)(2,1)S(1)} %copy-done, ...), custom_call_target="tpu_custom_call", output_to_operand_aliasing={{1}: (12, {})} | custom-call | flops 603979776 | bytes 4194304 | tf_op jit(solution)/shard_map/text_finish/pallas_call | solution.py:481
  (35 shorter events, 4.4 us)
Async XLA Ops:
  0.6 28.8 %collective-permute-start = (bf16[2,256,768]{2,1,0:T(8,128)(2,1)}, bf16[2,256,768]{2,1,0:T(8,128)(2,1)}, u32[]{:S(2)}, u32[]{:S(2)}) collective-permute-start(bf16[2,256,768]{2,1,0:T(8,128)(2,1)} %bitcast.7), channel_id=1, source_target_pairs={{0,2},{2,4},{4,6},{6,8},{8,10},{10,12},{12,14},{14,0},{1,3},{3,5},... | collective-permute-start | bytes 2359304 | tf_op jit(solution)/shard_map/ppermute | solution.py:556
  3.2 26.2 %collective-permute-start.1 = (bf16[2,256,768]{2,1,0:T(8,128)(2,1)}, bf16[2,256,768]{2,1,0:T(8,128)(2,1)}, u32[]{:S(2)}, u32[]{:S(2)}) collective-permute-start(bf16[2,256,768]{2,1,0:T(8,128)(2,1)} %bitcast.8), channel_id=1, source_target_pairs={{0,14},{2,0},{4,2},{6,4},{8,6},{10,8},{12,10},{14,12},{1,15},{3,1}... | collective-permute-start | bytes 2359304 | tf_op jit(solution)/shard_map/ppermute | solution.py:556
  7.8 21.6 %copy-start.4 = (bf16[2,8,4,8,768]{4,3,2,1,0:T(8,128)(2,1)S(1)}, bf16[2,8,4,8,768]{4,3,2,1,0:T(8,128)(2,1)}, u32[]{:S(2)}) copy-start(bf16[2,8,4,8,768]{4,3,2,1,0:T(8,128)(2,1)} %param.9) | copy-start | bytes 2359300
  13.0 16.4 %all-to-all-start = ((bf16[16,112,128]{2,1,0:T(8,128)(2,1)}), bf16[16,112,128]{2,1,0:T(8,128)(2,1)S(1)}, u32[]{:S(2)}, u32[]{:S(2)}) async-start(bf16[16,112,128]{2,1,0:T(8,128)(2,1)} %get-tuple-element.15), calls=%async_computation | async-start | bytes 917504 | tf_op jit(solution)/shard_map/all_to_all | solution.py:564
  19.8 22.6 %collective-permute-start.2 = (bf16[768,384]{1,0:T(8,128)(2,1)}, bf16[768,384]{1,0:T(8,128)(2,1)S(1)}, u32[]{:S(2)}, u32[]{:S(2)}) collective-permute-start(bf16[768,384]{1,0:T(8,128)(2,1)} %get-tuple-element.17), channel_id=1, source_target_pairs={{0,14},{2,0},{4,2},{6,4},{8,6},{10,8},{12,10},{14,12},{1,15},{3,1}... | collective-permute-start | bytes 1769480 | tf_op jit(solution)/shard_map/ppermute | solution.py:556
  21.3 23.9 %collective-permute-start.5 = (bf16[768,384]{1,0:T(8,128)(2,1)}, bf16[768,384]{1,0:T(8,128)(2,1)S(1)}, u32[]{:S(2)}, u32[]{:S(2)}) collective-permute-start(bf16[768,384]{1,0:T(8,128)(2,1)} %get-tuple-element.17), channel_id=1, source_target_pairs={{0,2},{2,4},{4,6},{6,8},{8,10},{10,12},{12,14},{14,0},{1,3},{3,5},... | collective-permute-start | bytes 1769480 | tf_op jit(solution)/shard_map/ppermute | solution.py:556
  32.7 32.8 %collective-permute-start.8 = (bf16[3,2,128,768]{3,2,1,0:T(8,128)(2,1)}, bf16[3,2,128,768]{3,2,1,0:T(8,128)(2,1)}, u32[]{:S(2)}, u32[]{:S(2)}) collective-permute-start(bf16[3,2,128,768]{3,2,1,0:T(8,128)(2,1)} %get-tuple-element.18), channel_id=1, source_target_pairs={{0,16},{16,32},{32,48},{48,64},{64,80},{80,96},{96,112},{112,128},... | collective-permute-start | bytes 3538952 | tf_op jit(solution)/shard_map/ppermute | solution.py:556
  33.2 32.3 %collective-permute-start.9 = (bf16[3,2,128,768]{3,2,1,0:T(8,128)(2,1)}, bf16[3,2,128,768]{3,2,1,0:T(8,128)(2,1)}, u32[]{:S(2)}, u32[]{:S(2)}) collective-permute-start(bf16[3,2,128,768]{3,2,1,0:T(8,128)(2,1)} %get-tuple-element.19), channel_id=1, source_target_pairs={{0,240},{16,0},{32,16},{48,32},{64,48},{80,64},{96,80},{112,96},{1... | collective-permute-start | bytes 3538952 | tf_op jit(solution)/shard_map/ppermute | solution.py:556
  37.5 14.0 %all-to-all-start.1 = ((bf16[8,112,128]{2,1,0:T(8,128)(2,1)}), bf16[8,112,128]{2,1,0:T(8,128)(2,1)S(1)}, u32[]{:S(2)}, u32[]{:S(2)}) async-start(bf16[8,112,128]{2,1,0:T(8,128)(2,1)} %get-tuple-element.16), calls=%async_computation.1 | async-start | bytes 458752 | tf_op jit(solution)/shard_map/all_to_all | solution.py:568
  42.4 14.4 %copy-start.5 = (s32[2,1,2,27]{3,2,1,0:T(2,128)S(1)}, s32[2,1,2,27]{3,2,1,0:T(2,128)}, u32[]{:S(2)}) copy-start(s32[2,1,2,27]{3,2,1,0:T(2,128)} %param.13) | copy-start | bytes 1300
  42.5 18.0 %collective-permute-start.3 = (bf16[768,384]{1,0:T(8,128)(2,1)S(1)}, bf16[768,384]{1,0:T(8,128)(2,1)S(1)}, u32[]{:S(2)}, u32[]{:S(2)}) collective-permute-start(bf16[768,384]{1,0:T(8,128)(2,1)S(1)} %collective-permute-done.2.rest_1_), channel_id=1, source_target_pairs={{0,14},{2,0},{4,2},{6,4},{8,6},{10,8},{12,10},{14,12},{1,15},{3,1}... | collective-permute-start | bytes 1769480 | tf_op jit(solution)/shard_map/ppermute | solution.py:556
  45.2 17.7 %collective-permute-start.6 = (bf16[768,384]{1,0:T(8,128)(2,1)S(1)}, bf16[768,384]{1,0:T(8,128)(2,1)S(1)}, u32[]{:S(2)}, u32[]{:S(2)}) collective-permute-start(bf16[768,384]{1,0:T(8,128)(2,1)S(1)} %collective-permute-done.5.rest_6_), channel_id=1, source_target_pairs={{0,2},{2,4},{4,6},{6,8},{8,10},{10,12},{12,14},{14,0},{1,3},{3,5},... | collective-permute-start | bytes 1769480 | tf_op jit(solution)/shard_map/ppermute | solution.py:556
  52.6 12.9 %all-to-all-start.2 = ((bf16[16,96,128]{2,1,0:T(8,128)(2,1)}), bf16[16,96,128]{2,1,0:T(8,128)(2,1)}, u32[]{:S(2)}, u32[]{:S(2)}) async-start(bf16[16,96,128]{2,1,0:T(8,128)(2,1)} %text_finish_sums.1), calls=%async_computation.2 | async-start | bytes 786432 | tf_op jit(solution)/shard_map/all_to_all | solution.py:573
  60.4 13.1 %collective-permute-start.4 = (bf16[768,384]{1,0:T(8,128)(2,1)S(1)}, bf16[768,384]{1,0:T(8,128)(2,1)S(1)}, u32[]{:S(2)}, u32[]{:S(2)}) collective-permute-start(bf16[768,384]{1,0:T(8,128)(2,1)S(1)} %collective-permute-done.3.rest_2_), channel_id=1, source_target_pairs={{0,14},{2,0},{4,2},{6,4},{8,6},{10,8},{12,10},{14,12},{1,15},{3,1}... | collective-permute-start | bytes 1769480 | tf_op jit(solution)/shard_map/ppermute | solution.py:556
  62.9 13.4 %collective-permute-start.7 = (bf16[768,384]{1,0:T(8,128)(2,1)S(1)}, bf16[768,384]{1,0:T(8,128)(2,1)S(1)}, u32[]{:S(2)}, u32[]{:S(2)}) collective-permute-start(bf16[768,384]{1,0:T(8,128)(2,1)S(1)} %collective-permute-done.6.rest_5_), channel_id=1, source_target_pairs={{0,2},{2,4},{4,6},{6,8},{8,10},{10,12},{12,14},{14,0},{1,3},{3,5},... | collective-permute-start | bytes 1769480 | tf_op jit(solution)/shard_map/ppermute | solution.py:556
  65.5 14.8 %copy-start.3 = (s32[5]{0:T(128)S(1)}, s32[5]{0:T(128)}, u32[]{:S(2)}) copy-start(s32[5]{0:T(128)} %stack.15.pos) | copy-start | bytes 64
  73.5 6.8 %copy-start = (bf16[768,384]{1,0:T(8,128)(2,1)S(1)}, bf16[768,384]{1,0:T(8,128)(2,1)}, u32[]{:S(2)}) copy-start(bf16[768,384]{1,0:T(8,128)(2,1)} %rest_0_.7) | copy-start | bytes 1769476
  76.3 1.0 copy-start.1
  77.3 3.0 %copy-start.2 = (bf16[256,768]{1,0:T(8,128)(2,1)S(1)}, bf16[256,768]{1,0:T(8,128)(2,1)}, u32[]{:S(2)}) copy-start(bf16[256,768]{1,0:T(8,128)(2,1)} %video_attention.1.after.rest_7_.rows_h) | copy-start | bytes 1179652
  77.6 9.4 %collective-permute-start.10 = (bf16[384,384]{1,0:T(8,128)(2,1)S(1)}, bf16[384,384]{1,0:T(8,128)(2,1)S(1)}, u32[]{:S(2)}, u32[]{:S(2)}) collective-permute-start(bf16[384,384]{1,0:T(8,128)(2,1)S(1)} %get-tuple-element.20), channel_id=1, source_target_pairs={{0,2},{2,4},{4,6},{6,8},{8,10},{10,12},{12,14},{14,0},{1,3},{3,5},... | collective-permute-start | bytes 884744 | tf_op jit(solution)/shard_map/ppermute | solution.py:556
  77.7 9.3 %collective-permute-start.11 = (bf16[384,384]{1,0:T(8,128)(2,1)S(1)}, bf16[384,384]{1,0:T(8,128)(2,1)S(1)}, u32[]{:S(2)}, u32[]{:S(2)}) collective-permute-start(bf16[384,384]{1,0:T(8,128)(2,1)S(1)} %get-tuple-element.21), channel_id=1, source_target_pairs={{0,14},{2,0},{4,2},{6,4},{8,6},{10,8},{12,10},{14,12},{1,15},{3,1}... | collective-permute-start | bytes 884744 | tf_op jit(solution)/shard_map/ppermute | solution.py:556
  82.7 10.5 %collective-permute-start.14 = (bf16[256,1536]{1,0:T(8,128)(2,1)S(1)}, bf16[256,1536]{1,0:T(8,128)(2,1)S(1)}, u32[]{:S(2)}, u32[]{:S(2)}) collective-permute-start(bf16[256,1536]{1,0:T(8,128)(2,1)S(1)} %video_share.1), channel_id=1, source_target_pairs={{0,1},{1,0},{2,3},{3,2},{4,5},{5,4},{6,7},{7,6},{8,9},{9,8},{10,11... | collective-permute-start | bytes 2359304 | tf_op jit(solution)/shard_map/ppermute | solution.py:584
  90.6 5.5 %collective-permute-start.12 = (bf16[256,1536]{1,0:T(8,128)(2,1)S(1)}, bf16[256,1536]{1,0:T(8,128)(2,1)S(1)}, u32[]{:S(2)}, u32[]{:S(2)}) collective-permute-start(bf16[256,1536]{1,0:T(8,128)(2,1)S(1)} %get-tuple-element.23), channel_id=1, source_target_pairs={{0,1},{1,0},{2,3},{3,2},{4,5},{5,4},{6,7},{7,6},{8,9},{9,8},{10,11... | collective-permute-start | bytes 2359304 | tf_op jit(solution)/shard_map/ppermute | solution.py:584
  93.0 3.1 %collective-permute-start.13 = (bf16[512,384]{1,0:T(8,128)(2,1)S(1)}, bf16[512,384]{1,0:T(8,128)(2,1)S(1)}, u32[]{:S(2)}, u32[]{:S(2)}) collective-permute-start(bf16[512,384]{1,0:T(8,128)(2,1)S(1)} %get-tuple-element.25), channel_id=1, source_target_pairs={{0,1},{1,0},{2,3},{3,2},{4,5},{5,4},{6,7},{7,6},{8,9},{9,8},{10,11... | collective-permute-start | bytes 1179656 | tf_op jit(solution)/shard_map/ppermute | solution.py:584

commit v6 on v5

--- a/solution.py
+++ b/solution.py
@@ -480,7 +480,7 @@
     depth, width = blocks[0].shape
     return pl.pallas_call(
         kernel,
-        in_specs=[SCALARS] + [FAR] + [ANY] * (len(left) - 1) + [FAR] * 7 + [ANY] * len(after),
+        in_specs=[SCALARS] + [FAR] + [ANY] * (len(left) - 1) + [ANY] * 7 + [ANY] * len(after),
         out_specs=out_specs,
         out_shape=out_shape,
         input_output_aliases=aliases or {},

time: 101 us -> 101 us (level)
  no operation moved by 1% of the time
where the time goes in v6:
time: 101 us; the launch traced here: 100 us
  starting transfers between devices  43.6 us (43%)
  Pallas kernels  31 us (31%)
  waiting for transfers between devices  22.8 us (23%)
  local copies, waits for them, and re-layouts  2.18 us (2%)
    ppermute x12, starting transfers between devices, up(): return lax.ppermute(x, axis, [(i, (i + by) % n) for i in range(n)])  20.9 us
    pallas_call x4, Pallas kernels, project_call(): pl.pallas_call(kernel, in_specs=[SCALARS] + [FAR] + [ANY] * (len(left) -...  13.2 us
    all_to_all x1, waiting for transfers between devices, shards(): parts = lax.all_to_all(parts, 'tm', 0, 0, tiled=True)  8.04 us
    pallas_call x1, Pallas kernels, video_attention(): pl.pallas_call(video_kernel, in_specs=[SCALARS, SCALARS, WHOLE] + [FAR] *...  7.97 us
    all_to_all x1, starting transfers between devices, shards(): parts = lax.all_to_all(parts, 'tm', 0, 0, tiled=True)  6.76 us
    ppermute x3, starting transfers between devices, swap(): return lax.ppermute(x, 'head', [(0, 1), (1, 0)])  6.75 us
    all_to_all x1, waiting for transfers between devices, shards(): parts = lax.all_to_all(parts, 'height', 0, 0, tiled=True)  6.32 us
    ppermute x12, waiting for transfers between devices, up(): return lax.ppermute(x, axis, [(i, (i + by) % n) for i in range(n)])  5.77 us
  transfers between devices with their start and end apart: 18, of which 5 were waited for; matrix products, arithmetic and copies ran while one was open for 1% of the time, Pallas kernels for 26%

profile of v6, /device:TPU:1, one launch (start us, length us, event | category | flops | bytes accessed | tf_op | source)
XLA Modules:
  0.0 100.5 jit_solution(13529940009839952972)
XLA Ops:
  0.6 2.5 %collective-permute-start = (bf16[2,256,768]{2,1,0:T(8,128)(2,1)}, bf16[2,256,768]{2,1,0:T(8,128)(2,1)}, u32[]{:S(2)}, u32[]{:S(2)}) collective-permute-start(bf16[2,256,768]{2,1,0:T(8,128)(2,1)} %bitcast.7), channel_id=1, source_target_pairs={{0,2},{2,4},{4,6},{6,8},{8,10},{10,12},{12,14},{14,0},{1,3},{3,5},... | collective-permute-start | bytes 2359304 | tf_op jit(solution)/shard_map/ppermute | solution.py:556
  3.2 4.0 %collective-permute-start.1 = (bf16[2,256,768]{2,1,0:T(8,128)(2,1)}, bf16[2,256,768]{2,1,0:T(8,128)(2,1)}, u32[]{:S(2)}, u32[]{:S(2)}) collective-permute-start(bf16[2,256,768]{2,1,0:T(8,128)(2,1)} %bitcast.8), channel_id=1, source_target_pairs={{0,14},{2,0},{4,2},{6,4},{8,6},{10,8},{12,10},{14,12},{1,15},{3,1}... | collective-permute-start | bytes 2359304 | tf_op jit(solution)/shard_map/ppermute | solution.py:556
  7.8 5.3 %text_part.1 = (bf16[16,112,128]{2,1,0:T(8,128)(2,1)}, bf16[768,384]{1,0:T(8,128)(2,1)}) custom-call(s32[5]{0:T(128)} %stack.15.pos, s32[1,256]{1,0:T(1,128)} %bitcast.14, bf16[256,768]{1,0:T(8,128)(2,1)} %tq_h.1, bf16[2,256,768]{2,1,0:T(8,128)(2,1)} %bitcast.9, bf16[256,768]{1,0:T(8,128)(2,1)} %rest_1_.1, bf16[256,768]{1,0:T(8,128)(2,1)} %rest_2_.1, ...), custom_call_target="tpu_custom_call" | custom-call | flops 5000000000 | bytes 2097152 | tf_op jit(solution)/shard_map/text_part/pallas_call | solution.py:121
  13.0 6.8 %all-to-all-start = ((bf16[16,112,128]{2,1,0:T(8,128)(2,1)}), bf16[16,112,128]{2,1,0:T(8,128)(2,1)S(1)}, u32[]{:S(2)}, u32[]{:S(2)}) async-start(bf16[16,112,128]{2,1,0:T(8,128)(2,1)} %get-tuple-element.15), calls=%async_computation | async-start | bytes 917504 | tf_op jit(solution)/shard_map/all_to_all | solution.py:564
  19.8 1.4 %collective-permute-start.2 = (bf16[768,384]{1,0:T(8,128)(2,1)}, bf16[768,384]{1,0:T(8,128)(2,1)S(1)}, u32[]{:S(2)}, u32[]{:S(2)}) collective-permute-start(bf16[768,384]{1,0:T(8,128)(2,1)} %get-tuple-element.17), channel_id=1, source_target_pairs={{0,14},{2,0},{4,2},{6,4},{8,6},{10,8},{12,10},{14,12},{1,15},{3,1}... | collective-permute-start | bytes 1769480 | tf_op jit(solution)/shard_map/ppermute | solution.py:556
  21.4 8.0 %all-to-all-done.parts = bf16[16,112,128]{2,1,0:T(8,128)(2,1)S(1)} async-done(((bf16[16,112,128]{2,1,0:T(8,128)(2,1)}), bf16[16,112,128]{2,1,0:T(8,128)(2,1)S(1)}, u32[]{:S(2)}, u32[]{:S(2)}) %all-to-all-start) | async-done | bytes 458784 | tf_op jit(solution)/shard_map/all_to_all | solution.py:564
  29.4 3.2 %text_merge.1 = (bf16[8,112,128]{2,1,0:T(8,128)(2,1)}, bf16[3,2,128,768]{3,2,1,0:T(8,128)(2,1)}, bf16[3,2,128,768]{3,2,1,0:T(8,128)(2,1)}) custom-call(bf16[16,112,128]{2,1,0:T(8,128)(2,1)S(1)} %all-to-all-done.parts, bf16[2,256,768]{2,1,0:T(8,128)(2,1)S(1)} %bitcast.11, bf16[2,256,768]{2,1,0:T(8,128)(2,1)} %collective-permute-done.z_low.rest_4_, ...), custom_call_target="tpu_custom_call" | custom-call | flops 2000000000 | bytes 6291456 | tf_op jit(solution)/shard_map/text_merge/pallas_call | solution.py:163
  33.2 4.3 %collective-permute-start.9 = (bf16[3,2,128,768]{3,2,1,0:T(8,128)(2,1)}, bf16[3,2,128,768]{3,2,1,0:T(8,128)(2,1)}, u32[]{:S(2)}, u32[]{:S(2)}) collective-permute-start(bf16[3,2,128,768]{3,2,1,0:T(8,128)(2,1)} %get-tuple-element.19), channel_id=1, source_target_pairs={{0,240},{16,0},{32,16},{48,32},{64,48},{80,64},{96,80},{112,96},{1... | collective-permute-start | bytes 3538952 | tf_op jit(solution)/shard_map/ppermute | solution.py:556
  37.5 4.9 %all-to-all-start.1 = ((bf16[8,112,128]{2,1,0:T(8,128)(2,1)}), bf16[8,112,128]{2,1,0:T(8,128)(2,1)S(1)}, u32[]{:S(2)}, u32[]{:S(2)}) async-start(bf16[8,112,128]{2,1,0:T(8,128)(2,1)} %get-tuple-element.16), calls=%async_computation.1 | async-start | bytes 458752 | tf_op jit(solution)/shard_map/all_to_all | solution.py:568
  42.5 2.7 %collective-permute-start.3 = (bf16[768,384]{1,0:T(8,128)(2,1)S(1)}, bf16[768,384]{1,0:T(8,128)(2,1)S(1)}, u32[]{:S(2)}, u32[]{:S(2)}) collective-permute-start(bf16[768,384]{1,0:T(8,128)(2,1)S(1)} %collective-permute-done.2.rest_1_), channel_id=1, source_target_pairs={{0,14},{2,0},{4,2},{6,4},{8,6},{10,8},{12,10},{14,12},{1,15},{3,1}... | collective-permute-start | bytes 1769480 | tf_op jit(solution)/shard_map/ppermute | solution.py:556
  45.2 6.3 %all-to-all-done.1.refs_0_ = bf16[8,112,128]{2,1,0:T(8,128)(2,1)S(1)} async-done(((bf16[8,112,128]{2,1,0:T(8,128)(2,1)}), bf16[8,112,128]{2,1,0:T(8,128)(2,1)S(1)}, u32[]{:S(2)}, u32[]{:S(2)}) %all-to-all-start.1) | async-done | bytes 229408 | tf_op jit(solution)/shard_map/all_to_all | solution.py:568
  52.6 4.2 %all-to-all-start.2 = ((bf16[16,96,128]{2,1,0:T(8,128)(2,1)}), bf16[16,96,128]{2,1,0:T(8,128)(2,1)}, u32[]{:S(2)}, u32[]{:S(2)}) async-start(bf16[16,96,128]{2,1,0:T(8,128)(2,1)} %text_finish_sums.1), calls=%async_computation.2 | async-start | bytes 786432 | tf_op jit(solution)/shard_map/all_to_all | solution.py:573
  57.4 3.0 %collective-permute-done.3.rest_2_ = bf16[768,384]{1,0:T(8,128)(2,1)S(1)} collective-permute-done((bf16[768,384]{1,0:T(8,128)(2,1)S(1)}, bf16[768,384]{1,0:T(8,128)(2,1)S(1)}, u32[]{:S(2)}, u32[]{:S(2)}) %collective-permute-start.3) | collective-permute-done | bytes 589856 | tf_op jit(solution)/shard_map/ppermute | solution.py:556
  60.4 2.4 %collective-permute-start.4 = (bf16[768,384]{1,0:T(8,128)(2,1)S(1)}, bf16[768,384]{1,0:T(8,128)(2,1)S(1)}, u32[]{:S(2)}, u32[]{:S(2)}) collective-permute-start(bf16[768,384]{1,0:T(8,128)(2,1)S(1)} %collective-permute-done.3.rest_2_), channel_id=1, source_target_pairs={{0,14},{2,0},{4,2},{6,4},{8,6},{10,8},{12,10},{14,12},{1,15},{3,1}... | collective-permute-start | bytes 1769480 | tf_op jit(solution)/shard_map/ppermute | solution.py:556
  62.9 2.6 %all-to-all-done.2.rest_8_.parts_h = bf16[16,96,128]{2,1,0:T(8,128)(2,1)} async-done(((bf16[16,96,128]{2,1,0:T(8,128)(2,1)}), bf16[16,96,128]{2,1,0:T(8,128)(2,1)}, u32[]{:S(2)}, u32[]{:S(2)}) %all-to-all-start.2) | async-done | bytes 393248 | tf_op jit(solution)/shard_map/all_to_all | solution.py:573
  65.5 8.0 %video_attention.1.after.rest_7_.rows_h = bf16[256,768]{1,0:T(8,128)(2,1)} custom-call(s32[5]{0:T(128)} %stack.15.pos, s32[108]{0:T(128)} %reshape.21.mask, s32[1,256]{1,0:T(1,128)} %bitcast.15, bf16[256,768]{1,0:T(8,128)(2,1)} %bitcast.13, bf16[256,768]{1,0:T(8,128)(2,1)} %rest_1_.1, bf16[256,768]{1,0:T(8,128)(2,1)} %rest_2_.1, ...), custom_call_target="tpu_custom_call" | custom-call | flops 8999999488 | bytes 6291456 | tf_op jit(solution)/shard_map/video_attention/pallas_call | solution.py:359
  73.5 2.8 %collective-permute-done.7.low.rest_4_ = bf16[768,384]{1,0:T(8,128)(2,1)S(1)} collective-permute-done((bf16[768,384]{1,0:T(8,128)(2,1)S(1)}, bf16[768,384]{1,0:T(8,128)(2,1)S(1)}, u32[]{:S(2)}, u32[]{:S(2)}) %collective-permute-start.7) | collective-permute-done | bytes 589856 | tf_op jit(solution)/shard_map/ppermute | solution.py:556
  77.7 2.7 %collective-permute-start.11 = (bf16[384,384]{1,0:T(8,128)(2,1)S(1)}, bf16[384,384]{1,0:T(8,128)(2,1)S(1)}, u32[]{:S(2)}, u32[]{:S(2)}) collective-permute-start(bf16[384,384]{1,0:T(8,128)(2,1)S(1)} %get-tuple-element.21), channel_id=1, source_target_pairs={{0,14},{2,0},{4,2},{6,4},{8,6},{10,8},{12,10},{14,12},{1,15},{3,1}... | collective-permute-start | bytes 884744 | tf_op jit(solution)/shard_map/ppermute | solution.py:556
  80.3 2.3 %video_share.1 = bf16[256,1536]{1,0:T(8,128)(2,1)S(1)} custom-call(s32[5]{0:T(128)S(1)} %copy-done.3, bf16[256,768]{1,0:T(8,128)(2,1)S(1)} %copy-done.2, bf16[768,384]{1,0:T(8,128)(2,1)S(1)} %copy-done, bf16[768,384]{1,0:T(8,128)(2,1)S(1)} %collective-permute-done.2.rest_1_, bf16[768,384]{1,0:T(8,128)(2,1)S(1)} %collective-permute-done.3.rest_2_, ...), custom_call_target="tpu_custom_call" | custom-call | flops 603979776 | bytes 4194304 | tf_op jit(solution)/shard_map/video_share/pallas_call | solution.py:481
  82.7 4.3 %collective-permute-start.14 = (bf16[256,1536]{1,0:T(8,128)(2,1)S(1)}, bf16[256,1536]{1,0:T(8,128)(2,1)S(1)}, u32[]{:S(2)}, u32[]{:S(2)}) collective-permute-start(bf16[256,1536]{1,0:T(8,128)(2,1)S(1)} %video_share.1), channel_id=1, source_target_pairs={{0,1},{1,0},{2,3},{3,2},{4,5},{5,4},{6,7},{7,6},{8,9},{9,8},{10,11... | collective-permute-start | bytes 2359304 | tf_op jit(solution)/shard_map/ppermute | solution.py:584
  86.9 3.7 %text_share.1 = (bf16[256,768]{1,0:T(8,128)(2,1)S(1)}, bf16[256,1536]{1,0:T(8,128)(2,1)S(1)}, f32[512,384]{1,0:T(8,128)S(1)}, bf16[512,384]{1,0:T(8,128)(2,1)S(1)}) custom-call(s32[5]{0:T(128)S(1)} %copy-done.3, bf16[16,96,128]{2,1,0:T(8,128)(2,1)} %all-to-all-done.2.rest_8_.parts_h, bf16[768,384]{1,0:T(8,128)(2,1)S(1)} %copy-done, ...), custom_call_target="tpu_custom_call" | custom-call | flops 603979776 | bytes 4194304 | tf_op jit(solution)/shard_map/text_share/pallas_call | solution.py:481
  90.6 2.4 %collective-permute-start.12 = (bf16[256,1536]{1,0:T(8,128)(2,1)S(1)}, bf16[256,1536]{1,0:T(8,128)(2,1)S(1)}, u32[]{:S(2)}, u32[]{:S(2)}) collective-permute-start(bf16[256,1536]{1,0:T(8,128)(2,1)S(1)} %get-tuple-element.23), channel_id=1, source_target_pairs={{0,1},{1,0},{2,3},{3,2},{4,5},{5,4},{6,7},{7,6},{8,9},{9,8},{10,11... | collective-permute-start | bytes 2359304 | tf_op jit(solution)/shard_map/ppermute | solution.py:584
  93.1 3.0 %video_finish.1.rest_9_ = bf16[256,1536]{1,0:T(8,128)(2,1)} custom-call(s32[5]{0:T(128)S(1)} %copy-done.3, bf16[256,768]{1,0:T(8,128)(2,1)S(1)} %copy-done.2, bf16[256,1536]{1,0:T(8,128)(2,1)S(1)} %collective-permute-done.14.other_h, bf16[768,384]{1,0:T(8,128)(2,1)S(1)} %copy-done, bf16[768,384]{1,0:T(8,128)(2,1)S(1)} %collective-permute-done.2.rest_1_, ...), custom_call_target="tpu_custom_call" | custom-call | flops 603979776 | bytes 4194304 | tf_op jit(solution)/shard_map/video_finish/pallas_call | solution.py:481
  96.2 4.1 %text_finish.1 = (bf16[256,1536]{1,0:T(8,128)(2,1)}, bf16[256,1536]{1,0:T(8,128)(2,1)}) custom-call(s32[5]{0:T(128)S(1)} %copy-done.3, bf16[256,768]{1,0:T(8,128)(2,1)S(1)} %get-tuple-element.22.rows_h, bf16[256,1536]{1,0:T(8,128)(2,1)S(1)} %collective-permute-done.12.other_h, bf16[768,384]{1,0:T(8,128)(2,1)S(1)} %copy-done, ...), custom_call_target="tpu_custom_call", output_to_operand_aliasing={{1}: (12, {})} | custom-call | flops 603979776 | bytes 4194304 | tf_op jit(solution)/shard_map/text_finish/pallas_call | solution.py:481
  (35 shorter events, 4.4 us)
Async XLA Ops:
  0.6 28.8 %collective-permute-start = (bf16[2,256,768]{2,1,0:T(8,128)(2,1)}, bf16[2,256,768]{2,1,0:T(8,128)(2,1)}, u32[]{:S(2)}, u32[]{:S(2)}) collective-permute-start(bf16[2,256,768]{2,1,0:T(8,128)(2,1)} %bitcast.7), channel_id=1, source_target_pairs={{0,2},{2,4},{4,6},{6,8},{8,10},{10,12},{12,14},{14,0},{1,3},{3,5},... | collective-permute-start | bytes 2359304 | tf_op jit(solution)/shard_map/ppermute | solution.py:556
  3.2 26.2 %collective-permute-start.1 = (bf16[2,256,768]{2,1,0:T(8,128)(2,1)}, bf16[2,256,768]{2,1,0:T(8,128)(2,1)}, u32[]{:S(2)}, u32[]{:S(2)}) collective-permute-start(bf16[2,256,768]{2,1,0:T(8,128)(2,1)} %bitcast.8), channel_id=1, source_target_pairs={{0,14},{2,0},{4,2},{6,4},{8,6},{10,8},{12,10},{14,12},{1,15},{3,1}... | collective-permute-start | bytes 2359304 | tf_op jit(solution)/shard_map/ppermute | solution.py:556
  7.8 21.6 %copy-start.4 = (bf16[2,8,4,8,768]{4,3,2,1,0:T(8,128)(2,1)S(1)}, bf16[2,8,4,8,768]{4,3,2,1,0:T(8,128)(2,1)}, u32[]{:S(2)}) copy-start(bf16[2,8,4,8,768]{4,3,2,1,0:T(8,128)(2,1)} %param.9) | copy-start | bytes 2359300
  13.0 16.4 %all-to-all-start = ((bf16[16,112,128]{2,1,0:T(8,128)(2,1)}), bf16[16,112,128]{2,1,0:T(8,128)(2,1)S(1)}, u32[]{:S(2)}, u32[]{:S(2)}) async-start(bf16[16,112,128]{2,1,0:T(8,128)(2,1)} %get-tuple-element.15), calls=%async_computation | async-start | bytes 917504 | tf_op jit(solution)/shard_map/all_to_all | solution.py:564
  19.8 22.6 %collective-permute-start.2 = (bf16[768,384]{1,0:T(8,128)(2,1)}, bf16[768,384]{1,0:T(8,128)(2,1)S(1)}, u32[]{:S(2)}, u32[]{:S(2)}) collective-permute-start(bf16[768,384]{1,0:T(8,128)(2,1)} %get-tuple-element.17), channel_id=1, source_target_pairs={{0,14},{2,0},{4,2},{6,4},{8,6},{10,8},{12,10},{14,12},{1,15},{3,1}... | collective-permute-start | bytes 1769480 | tf_op jit(solution)/shard_map/ppermute | solution.py:556
  21.3 23.9 %collective-permute-start.5 = (bf16[768,384]{1,0:T(8,128)(2,1)}, bf16[768,384]{1,0:T(8,128)(2,1)S(1)}, u32[]{:S(2)}, u32[]{:S(2)}) collective-permute-start(bf16[768,384]{1,0:T(8,128)(2,1)} %get-tuple-element.17), channel_id=1, source_target_pairs={{0,2},{2,4},{4,6},{6,8},{8,10},{10,12},{12,14},{14,0},{1,3},{3,5},... | collective-permute-start | bytes 1769480 | tf_op jit(solution)/shard_map/ppermute | solution.py:556
  32.7 32.8 %collective-permute-start.8 = (bf16[3,2,128,768]{3,2,1,0:T(8,128)(2,1)}, bf16[3,2,128,768]{3,2,1,0:T(8,128)(2,1)}, u32[]{:S(2)}, u32[]{:S(2)}) collective-permute-start(bf16[3,2,128,768]{3,2,1,0:T(8,128)(2,1)} %get-tuple-element.18), channel_id=1, source_target_pairs={{0,16},{16,32},{32,48},{48,64},{64,80},{80,96},{96,112},{112,128},... | collective-permute-start | bytes 3538952 | tf_op jit(solution)/shard_map/ppermute | solution.py:556
  33.2 32.3 %collective-permute-start.9 = (bf16[3,2,128,768]{3,2,1,0:T(8,128)(2,1)}, bf16[3,2,128,768]{3,2,1,0:T(8,128)(2,1)}, u32[]{:S(2)}, u32[]{:S(2)}) collective-permute-start(bf16[3,2,128,768]{3,2,1,0:T(8,128)(2,1)} %get-tuple-element.19), channel_id=1, source_target_pairs={{0,240},{16,0},{32,16},{48,32},{64,48},{80,64},{96,80},{112,96},{1... | collective-permute-start | bytes 3538952 | tf_op jit(solution)/shard_map/ppermute | solution.py:556
  37.5 14.0 %all-to-all-start.1 = ((bf16[8,112,128]{2,1,0:T(8,128)(2,1)}), bf16[8,112,128]{2,1,0:T(8,128)(2,1)S(1)}, u32[]{:S(2)}, u32[]{:S(2)}) async-start(bf16[8,112,128]{2,1,0:T(8,128)(2,1)} %get-tuple-element.16), calls=%async_computation.1 | async-start | bytes 458752 | tf_op jit(solution)/shard_map/all_to_all | solution.py:568
  42.4 14.4 %copy-start.5 = (s32[2,1,2,27]{3,2,1,0:T(2,128)S(1)}, s32[2,1,2,27]{3,2,1,0:T(2,128)}, u32[]{:S(2)}) copy-start(s32[2,1,2,27]{3,2,1,0:T(2,128)} %param.13) | copy-start | bytes 1300
  42.5 18.0 %collective-permute-start.3 = (bf16[768,384]{1,0:T(8,128)(2,1)S(1)}, bf16[768,384]{1,0:T(8,128)(2,1)S(1)}, u32[]{:S(2)}, u32[]{:S(2)}) collective-permute-start(bf16[768,384]{1,0:T(8,128)(2,1)S(1)} %collective-permute-done.2.rest_1_), channel_id=1, source_target_pairs={{0,14},{2,0},{4,2},{6,4},{8,6},{10,8},{12,10},{14,12},{1,15},{3,1}... | collective-permute-start | bytes 1769480 | tf_op jit(solution)/shard_map/ppermute | solution.py:556
  45.2 17.7 %collective-permute-start.6 = (bf16[768,384]{1,0:T(8,128)(2,1)S(1)}, bf16[768,384]{1,0:T(8,128)(2,1)S(1)}, u32[]{:S(2)}, u32[]{:S(2)}) collective-permute-start(bf16[768,384]{1,0:T(8,128)(2,1)S(1)} %collective-permute-done.5.rest_6_), channel_id=1, source_target_pairs={{0,2},{2,4},{4,6},{6,8},{8,10},{10,12},{12,14},{14,0},{1,3},{3,5},... | collective-permute-start | bytes 1769480 | tf_op jit(solution)/shard_map/ppermute | solution.py:556
  52.6 12.9 %all-to-all-start.2 = ((bf16[16,96,128]{2,1,0:T(8,128)(2,1)}), bf16[16,96,128]{2,1,0:T(8,128)(2,1)}, u32[]{:S(2)}, u32[]{:S(2)}) async-start(bf16[16,96,128]{2,1,0:T(8,128)(2,1)} %text_finish_sums.1), calls=%async_computation.2 | async-start | bytes 786432 | tf_op jit(solution)/shard_map/all_to_all | solution.py:573
  60.4 13.1 %collective-permute-start.4 = (bf16[768,384]{1,0:T(8,128)(2,1)S(1)}, bf16[768,384]{1,0:T(8,128)(2,1)S(1)}, u32[]{:S(2)}, u32[]{:S(2)}) collective-permute-start(bf16[768,384]{1,0:T(8,128)(2,1)S(1)} %collective-permute-done.3.rest_2_), channel_id=1, source_target_pairs={{0,14},{2,0},{4,2},{6,4},{8,6},{10,8},{12,10},{14,12},{1,15},{3,1}... | collective-permute-start | bytes 1769480 | tf_op jit(solution)/shard_map/ppermute | solution.py:556
  62.9 13.4 %collective-permute-start.7 = (bf16[768,384]{1,0:T(8,128)(2,1)S(1)}, bf16[768,384]{1,0:T(8,128)(2,1)S(1)}, u32[]{:S(2)}, u32[]{:S(2)}) collective-permute-start(bf16[768,384]{1,0:T(8,128)(2,1)S(1)} %collective-permute-done.6.rest_5_), channel_id=1, source_target_pairs={{0,2},{2,4},{4,6},{6,8},{8,10},{10,12},{12,14},{14,0},{1,3},{3,5},... | collective-permute-start | bytes 1769480 | tf_op jit(solution)/shard_map/ppermute | solution.py:556
  65.5 14.8 %copy-start.3 = (s32[5]{0:T(128)S(1)}, s32[5]{0:T(128)}, u32[]{:S(2)}) copy-start(s32[5]{0:T(128)} %stack.15.pos) | copy-start | bytes 64
  73.5 6.8 %copy-start = (bf16[768,384]{1,0:T(8,128)(2,1)S(1)}, bf16[768,384]{1,0:T(8,128)(2,1)}, u32[]{:S(2)}) copy-start(bf16[768,384]{1,0:T(8,128)(2,1)} %rest_0_.7) | copy-start | bytes 1769476
  76.3 1.0 copy-start.1
  77.3 3.0 %copy-start.2 = (bf16[256,768]{1,0:T(8,128)(2,1)S(1)}, bf16[256,768]{1,0:T(8,128)(2,1)}, u32[]{:S(2)}) copy-start(bf16[256,768]{1,0:T(8,128)(2,1)} %video_attention.1.after.rest_7_.rows_h) | copy-start | bytes 1179652
  77.6 9.4 %collective-permute-start.10 = (bf16[384,384]{1,0:T(8,128)(2,1)S(1)}, bf16[384,384]{1,0:T(8,128)(2,1)S(1)}, u32[]{:S(2)}, u32[]{:S(2)}) collective-permute-start(bf16[384,384]{1,0:T(8,128)(2,1)S(1)} %get-tuple-element.20), channel_id=1, source_target_pairs={{0,2},{2,4},{4,6},{6,8},{8,10},{10,12},{12,14},{14,0},{1,3},{3,5},... | collective-permute-start | bytes 884744 | tf_op jit(solution)/shard_map/ppermute | solution.py:556
  77.7 9.3 %collective-permute-start.11 = (bf16[384,384]{1,0:T(8,128)(2,1)S(1)}, bf16[384,384]{1,0:T(8,128)(2,1)S(1)}, u32[]{:S(2)}, u32[]{:S(2)}) collective-permute-start(bf16[384,384]{1,0:T(8,128)(2,1)S(1)} %get-tuple-element.21), channel_id=1, source_target_pairs={{0,14},{2,0},{4,2},{6,4},{8,6},{10,8},{12,10},{14,12},{1,15},{3,1}... | collective-permute-start | bytes 884744 | tf_op jit(solution)/shard_map/ppermute | solution.py:556
  82.7 10.5 %collective-permute-start.14 = (bf16[256,1536]{1,0:T(8,128)(2,1)S(1)}, bf16[256,1536]{1,0:T(8,128)(2,1)S(1)}, u32[]{:S(2)}, u32[]{:S(2)}) collective-permute-start(bf16[256,1536]{1,0:T(8,128)(2,1)S(1)} %video_share.1), channel_id=1, source_target_pairs={{0,1},{1,0},{2,3},{3,2},{4,5},{5,4},{6,7},{7,6},{8,9},{9,8},{10,11... | collective-permute-start | bytes 2359304 | tf_op jit(solution)/shard_map/ppermute | solution.py:584
  90.6 5.5 %collective-permute-start.12 = (bf16[256,1536]{1,0:T(8,128)(2,1)S(1)}, bf16[256,1536]{1,0:T(8,128)(2,1)S(1)}, u32[]{:S(2)}, u32[]{:S(2)}) collective-permute-start(bf16[256,1536]{1,0:T(8,128)(2,1)S(1)} %get-tuple-element.23), channel_id=1, source_target_pairs={{0,1},{1,0},{2,3},{3,2},{4,5},{5,4},{6,7},{7,6},{8,9},{9,8},{10,11... | collective-permute-start | bytes 2359304 | tf_op jit(solution)/shard_map/ppermute | solution.py:584
  93.0 3.1 %collective-permute-start.13 = (bf16[512,384]{1,0:T(8,128)(2,1)S(1)}, bf16[512,384]{1,0:T(8,128)(2,1)S(1)}, u32[]{:S(2)}, u32[]{:S(2)}) collective-permute-start(bf16[512,384]{1,0:T(8,128)(2,1)S(1)} %get-tuple-element.25), channel_id=1, source_target_pairs={{0,1},{1,0},{2,3},{3,2},{4,5},{5,4},{6,7},{7,6},{8,9},{9,8},{10,11... | collective-permute-start | bytes 1179656 | tf_op jit(solution)/shard_map/ppermute | solution.py:584
